TPU v7x, 32 devices: a whole 2x2x4 slice. The times are simulated.
32 devices in a mesh: cube: 2 (over x), row: 4 (over y, core), col: 4 (over z).
Axes of the slice: x: 2, y: 2, z: 4, core: 2. Of those that a mesh axis runs over, the one named last changes fastest.
Arguments:
- child_update: float32 [8, 2, 16, 128, 128, 128], P(('cube', 'row'), None, None, None, 'col'), may hold values from -13 to 13
- child_map: int32 [2, 16384], replicated, may hold values from -1 to 16383, as said below
- parent_diag: float32 [16384], replicated, may hold values from 0.5 to 2
Outputs:
- updated: float32 [8, 16, 128, 128, 128], P(('cube', 'row'), None, None, 'col')
Inputs may be any that keep to these rules, and one draw needn't show every extreme that they name: `child_map`: for each child and each aligned block of 128 child rows, the live rows (entries other than -1) come first and map, strictly increasing, into the same aligned block of 128 parent rows; every block has at least one -1 entry and uses the last parent row of its block.
All inputs are finite; a program needn't handle non-finite values.
Results may differ from a plain program's by a relative error of at most 0.0001.
Values sent between devices are 32-bit elements; how exact they have to be, the bound alone decides.
No kernel may reach another device: no remote copies, remote signals or barrier semaphores. Data moves between devices by JAX's collectives and lax.ppermute only.
A program may use at most 320 MiB of HBM per device.

v0:
```python
import jax
import jax.numpy as jnp
from jax import lax
from jax.sharding import PartitionSpec as P

K = 1024


def swapped(value, axis, distance):
    mask = 2**distance
    pairs = [(source, source ^ mask) for source in range(lax.axis_size(axis))]
    return lax.ppermute(value, axis, pairs)


def broadcast(value, axis, root):
    mine = lax.axis_index(axis) == root
    return lax.psum(jnp.where(mine, value, jnp.zeros_like(value)), axis)


def tile_onehot(values, targets):
    offsets = jnp.arange(values.shape[-1], dtype=jnp.int32)
    return (values[..., None, :] == targets[..., None, None] + offsets[:, None]).astype(jnp.float32)


def on_device(child_update, child_map, parent_diag):
    grid_size = lax.axis_size(("cube", "row"))
    half_grid = grid_size // 2
    columns = lax.axis_size("col")
    position = lax.axis_index(("cube", "row"))
    column_index = lax.axis_index("col")
    sibling = position // half_grid
    within = position % half_grid
    block = child_update[0]
    tile = block.shape[2]
    local_tiles = block.shape[1]
    local_cols = block.shape[3]
    own_map = lax.dynamic_index_in_dim(child_map, sibling, 0, keepdims=False)
    row_map = lax.dynamic_index_in_dim(
        own_map.reshape(local_tiles, 2, half_grid, tile), within, 2, keepdims=False
    )
    row_map = jnp.swapaxes(row_map, 0, 1)
    tile_rows = (
        grid_size * jnp.arange(local_tiles, dtype=jnp.int32)[None, :]
        + half_grid * jnp.arange(2, dtype=jnp.int32)[:, None]
        + within
    )
    row_onehot = tile_onehot(row_map, tile * tile_rows)
    col_map = lax.dynamic_index_in_dim(
        own_map.reshape(local_cols, columns, tile), column_index, 1, keepdims=False
    )
    tile_cols = columns * jnp.arange(local_cols, dtype=jnp.int32) + column_index
    col_onehot = tile_onehot(col_map, tile * tile_cols)
    placed = jnp.einsum("wjos,wjsmv->wjomv", row_onehot, block, precision=lax.Precision.HIGHEST)
    placed = jnp.einsum("wjomv,mpv->wjomp", placed, col_onehot, precision=lax.Precision.HIGHEST)
    kept = lax.dynamic_index_in_dim(placed, sibling, 0, keepdims=False)
    sent = lax.dynamic_index_in_dim(placed, 1 - sibling, 0, keepdims=False)
    arrived = swapped(sent, ("cube", "row"), half_grid.bit_length() - 1)
    global_rows = (
        tile * (grid_size * jnp.arange(local_tiles, dtype=jnp.int32)[:, None] + position)
        + jnp.arange(tile, dtype=jnp.int32)[None, :]
    )
    global_cols = tile * tile_cols[:, None] + jnp.arange(tile, dtype=jnp.int32)[None, :]
    diag_values = lax.dynamic_index_in_dim(
        parent_diag.reshape(local_tiles, grid_size, tile), position, 1, keepdims=False
    )
    on_diagonal = global_rows[:, :, None, None] == global_cols[None, None, :, :]
    front = kept + arrived + jnp.where(on_diagonal, diag_values[:, :, None, None], 0.0)
    panel_local = K // (tile * columns)
    panel_piece = front[:, :, :panel_local, :][:, :, :, None, :]
    panel_rows = lax.all_gather(panel_piece, "col", axis=3, tiled=True).reshape(
        local_tiles, tile, K
    )
    first_tile = panel_rows[0]
    pivot_count = K // tile
    slots = jnp.arange(pivot_count, dtype=jnp.int32)
    spread = jnp.where((slots == position)[:, None, None], first_tile[None], 0.0)
    pivot_block = lax.psum(spread, ("cube", "row")).reshape(K, K)
    factor = jnp.linalg.cholesky(pivot_block)
    count = panel_rows.shape[0]
    flat = panel_rows.reshape(count * tile, K)
    solved_flat = jax.scipy.linalg.solve_triangular(factor, flat.T, lower=True).T
    solved = solved_flat.reshape(count, tile, K)
    diagonal = broadcast(solved, "row", column_index)
    gathered = lax.all_gather(diagonal[None], "cube", axis=0, tiled=True)
    update = jnp.einsum("rsk,cjvk->rsjcv", solved, gathered, precision=lax.Precision.HIGHEST)
    update = update.reshape(local_tiles, tile, local_cols, tile)
    trailing = front - update
    panel_cols = lax.dynamic_index_in_dim(
        solved.reshape(local_tiles, tile, panel_local, columns, tile),
        column_index,
        3,
        keepdims=False,
    )
    result = jnp.concatenate([panel_cols, trailing[:, :, panel_local:]], axis=2)
    return result[None]


def solution(mesh):
    return jax.shard_map(
        on_device,
        mesh=mesh,
        in_specs=(P(("cube", "row"), None, None, None, "col", None), P(), P()),
        out_specs=P(("cube", "row"), None, None, "col", None),
        check_vma=False,
    )
```

profile of v0, /device:TPU:6, one launch (start us, length us, event | category | flops | bytes accessed | tf_op | source)
XLA Modules:
  0.0 2147.1 jit_solution(7453616287589428008)
XLA Ops:
  7.8 86.0 %fusion = f32[2,16,128,32,128]{4,2,1,0,3:T(8,128)} fusion(f32[2,16,128,32,128]{4,3,2,1,0:T(8,128)} %bitcast.8, s32[2,16,128]{2,1,0:T(8,128)S(1)} %iota_add_fusion, s32[2,16,128]{2,1,0:T(8,128)S(1)} %bitcast.204), kind=kOutput, calls=%fused_computation.2 | convolution fusion | flops 25770328064 | bytes 134250496 | tf_op jit(solution)/shard_map/wjos,wjsmv->wjomv/dot_general | solution.py:53
  93.8 55.0 %fusion.29 = f32[32,128,2,16,128]{4,1,3,2,0:T(8,128)} fusion(f32[2,16,128,32,128]{4,2,1,0,3:T(8,128)} %fusion, s32[32,128]{1,0:T(8,128)S(1)} %iota_add_fusion.1, s32[32,128]{1,0:T(8,128)S(1)} %bitcast.205), kind=kOutput, calls=%fused_computation.46 | convolution fusion | flops 25770328064 | bytes 134250496 | tf_op jit(solution)/shard_map/wjomv,mpv->wjomp/dot_general | solution.py:54
  148.8 23.2 %dynamic-slice_bitcast_fusion = f32[16,128,32,128]{1,3,0,2:T(8,128)} fusion(f32[32,128,2,16,128]{4,1,3,2,0:T(8,128)} %fusion.29, s32[]{:T(128)S(6)} %select_n.59), kind=kLoop, calls=%fused_computation.7 | loop fusion | bytes 67108864 | tf_op jit(solution)/shard_map/jit(dynamic_index_in_dim)/squeeze | solution.py:56
  173.5 720.3 %collective-permute-done = f32[16,128,32,128]{1,3,0,2:T(8,128)} collective-permute-done((f32[16,128,32,128]{1,3,0,2:T(8,128)}, f32[16,128,32,128]{1,3,0,2:T(8,128)}, u32[]{:S(2)}, u32[]{:S(2)}) %collective-permute-start) | collective-permute-done | bytes 33554464 | tf_op jit(solution)/shard_map/ppermute | solution.py:12
  893.8 33.0 %fusion.2 = f32[16,128,32,128]{1,3,0,2:T(8,128)} fusion(f32[16,128,32,128]{1,3,0,2:T(8,128)} %collective-permute-done, f32[32,128,2,16,128]{4,1,3,2,0:T(8,128)} %fusion.29, s32[]{:T(128)S(6)} %select_n.55, f32[16,128]{1,0:T(8,128)S(1)} %bitcast.206, s32[32,128]{1,0:T(8,128)S(1)} %iota_add_fusion.1, s32[16,128]{1,0:T(8,128)S(1)} %iota_add_fusion.2), kind=kLoop, calls=%fused_computation.6 | loop fusion | flops 33554432 | bytes 100696064 | tf_op jit(solution)/shard_map/add | solution.py:67
  926.8 3.2 slice.271
  930.1 150.9 %all-gather.6.cloned.1.call-done = f32[16,128,2,512]{1,3,0,2:T(8,128)} async-done(((f32[16,128,2,128]{1,3,0,2:T(8,128)}), f32[16,128,2,512]{1,3,0,2:T(8,128)}) %all-gather.6.cloned.1.call-update) | async-done | bytes 8388624 | tf_op jit(solution)/shard_map/all_gather | solution.py:70
  1082.5 3.0 copy.60
  1086.0 8.2 copy.33
  1094.2 7.3 copy.59
  1101.6 62.5 %all-reduce.4.cloned.1.call-done = f32[1024,1024]{0,1:T(8,128)} async-done(((f32[1024,1024]{0,1:T(8,128)}), f32[1024,1024]{0,1:T(8,128)}) %all-reduce.4.cloned.1.call-update) | async-done | bytes 4194320 | tf_op jit(solution)/shard_map/psum | solution.py:77
  1164.0 5.5 copy.32
  1169.6 4.4 fusion.13
  1176.0 11.7 cholesky.223
  1190.2 9.8 custom-call.63
  1204.0 11.9 cholesky.244
  1216.6 9.8 custom-call.64
  1229.7 11.7 cholesky.468
  1242.7 9.8 custom-call.65
  1256.1 12.1 cholesky.487
  1269.5 9.8 custom-call.66
  1282.8 11.7 cholesky.506
  1295.8 9.9 custom-call.67
  1309.1 11.7 cholesky.526
  1322.1 9.8 custom-call.68
  1334.9 11.9 cholesky.546
  1348.1 9.8 custom-call.69
  1360.5 11.7 cholesky.564
  1379.0 4.8 select_select_fusion
  1383.9 23.6 %while.1 = (s32[]{:T(128)}, f32[1024,1024]{1,0:T(8,128)}, s32[8,2]{0,1:T(2,128)S(1)}, f32[8,128,128]{2,1,0:T(8,128)S(1)}, s32[]{:T(128)}) while((s32[]{:T(128)}, f32[1024,1024]{1,0:T(8,128)}, s32[8,2]{0,1:T(2,128)S(1)}, f32[8,128,128]{2,1,0:T(8,128)S(1)}, s32[]{:T(128)}) %tuple.57), condition=%wide.while_cond, body=%wide.while_body.sunk | while | flops 2 | bytes 131181 | solution.py:81
  1407.4 79.0 %custom-call.70 = f32[8,128,128]{1,2,0:T(8,128)S(1)} custom-call(f32[8,128,128]{2,1,0:T(8,128)S(1)} %get-tuple-element.12), custom_call_target="InvertDiagBlocksLowerTriangular" | custom-call | tf_op jit(solution)/shard_map/jit(_solve_triangular)/triangular_solve | solution.py:81
  1486.5 2.7 constant_dynamic-update-slice_fusion.17
  1497.3 3.0 fusion.20
  1502.5 4.7 fusion.23
  1507.2 2.6 constant_dynamic-update-slice_fusion.13
  1509.8 4.2 convolution_subtract_fusion.2
  1515.1 4.5 convolution_subtract_fusion
  1520.6 5.5 convolution_subtract_fusion.1
  1528.0 5.2 copy.48
  1533.2 8.7 copy.35
  1542.0 5.1 select_bitcast_fusion
  1547.2 156.0 %all-reduce.6.cloned.1.call-done = f32[1,16,128,1024]{3,2,1,0:T(8,128)} async-done(((f32[1,16,128,1024]{3,2,1,0:T(8,128)}), f32[1,16,128,1024]{3,2,1,0:T(8,128)}) %all-reduce.6.cloned.1.call-update) | async-done | bytes 8388624 | tf_op jit(solution)/shard_map/psum | solution.py:17
  1705.6 198.0 %all-gather.4.cloned.1.call-done = f32[2,16,128,1024]{3,2,1,0:T(8,128)} async-done(((f32[1,16,128,1024]{3,2,1,0:T(8,128)}), f32[2,16,128,1024]{3,2,1,0:T(8,128)}) %all-gather.4.cloned.1.call-update) | async-done | bytes 16777232 | tf_op jit(solution)/shard_map/all_gather | solution.py:84
  1903.6 126.3 %convolution_bitcast_fusion = f32[16,128,16,2,128]{1,4,0,2,3:T(8,128)} fusion(f32[2,16,128,1024]{3,2,1,0:T(8,128)} %all-gather.4.cloned.1.call-done, f32[16,128,1024,1,1]{1,0,2,4,3:T(8,128)} %bitcast.185), kind=kOutput, calls=%fused_computation.9 | convolution fusion | flops 103079215104 | bytes 58720256 | tf_op jit(solution)/shard_map/rsk,cjvk->rsjcv/dot_general | solution.py:85
  2029.9 23.0 %copy.37 = f32[16,128,16,2,128]{1,4,0,3,2:T(8,128)} copy(f32[16,128,16,2,128]{1,4,0,2,3:T(8,128)} %convolution_bitcast_fusion) | data formatting | bytes 67108864 | tf_op jit(solution)/shard_map/rsk,cjvk->rsjcv/transpose | solution.py:85
  2052.9 30.6 %slice_subtract_fusion = f32[16,128,30,128]{1,3,0,2:T(8,128)} fusion(f32[16,128,32,128]{1,3,0,2:T(8,128)} %bitcast.182, f32[16,128,32,128]{1,3,0,2:T(8,128)} %fusion.2), kind=kLoop, calls=%fused_computation.8 | loop fusion | flops 7864320 | bytes 94371840 | tf_op jit(solution)/shard_map/sub | solution.py:87
  2083.4 22.2 %maximum_bitcast_fusion = f32[1,16,128,32,128]{2,4,1,3,0:T(8,128)} fusion(f32[16,128,30,128]{1,3,0,2:T(8,128)} %slice_subtract_fusion, f32[16,128,2,128]{1,3,0,2:T(8,128)S(1)} %bitcast.200), kind=kLoop, calls=%fused_computation.4 | loop fusion | flops 8388608 | bytes 67108864 | tf_op jit(solution)/shard_map/broadcast_in_dim | solution.py:95
  2105.6 34.6 %copy.38 = f32[1,16,128,32,128]{4,3,2,1,0:T(8,128)} copy(f32[1,16,128,32,128]{2,4,1,3,0:T(8,128)} %maximum_bitcast_fusion) | data formatting | bytes 67108864 | tf_op jit(solution)/shard_map/broadcast_in_dim | solution.py:95
  (114 shorter events, 81.7 us)
Async XLA Ops:
  6.5 0.9 copy-start
  6.5 1074.5 %all-gather.6.cloned.1.call-start = ((), (), s32[]{:S(2)}) async-start(), calls=%async_computation.3 | async-start | bytes 10485760 | tf_op jit(solution)/shard_map/all_gather | solution.py:70
  172.0 721.8 %collective-permute-start = (f32[16,128,32,128]{1,3,0,2:T(8,128)}, f32[16,128,32,128]{1,3,0,2:T(8,128)}, u32[]{:S(2)}, u32[]{:S(2)}) collective-permute-start(f32[16,128,32,128]{1,3,0,2:T(8,128)} %dynamic-slice_bitcast_fusion), channel_id=1, source_target_pairs={{0,16},{4,20},{8,24},{12,28},{16,0},{20,4},{24,8},{28,12},{1,17},{... | collective-permute-start | bytes 100663304 | tf_op jit(solution)/shard_map/ppermute | solution.py:12
  930.0 234.0 %all-reduce.4.cloned.1.call-start = ((), (), s32[]{:S(2)}) async-start(), calls=%async_computation | async-start | bytes 8388608 | tf_op jit(solution)/shard_map/psum | solution.py:77
  1085.5 617.7 %all-reduce.6.cloned.1.call-start = ((), (), s32[]{:S(2)}) async-start(), calls=%async_computation.1 | async-start | bytes 16777216 | tf_op jit(solution)/shard_map/psum | solution.py:17
  1174.0 2.0 copy-start.2
  1486.4 6.4 copy-start.3
  1486.4 6.4 slice-start
  1489.1 3.8 slice-start.1
  1495.1 5.2 copy-start.4
  1547.1 356.4 %all-gather.4.cloned.1.call-start = ((), (), s32[]{:S(2)}) async-start(), calls=%async_computation.2 | async-start | bytes 25165824 | tf_op jit(solution)/shard_map/all_gather | solution.py:84
  2105.6 34.6 %copy-start.1 = (s32[2,16384]{1,0:T(2,128)S(1)}, s32[2,16384]{1,0:T(2,128)}, u32[]{:S(2)}) copy-start(s32[2,16384]{1,0:T(2,128)} %param.4) | copy-start | bytes 393220
Sparse Core Ops, SparseCore 0:
  930.2 150.8 all-gather.5
  1085.6 78.3 all-reduce.3
  1547.2 155.9 all-reduce.5
  1704.7 198.8 all-gather.3
where the time goes:
time: 2160 us; the launch traced here: 2150 us
  waiting for transfers between devices  1290 us (60%)
  other arithmetic  352 us (16%)
  matrix products  332 us (15%)
  local copies, waits for them, and re-layouts  155 us (7%)
    ppermute x1, waiting for transfers between devices, swapped(): return lax.ppermute(value, axis, pairs)  720 us
    all_gather x1, waiting for transfers between devices, on_device(): gathered = lax.all_gather(diagonal[None], 'cube', axis=0, tiled=True)  198 us
    another operation x30, other arithmetic, on_device(): factor = jnp.linalg.cholesky(pivot_block)  172 us
    psum x1, waiting for transfers between devices, broadcast(): return lax.psum(jnp.where(mine, value, jnp.zeros_like(value)), axis)  156 us
    all_gather x1, waiting for transfers between devices, on_device(): lax.all_gather(panel_piece, 'col', axis=3, tiled=True)  151 us
    dot_general x1, matrix products, on_device(): jnp.einsum('rsk,cjvk->rsjcv', solved, gathered, precision=lax.Precision.H...  126 us
    dot_general x1, matrix products, on_device(): jnp.einsum('wjos,wjsmv->wjomv', row_onehot, block, precision=lax.Precisio...  86 us
    another operation x3, other arithmetic, on_device(): jax.scipy.linalg.solve_triangular(factor, flat.T, lower=True)  83.8 us
  transfers between devices with their start and end apart: 5, of which 5 were waited for; matrix products, arithmetic and copies ran while one was open for 1% of the time, Pallas kernels for 0%

commit v1 on v0

v1 whole, which is shorter than its diff:
```python
import jax
import jax.numpy as jnp
import numpy as np
from jax import lax
from jax.experimental import pallas as pl
from jax.experimental.pallas import tpu as pltpu
from jax.sharding import PartitionSpec as P

K = 1024
F32 = jnp.float32
BF16 = jnp.bfloat16
SUB = 8
VMEM_LIMIT = 56 * 1024 * 1024


def params(steps=1):
    return pltpu.CompilerParams(
        dimension_semantics=("arbitrary",) * steps, vmem_limit_bytes=VMEM_LIMIT
    )


def cost(flops, moved):
    return pl.CostEstimate(flops=int(flops), bytes_accessed=int(moved), transcendentals=0)


def swapped(value, axis, distance):
    mask = 2**distance
    pairs = [(source, source ^ mask) for source in range(lax.axis_size(axis))]
    return lax.ppermute(value, axis, pairs)


def after(value, *others):
    return lax.optimization_barrier((value,) + others)[0]


def inverse_map(values, starts):
    tile = values.shape[-1]
    offsets = jnp.arange(tile, dtype=jnp.int32)
    hit = (values - starts[:, None])[:, None, :] == offsets[None, :, None]
    return jnp.sum(jnp.where(hit, offsets[None, None, :] + 1, 0), axis=-1).astype(jnp.int32) - 1


def split(value):
    high = value.astype(BF16)
    return high, (value - high.astype(F32)).astype(BF16)


def dot(a, b):
    return jnp.dot(a, b, preferred_element_type=F32)


def dot_nt(a, b):
    return lax.dot_general(a, b, (((1,), (1,)), ((), ())), preferred_element_type=F32)


def dot_full(a, b, dims):
    return lax.dot_general(
        a, b, (dims, ((), ())), precision=lax.Precision.HIGHEST, preferred_element_type=F32
    )


def pack_panel(child, half, count):
    _, _, rows, tile, _, lanes = child.shape

    def kernel(half_ref, raw, out):
        for p in range(count):
            out[0, p] = raw.reshape(tile * SUB, lanes)[pl.ds(p, tile, SUB), :]

    return pl.pallas_call(
        kernel,
        grid_spec=pltpu.PrefetchScalarGridSpec(
            num_scalar_prefetch=1,
            grid=(rows,),
            in_specs=[
                pl.BlockSpec((1, 1, 1, tile, SUB, lanes), lambda j, h: (0, h[0], j, 0, 0, 0))
            ],
            out_specs=pl.BlockSpec((1, count, tile, lanes), lambda j, h: (j, 0, 0, 0)),
        ),
        out_shape=jax.ShapeDtypeStruct((rows, count, tile, lanes), F32),
        compiler_params=params(),
        cost_estimate=cost(0, rows * tile * lanes * 4 * (SUB + count)),
        name="pack_panel",
    )(half, child)


def pack_cross(child, half, parity):
    _, _, rows, tile, cols, lanes = child.shape
    pairs = cols // 2

    def kernel(half_ref, parity_ref, raw, out):
        for i in range(1, pairs):
            at = pl.ds(2 * i + parity_ref[0], tile, cols)
            out[0, i - 1] = raw.reshape(tile * cols, lanes)[at, :]

    return pl.pallas_call(
        kernel,
        grid_spec=pltpu.PrefetchScalarGridSpec(
            num_scalar_prefetch=2,
            grid=(rows - 1,),
            in_specs=[
                pl.BlockSpec(
                    (1, 1, 1, tile, cols, lanes), lambda j, h, b: (0, h[0], j + 1, 0, 0, 0)
                )
            ],
            out_specs=pl.BlockSpec((1, pairs - 1, tile, lanes), lambda j, h, b: (j, 0, 0, 0)),
        ),
        out_shape=jax.ShapeDtypeStruct((rows - 1, pairs - 1, tile, lanes), F32),
        compiler_params=params(),
        cost_estimate=cost(0, rows * tile * lanes * 4 * (cols + pairs)),
        name="pack_cross",
    )(half, parity, child)


def pack_lower(child, half, parity, first, last):
    _, _, _, tile, cols, lanes = child.shape
    base = first * (first - 1) // 2
    count = last * (last - 1) // 2 - base

    def kernel(half_ref, parity_ref, raw, out):
        j = pl.program_id(0) + first
        start = j * (j - 1) // 2 - base - 1
        for i in range(1, last):
            @pl.when(i <= j)
            def _():
                at = pl.ds(2 * i + parity_ref[0], tile, cols)
                out[start + i] = raw.reshape(tile * cols, lanes)[at, :]

    return pl.pallas_call(
        kernel,
        grid_spec=pltpu.PrefetchScalarGridSpec(
            num_scalar_prefetch=2,
            grid=(last - first,),
            in_specs=[
                pl.BlockSpec(
                    (1, 1, 1, tile, cols, lanes), lambda j, h, b: (0, h[0], j + first, 0, 0, 0)
                )
            ],
            out_specs=pl.BlockSpec((count, tile, lanes), lambda j, h, b: (0, 0, 0)),
        ),
        out_shape=jax.ShapeDtypeStruct((count, tile, lanes), F32),
        compiler_params=params(),
        cost_estimate=cost(0, tile * lanes * 4 * ((last - first) * cols + count)),
        name="pack_lower",
    )(half, parity, child)


def pack_all(child, half):
    _, _, rows, tile, cols, lanes = child.shape

    def kernel(half_ref, raw, out):
        for p in range(cols):
            out[0, p] = raw.reshape(tile * cols, lanes)[pl.ds(p, tile, cols), :]

    return pl.pallas_call(
        kernel,
        grid_spec=pltpu.PrefetchScalarGridSpec(
            num_scalar_prefetch=1,
            grid=(rows - 1,),
            in_specs=[
                pl.BlockSpec((1, 1, 1, tile, cols, lanes), lambda j, h: (0, h[0], j + 1, 0, 0, 0))
            ],
            out_specs=pl.BlockSpec((1, cols, tile, lanes), lambda j, h: (j, 0, 0, 0)),
        ),
        out_shape=jax.ShapeDtypeStruct((rows - 1, cols, tile, lanes), F32),
        compiler_params=params(),
        cost_estimate=cost(0, rows * tile * lanes * 8 * cols),
        name="pack_all",
    )(half, child)


def gathered_row(index, load, columns):
    row = load(jnp.maximum(index, 0))
    placed = jnp.take_along_axis(
        row, jnp.maximum(columns, 0), axis=1, mode="promise_in_bounds"
    )
    return jnp.where((columns >= 0) & (index >= 0), placed, 0.0)


def place_rows(first, second, maps, diag, where):
    count, tile, cols, lanes = first.shape
    (rows0, cols0), (rows1, cols1) = maps

    def kernel(rows0_ref, rows1_ref, where_ref, u0, u1, c0, c1, d, out):
        n, g = pl.program_id(0), pl.program_id(1)
        cols_0, cols_1 = c0[...], c1[...]

        def body(step, carry):
            for r in range(SUB):
                o = step * SUB + r
                value = gathered_row(rows0_ref[n, o], lambda s: u0[0, s], cols_0)
                value += gathered_row(rows1_ref[n, o], lambda s: u1[0, s], cols_1)
                for p in range(SUB):
                    out[0, p, pl.ds(o, 1), :] = value[p : p + 1, :]
            return carry

        lax.fori_loop(0, tile // SUB, body, 0)
        for p in range(SUB):
            @pl.when(where_ref[n] == g * SUB + p)
            def _():
                eye = lax.broadcasted_iota(jnp.int32, (tile, lanes), 0) == (
                    lax.broadcasted_iota(jnp.int32, (tile, lanes), 1)
                )
                out[0, p] += jnp.where(eye, d[0], 0.0)

    return pl.pallas_call(
        kernel,
        grid_spec=pltpu.PrefetchScalarGridSpec(
            num_scalar_prefetch=3,
            grid=(count, cols // SUB),
            in_specs=[
                pl.BlockSpec((1, tile, SUB, lanes), lambda n, g, *_: (n, 0, g, 0)),
                pl.BlockSpec((1, tile, SUB, lanes), lambda n, g, *_: (n, 0, g, 0)),
                pl.BlockSpec((SUB, lanes), lambda n, g, *_: (g, 0)),
                pl.BlockSpec((SUB, lanes), lambda n, g, *_: (g, 0)),
                pl.BlockSpec((1, 1, lanes), lambda n, g, *_: (n, 0, 0)),
            ],
            out_specs=pl.BlockSpec((1, SUB, tile, lanes), lambda n, g, *_: (n, g, 0, 0)),
        ),
        out_shape=jax.ShapeDtypeStruct((count, cols, tile, lanes), F32),
        compiler_params=params(2),
        cost_estimate=cost(0, count * cols * tile * lanes * 12),
        name="place_rows",
    )(rows0, rows1, where, first, second, cols0, cols1, diag[:, None, :])


def eliminate(block):
    tile = block.shape[0]
    lane = lax.broadcasted_iota(jnp.int32, (1, tile), 1)
    sub = lax.broadcasted_iota(jnp.int32, (tile, 1), 0)

    def body(j, carry):
        whole = block[...]
        row = block[pl.ds(j, 1), :]
        here = lane == j
        pivot = jnp.sum(jnp.where(here, row, 0.0), axis=1, keepdims=True)
        root = lax.rsqrt(pivot)
        root = root * (1.5 - 0.5 * pivot * root * root)
        row = jnp.where(here, root, row * root)
        column = jnp.sum(jnp.where(here, whole, 0.0), axis=1, keepdims=True) * root
        column = jnp.where(sub > j, column, 0.0)
        kept = jnp.where(here & (sub > j), 0.0, whole)
        block[...] = jnp.where(sub == j, row, kept - column * row)
        return carry

    lax.fori_loop(0, tile, body, 0)
    low = lax.broadcasted_iota(jnp.int32, (tile, tile), 0) >= (
        lax.broadcasted_iota(jnp.int32, (tile, tile), 1)
    )
    return jnp.where(low, block[...], 0.0)


def inverse_factor(pivot, tile):
    order = pivot.shape[0]
    steps = order // tile

    def kernel(a, high, low, m, block):
        m[...] = a[...]
        for s in range(steps):
            top, end = s * tile, (s + 1) * tile
            block[...] = m[top:end, top:end]
            inverse = eliminate(block)
            if end < order:
                right = dot_full(inverse, m[top:end, end:], ((1,), (0,)))
                for t in range(s + 1, steps):
                    left = right[:, t * tile - end : (t + 1) * tile - end]
                    span = slice(t * tile, (t + 1) * tile)
                    m[span, t * tile :] -= dot_full(
                        left, right[:, t * tile - end :], ((0,), (0,))
                    )
                    m[span, top:end] = -dot_full(left, inverse, ((0,), (0,)))
            m[top:end, top:end] = inverse
            if s > 0:
                done = dot_full(inverse, m[top:end, :top], ((1,), (0,)))
                m[top:end, :top] = done
                for t in range(s + 1, steps):
                    span = slice(t * tile, (t + 1) * tile)
                    left = right[:, t * tile - end : (t + 1) * tile - end]
                    m[span, :top] -= dot_full(left, done, ((0,), (0,)))
            if end < order:
                m[top:end, end:] = jnp.zeros((tile, order - end), F32)
        head, tail = split(m[...])
        high[...] = head
        low[...] = tail

    return pl.pallas_call(
        kernel,
        in_specs=[pl.BlockSpec(memory_space=pltpu.VMEM)],
        out_specs=[pl.BlockSpec(memory_space=pltpu.VMEM)] * 2,
        out_shape=[jax.ShapeDtypeStruct((order, order), BF16)] * 2,
        scratch_shapes=[pltpu.VMEM((order, order), F32), pltpu.VMEM((tile, tile), F32)],
        compiler_params=pltpu.CompilerParams(vmem_limit_bytes=VMEM_LIMIT),
        cost_estimate=cost(100e9, order * order * 8),
        name="inverse_factor",
    )(pivot)


def solve_rows(gathered, high, low, column_index):
    columns, rows, local = gathered.shape
    order = high.shape[0]
    tile = 128
    pieces = local // tile
    step = 256

    def kernel(me, f, h, l, out_h, out_l, out_f, acc):
        total = jnp.zeros((step, order), F32)
        for c in range(columns):
            fh, fl = split(f[c])
            spans = [
                slice((n * columns + c) * tile, (n * columns + c + 1) * tile) for n in range(pieces)
            ]
            gh = jnp.concatenate([h[:, s] for s in spans], axis=1)
            gl = jnp.concatenate([l[:, s] for s in spans], axis=1)
            total += dot_nt(fh, gh) + (dot_nt(fh, gl) + dot_nt(fl, gh))
        acc[...] = total
        xh, xl = split(total)
        out_h[...] = xh
        out_l[...] = xl
        for n in range(pieces):
            at = pl.multiple_of((n * columns + me[0]) * tile, tile)
            out_f[n] = acc[:, pl.ds(at, tile)]

    return pl.pallas_call(
        kernel,
        grid_spec=pltpu.PrefetchScalarGridSpec(
            num_scalar_prefetch=1,
            grid=(rows // step,),
            in_specs=[
                pl.BlockSpec((columns, step, local), lambda r, *_: (0, r, 0)),
                pl.BlockSpec((order, order), lambda r, *_: (0, 0)),
                pl.BlockSpec((order, order), lambda r, *_: (0, 0)),
            ],
            out_specs=[
                pl.BlockSpec((step, order), lambda r, *_: (r, 0)),
                pl.BlockSpec((step, order), lambda r, *_: (r, 0)),
                pl.BlockSpec((pieces, step, tile), lambda r, *_: (0, r, 0)),
            ],
            scratch_shapes=[pltpu.VMEM((step, order), F32)],
        ),
        out_shape=[
            jax.ShapeDtypeStruct((rows, order), BF16),
            jax.ShapeDtypeStruct((rows, order), BF16),
            jax.ShapeDtypeStruct((pieces, rows, tile), F32),
        ],
        compiler_params=params(),
        cost_estimate=cost(6 * rows * order * order, rows * order * 8),
        name="solve_rows",
    )(column_index, gathered, high, low)


def solve_columns(rows, high, low, places):
    blocks, cols, tile, lanes = rows.shape
    order = high.shape[0]
    wide = 4
    deep = 256

    def kernel(f, h, l, out_h, out_l):
        full = jnp.concatenate(
            [
                jnp.concatenate([f[places[b], p] for p in range(wide)], axis=1)
                for b in range(order // tile)
            ],
            axis=0,
        )
        fh, fl = split(full)
        for r in range(order // deep):
            span, depth = slice(r * deep, (r + 1) * deep), (r + 1) * deep
            lh, ll = h[span, :depth], l[span, :depth]
            x = dot(lh, fh[:depth]) + (dot(lh, fl[:depth]) + dot(ll, fh[:depth]))
            xh, xl = split(x)
            out_h[span, :] = xh
            out_l[span, :] = xl

    return pl.pallas_call(
        kernel,
        grid=(cols // wide,),
        in_specs=[
            pl.BlockSpec((blocks, wide, tile, lanes), lambda g: (0, g, 0, 0)),
            pl.BlockSpec((order, order), lambda g: (0, 0)),
            pl.BlockSpec((order, order), lambda g: (0, 0)),
        ],
        out_specs=[pl.BlockSpec((order, wide * lanes), lambda g: (0, g))] * 2,
        out_shape=[jax.ShapeDtypeStruct((order, cols * lanes), BF16)] * 2,
        compiler_params=params(),
        cost_estimate=cost(4 * order * order * cols * lanes, order * cols * lanes * 8),
        name="solve_columns",
    )(rows, high, low)


def own_part(child, half, own_maps, diag, where, left, right, panel):
    _, _, rows, tile, cols, lanes = child.shape
    rowmap, colmap = own_maps
    xh, xl = left
    ch, cl = right
    order = xh.shape[1]
    count = panel.shape[0]
    block = min(4, rows)

    def kernel(half_ref, map_ref, where_ref, u, c, d, lh, ll, rh, rl, pan, out, flat):
        g, n = pl.program_id(0), pl.program_id(1)
        columns = c[...]
        for b in range(block):
            j = n * block + b

            def body(step, carry):
                for r in range(SUB):
                    o = step * SUB + r
                    at = pl.multiple_of((b * tile + o) * SUB, SUB)
                    flat[pl.ds(at, SUB), :] = gathered_row(
                        map_ref[j, o], lambda s: u[0, 0, b, s], columns
                    )
                return carry

            lax.fori_loop(0, tile // SUB, body, 0)
            for p in range(SUB):
                @pl.when(where_ref[j] == g * SUB + p)
                def _():
                    eye = lax.broadcasted_iota(jnp.int32, (tile, lanes), 0) == (
                        lax.broadcasted_iota(jnp.int32, (tile, lanes), 1)
                    )
                    flat[pl.ds(b * tile * SUB + p, tile, SUB), :] += jnp.where(eye, d[b], 0.0)
        lhs_h, lhs_l = lh[...], ll[...]
        for pair in range(SUB // 2):
            span = slice(pair * 2 * lanes, (pair + 1) * 2 * lanes)
            update = dot(lhs_h, rh[:, span]) + (dot(lhs_h, rl[:, span]) + dot(lhs_l, rh[:, span]))
            for b in range(block):
                for side in range(2):
                    at = pl.ds(b * tile * SUB + 2 * pair + side, tile, SUB)
                    part = update[b * tile : (b + 1) * tile, side * lanes : (side + 1) * lanes]
                    flat[at, :] -= part

        @pl.when(g == 0)
        def _():
            for b in range(block):
                for p in range(count):
                    flat[pl.ds(b * tile * SUB + p, tile, SUB), :] = pan[
                        p, b * tile : (b + 1) * tile, :
                    ]

        out[...] = flat[...].reshape(out.shape)

    return pl.pallas_call(
        kernel,
        grid_spec=pltpu.PrefetchScalarGridSpec(
            num_scalar_prefetch=3,
            grid=(cols // SUB, rows // block),
            in_specs=[
                pl.BlockSpec(
                    (1, 1, block, tile, SUB, lanes), lambda g, n, h, *_: (0, h[0], n, 0, g, 0)
                ),
                pl.BlockSpec((SUB, lanes), lambda g, n, *_: (g, 0)),
                pl.BlockSpec((block, 1, lanes), lambda g, n, *_: (n, 0, 0)),
                pl.BlockSpec((block * tile, order), lambda g, n, *_: (n, 0)),
                pl.BlockSpec((block * tile, order), lambda g, n, *_: (n, 0)),
                pl.BlockSpec((order, SUB * lanes), lambda g, n, *_: (0, g)),
                pl.BlockSpec((order, SUB * lanes), lambda g, n, *_: (0, g)),
                pl.BlockSpec((count, block * tile, lanes), lambda g, n, *_: (0, n, 0)),
            ],
            out_specs=pl.BlockSpec((1, block, tile, SUB, lanes), lambda g, n, *_: (0, n, 0, g, 0)),
            scratch_shapes=[pltpu.VMEM((block * tile * SUB, lanes), F32)],
        ),
        out_shape=jax.ShapeDtypeStruct((1, rows, tile, cols, lanes), F32),
        compiler_params=params(2),
        cost_estimate=cost(
            6 * rows * tile * order * cols * lanes, rows * tile * cols * lanes * 8
        ),
        name="own_part",
    )(half, rowmap, where, child, colmap, diag[:, None, :], xh, xl, ch, cl, panel)


def add_first(front, block, rowmap, colmap):
    _, _, tile, cols, lanes = front.shape

    def kernel(map_ref, before, u, c, out):
        columns = c[...]

        def body(step, carry):
            for r in range(SUB):
                o = step * SUB + r
                value = gathered_row(map_ref[0, o], lambda s: u[0, s], columns)
                out[0, 0, o] = before[0, 0, o] + value
            return carry

        lax.fori_loop(0, tile // SUB, body, 0)

    spec = pl.BlockSpec((1, 1, tile, SUB, lanes), lambda g, *_: (0, 0, 0, g, 0))
    return pl.pallas_call(
        kernel,
        grid_spec=pltpu.PrefetchScalarGridSpec(
            num_scalar_prefetch=1,
            grid=(cols // SUB,),
            in_specs=[
                spec,
                pl.BlockSpec((1, tile, SUB, lanes), lambda g, *_: (0, 0, g, 0)),
                pl.BlockSpec((SUB, lanes), lambda g, *_: (g, 0)),
            ],
            out_specs=spec,
        ),
        out_shape=jax.ShapeDtypeStruct(front.shape, F32),
        input_output_aliases={1: 0},
        compiler_params=params(),
        cost_estimate=cost(0, tile * cols * lanes * 12),
        name="add_first",
    )(rowmap, front, block, colmap)


def add_tiles(front, sources, picks, stands, rowmap, colmap, first, count):
    _, _, tile, cols, lanes = front.shape
    width = len(sources)
    groups = cols // SUB
    picks, stands = picks.reshape(-1), stands.reshape(-1)

    def entry(slot, n, g):
        return (slot * count + n) * groups + g

    def kernel(map_ref, picks_ref, stands_ref, before, *refs):
        tiles, (c, out, flat) = refs[:width], refs[width:]
        n, g = pl.program_id(0), pl.program_id(1)
        columns = c[...]
        for slot in range(width):
            stand = stands_ref[entry(slot, n, g)]
            p = stand // 2

            @pl.when((stand >= 0) & (stand % 2 == 0))
            def _():
                flat[pl.ds(p, tile, SUB), :] = tiles[slot][0]

            @pl.when((stand >= 0) & (stand % 2 == 1))
            def _():
                flat[pl.ds(p, tile, SUB), :] = tiles[slot][0].T

        def body(step, carry):
            for r in range(SUB):
                o = step * SUB + r
                value = gathered_row(
                    map_ref[n + first, o],
                    lambda s: flat[pl.ds(pl.multiple_of(s * SUB, SUB), SUB), :],
                    columns,
                )
                out[0, 0, o] = before[0, 0, o] + value
            return carry

        lax.fori_loop(0, tile // SUB, body, 0)

    spec = pl.BlockSpec((1, 1, tile, SUB, lanes), lambda n, g, *_: (0, n + first, 0, g, 0))

    def tile_spec(slot):
        return pl.BlockSpec((1, tile, lanes), lambda n, g, m, k, t: (k[entry(slot, n, g)], 0, 0))

    return pl.pallas_call(
        kernel,
        grid_spec=pltpu.PrefetchScalarGridSpec(
            num_scalar_prefetch=3,
            grid=(count, groups),
            in_specs=[spec]
            + [tile_spec(slot) for slot in range(width)]
            + [pl.BlockSpec((SUB, lanes), lambda n, g, *_: (g, 0))],
            out_specs=spec,
            scratch_shapes=[pltpu.VMEM((tile * SUB, lanes), F32)],
        ),
        out_shape=jax.ShapeDtypeStruct(front.shape, F32),
        input_output_aliases={3: 0},
        compiler_params=params(2),
        cost_estimate=cost(0, count * tile * cols * lanes * 12),
        name="add_tiles",
    )(rowmap, picks, stands, front, *sources, colmap)


def triangle(row):
    return row * (row - 1) // 2


def lower_tables(exchanged, first, last, rows, parity, start, count):
    groups = rows // (SUB // 2)
    slot, n, g = np.meshgrid(
        np.arange(SUB // 2), np.arange(start, start + count), np.arange(groups), indexing="ij"
    )
    i = g * (SUB // 2) + slot
    row, col = (i, n) if exchanged else (n, i)
    mine = (row >= first) & (row < last) & (col >= 1)
    mine &= (col < row) if exchanged else (col <= row)
    picks = np.where(mine, triangle(row) - triangle(first) + col - 1, 0)
    flat = mine.reshape(SUB // 2, -1)
    held = picks.reshape(SUB // 2, -1).copy()
    for step in range(1, held.shape[1]):
        held[:, step] = np.where(flat[:, step], held[:, step], held[:, step - 1])
    stands = jnp.where(mine, 2 * (2 * slot + parity) + int(exchanged), -1)
    return held.reshape(mine.shape).astype(np.int32), stands.astype(jnp.int32)


def cross_tables(rows, parity, start, count):
    groups = rows // (SUB // 2)
    slot, n, g = np.meshgrid(
        np.arange(SUB // 2), np.arange(count), np.arange(groups), indexing="ij"
    )
    i = g * (SUB // 2) + slot
    picks = np.where(i >= 1, n * (rows - 1) + i - 1, n * (rows - 1))
    stands = jnp.where(i >= 1, 2 * (2 * slot + parity), -1)
    return picks.astype(np.int32), stands.astype(jnp.int32)


def on_device(child_update, child_map, parent_diag):
    grid_size = lax.axis_size(("cube", "row"))
    half_grid = grid_size // 2
    columns = lax.axis_size("col")
    position = lax.axis_index(("cube", "row"))
    column_index = lax.axis_index("col")
    sibling = position // half_grid
    within = position % half_grid
    _, _, rows, tile, cols, lanes = child_update.shape
    distance = half_grid.bit_length() - 1
    pivots = K // tile
    local = pivots // columns
    mirrored = (
        grid_size == pivots
        and half_grid == columns
        and lax.axis_size("row") == half_grid
        and cols == 2 * rows
    )
    own = sibling.astype(jnp.int32)[None]
    other = 1 - own

    starts = tile * jnp.arange(rows * grid_size, dtype=jnp.int32)
    sources = jnp.stack(
        [inverse_map(child_map[e].reshape(-1, tile), starts) for e in range(2)]
    )

    def row_maps(child):
        of = lax.dynamic_index_in_dim(sources, child, 0, keepdims=False)
        of = of.reshape(rows, 2, half_grid, tile)
        return lax.dynamic_index_in_dim(of, within, 2, keepdims=False)

    def col_maps(child):
        of = lax.dynamic_index_in_dim(sources, child, 0, keepdims=False)
        of = of.reshape(cols, columns, tile)
        return lax.dynamic_index_in_dim(of, column_index, 1, keepdims=False)

    own_halves, other_halves = row_maps(sibling), row_maps(1 - sibling)
    own_cols, other_cols = col_maps(sibling), col_maps(1 - sibling)
    own_rows = lax.dynamic_index_in_dim(own_halves, sibling, 1, keepdims=False)
    other_rows = lax.dynamic_index_in_dim(other_halves, sibling, 1, keepdims=False)
    trailing_cols = jnp.where(jnp.arange(cols)[:, None] < local, -1, other_cols)

    blocks = grid_size * jnp.arange(rows, dtype=jnp.int32) + position
    diag_tiles = parent_diag.reshape(-1, tile)

    def on_diagonal(block_rows):
        offset = block_rows - column_index
        return jnp.where(offset % columns == 0, offset // columns, -1).astype(jnp.int32)

    diag_rows = diag_tiles[blocks]

    panel_sent = pack_panel(child_update, other, local)
    panel_came = swapped(panel_sent, ("cube", "row"), distance)
    if mirrored:
        near = 1 + (rows * 11) // 16
        cuts = [(1, near), (near, rows)]
        lower_sent = [pack_lower(child_update, other, other, a, b) for a, b in cuts]
        pivot_sent = child_update[0, :, 0]
        pairs = [
            (r * columns + c, c * columns + r) for r in range(half_grid) for c in range(columns)
        ]
        lower_a = swapped(lower_sent[0], ("cube", "row"), distance)
        pivot_came = swapped(after(pivot_sent, panel_came), ("cube", "row"), distance)
        turned_a = lax.ppermute(lower_a, ("row", "col"), pairs)
        lower_b = swapped(after(lower_sent[1], lower_a), ("cube", "row"), distance)
        turned_b = lax.ppermute(after(lower_b, turned_a), ("row", "col"), pairs)
        sent = pack_cross(child_update, other, own)
        chain = [pivot_came, lower_b]
    else:
        pivot_sent = lax.dynamic_slice_in_dim(child_update[0, :, 0], 1 - sibling, 1, 0)
        pivot_came = swapped(after(pivot_sent, panel_came), ("cube", "row"), distance)
        sent = pack_all(child_update, other)
        chain = [panel_came, pivot_came]
    per = -(-(rows - 1) // 5)
    spans = [(at, min(per, rows - at)) for at in range(1, rows, per)]
    came = []
    for at, count in spans:
        part = after(sent[at - 1 : at - 1 + count], chain[-2])
        came.append(swapped(part, ("cube", "row"), distance))
        chain.append(came[-1])

    panel_own = pack_panel(child_update, own, local)

    def placed(tiles, row_map, col_map):
        offsets = jnp.arange(tile, dtype=jnp.int32)
        row_hot = (row_map[:, :, None] == offsets).astype(F32)
        col_hot = (col_map[:local, :, None] == offsets).astype(F32)
        done = jnp.einsum("jos,jpsv->jpov", row_hot, tiles, precision=lax.Precision.HIGHEST)
        return jnp.einsum("jpov,pqv->jopq", done, col_hot, precision=lax.Precision.HIGHEST)

    hits = on_diagonal(blocks)[:, None] == jnp.arange(local)
    eye = jnp.eye(tile, dtype=bool)[None, :, None, :] & hits[:, None, :, None]
    front_panel = placed(panel_own, own_rows, own_cols)
    front_panel += placed(panel_came, other_rows, other_cols)
    front_panel += jnp.where(eye, diag_rows[:, :, None, None], 0.0)

    pivot = lax.all_gather(front_panel[0], ("cube", "row", "col"), axis=0, tiled=False)
    pivot = pivot.reshape(grid_size, columns, tile, local, tile)[:pivots]
    pivot = jnp.transpose(pivot, (0, 2, 3, 1, 4)).reshape(K, K)
    high, low = inverse_factor(pivot, tile)

    gathered = lax.all_gather(
        front_panel.reshape(rows * tile, local * tile), "col", axis=0, tiled=False
    )
    left_h, left_l, panel = solve_rows(
        gathered, high, low, column_index.astype(jnp.int32)[None]
    )

    if mirrored:
        block_rows = half_grid * jnp.arange(2, dtype=jnp.int32) + within
        pivot_rows = place_rows(
            pivot_sent,
            pivot_came,
            ((own_halves[0], own_cols), (other_halves[0], other_cols)),
            diag_tiles[block_rows],
            on_diagonal(block_rows),
        )
        pivot_rows = lax.all_gather(pivot_rows, "row", axis=0, tiled=True)
        places = [2 * (b % half_grid) + b // half_grid for b in range(pivots)]
        first = lax.dynamic_slice_in_dim(pivot_came, sibling, 1, 0)
    else:
        pivot_rows = place_rows(
            lax.dynamic_slice_in_dim(child_update[0, :, 0], sibling, 1, 0),
            pivot_came,
            ((own_rows[:1], own_cols), (other_rows[:1], other_cols)),
            diag_rows[:1],
            on_diagonal(blocks[:1]),
        )
        mine = (jnp.arange(pivots) == position)[:, None, None, None]
        pivot_rows = lax.psum(jnp.where(mine, pivot_rows, 0.0), ("cube", "row"))
        places = list(range(pivots))
        first = pivot_came
    right_h, right_l = solve_columns(pivot_rows, high, low, places)

    front = own_part(
        child_update,
        own,
        (own_rows, own_cols),
        diag_rows,
        on_diagonal(blocks),
        (left_h, left_l),
        (right_h, right_l),
        panel,
    )
    front = add_first(front, first, other_rows[:1], trailing_cols)
    for (at, count), array in zip(spans, came):
        flat = array.reshape(-1, tile, tile)
        if mirrored:
            half = SUB // 2
            picks, stands = [], []
            arrays = []
            tables = [(flat, cross_tables(rows, 1 - sibling, at, count))]
            for exchanged, group in ((False, (lower_a, lower_b)), (True, (turned_a, turned_b))):
                for (a, b), source in zip(cuts, group):
                    tables.append(
                        (source, lower_tables(exchanged, a, b, rows, sibling, at, count))
                    )
            for source, (pick, stand) in tables:
                arrays += [source] * half
                picks.append(pick)
                stands.append(stand)
            picks, stands = jnp.concatenate(picks), jnp.concatenate(stands)
        else:
            arrays = [flat] * SUB
            shape = (SUB, count, cols // SUB)
            slot, n, g = (lax.broadcasted_iota(jnp.int32, shape, axis) for axis in range(3))
            picks, stands = n * cols + g * SUB + slot, 2 * slot
        front = add_tiles(front, arrays, picks, stands, other_rows, trailing_cols, at, count)
    return front


def solution(mesh):
    return jax.shard_map(
        on_device,
        mesh=mesh,
        in_specs=(P(("cube", "row"), None, None, None, "col", None), P(), P()),
        out_specs=P(("cube", "row"), None, None, "col", None),
        check_vma=False,
    )
```

time: 2160 us -> 1100 us (0.51)
  waiting for transfers between devices: 1290 us -> 386 us
  Pallas kernels: 0 us -> 609 us
  other arithmetic: 352 us -> 5.84 us
  matrix products: 332 us -> 8.81 us
  local copies, waits for them, and re-layouts: 155 us -> 45.7 us
    pallas_call x0 -> x16, Pallas kernels: none -> 609 us  [the longest x5 173 us: add_tiles(): pl.pallas_call(kernel, grid_spec=pltpu.PrefetchScalarGridSpec(num_scalar_...]
    ppermute x1 -> x9, waiting for transfers between devices: 720 us -> 276 us  [swapped(): return lax.ppermute(value, axis, pairs)]
    all_gather x2 -> x3, waiting for transfers between devices: 349 us -> 0.01 us  [the longest x1 0.01 us: on_device(): lax.all_gather(front_panel[0], ('cube', 'row', 'col'), axis=0, tiled=False)]
    dot_general x3 -> x4, matrix products: 267 us -> 8.81 us  [the longest x2 5.9 us: placed(): jnp.einsum('jos,jpsv->jpov', row_hot, tiles, precision=lax.Precision.HIGH...]
    another operation x33 -> x1, other arithmetic: 256 us -> 0.04 us  [on_device(): jnp.stack([inverse_map(child_map[e].reshape(-1, tile), starts) for e in r...]
    psum x2 -> x0, waiting for transfers between devices: 218 us -> none  [the longest x1 156 us: broadcast(): return lax.psum(jnp.where(mine, value, jnp.zeros_like(value)), axis)]
    ppermute x0 -> x2, waiting for transfers between devices: none -> 110 us  [the longest x1 110 us: on_device(): turned_a = lax.ppermute(lower_a, ('row', 'col'), pairs)]
    another operation x29 -> x0, matrix products: 64.5 us -> none  [the longest x15 41.4 us: on_device(): jax.scipy.linalg.solve_triangular(factor, flat.T, lower=True)]
  transfers between devices with their start and end apart: 5 -> 14, of which waited for: 5 -> 5; matrix products, arithmetic and copies ran while one was open for 1% -> 5% of each run, Pallas kernels for 0% -> 52%
where the time goes in v1:
time: 1100 us; the launch traced here: 1080 us
  Pallas kernels  609 us (55%)
  waiting for transfers between devices  386 us (35%)
  local copies, waits for them, and re-layouts  45.7 us (4%)
  starting transfers between devices  15.7 us (1%)
  between operations  14.1 us (1%)
    ppermute x9, waiting for transfers between devices, swapped(): return lax.ppermute(value, axis, pairs)  276 us
    pallas_call x5, Pallas kernels, add_tiles(): pl.pallas_call(kernel, grid_spec=pltpu.PrefetchScalarGridSpec(num_scalar_...  173 us
    pallas_call x1, Pallas kernels, own_part(): pl.pallas_call(kernel, grid_spec=pltpu.PrefetchScalarGridSpec(num_scalar_...  168 us
    pallas_call x1, Pallas kernels, inverse_factor(): pl.pallas_call(kernel, in_specs=[pl.BlockSpec(memory_space=pltpu.VMEM)],...  131 us
    ppermute x1, waiting for transfers between devices, on_device(): turned_a = lax.ppermute(lower_a, ('row', 'col'), pairs)  110 us
    pallas_call x1, Pallas kernels, pack_cross(): pl.pallas_call(kernel, grid_spec=pltpu.PrefetchScalarGridSpec(num_scalar_...  25 us
    pallas_call x2, Pallas kernels, pack_lower(): pl.pallas_call(kernel, grid_spec=pltpu.PrefetchScalarGridSpec(num_scalar_...  23.2 us
    pallas_call x1, Pallas kernels, solve_columns(): pl.pallas_call(kernel, grid=(cols // wide,), in_specs=[pl.BlockSpec((bloc...  22.7 us
  transfers between devices with their start and end apart: 14, of which 5 were waited for; matrix products, arithmetic and copies ran while one was open for 5% of the time, Pallas kernels for 52%

profile of v1, /device:TPU:6, one launch (start us, length us, event | category | flops | bytes accessed | tf_op | source)
XLA Modules:
  0.0 1084.9 jit_solution(6061544248672597027)
XLA Ops:
  6.5 10.6 pack_panel.3
  18.0 10.6 pack_panel.2
  29.1 4.4 select_reduce_fusion
  33.7 3.7 fusion.6
  37.4 27.3 %collective-permute-done = f32[16,2,128,128]{3,2,1,0:T(8,128)S(1)} collective-permute-done((f32[16,2,128,128]{3,2,1,0:T(8,128)}, f32[16,2,128,128]{3,2,1,0:T(8,128)S(1)}, u32[]{:S(2)}, u32[]{:S(2)}) %collective-permute-start) | collective-permute-done | bytes 2097184 | tf_op jit(solution)/shard_map/ppermute | solution.py:29
  64.7 2.2 fusion.2
  67.0 1.2 fusion
  68.3 1.7 bitcast_add_fusion
  70.7 2.3 copy.144
  73.0 4.0 reshape.292
  77.5 4.6 slice_bitcast_fusion.u0
  82.7 1.1 gather_fusion.1
  86.8 98.2 %collective-permute-done.1.u1 = f32[2,128,32,128]{3,2,1,0:T(8,128)} collective-permute-done((f32[2,128,32,128]{3,2,1,0:T(8,128)}, f32[2,128,32,128]{3,2,1,0:T(8,128)}, u32[]{:S(2)}, u32[]{:S(2)}) %collective-permute-start.1) | collective-permute-done | bytes 4194336 | tf_op jit(solution)/shard_map/ppermute | solution.py:29
  185.0 18.1 %place_rows.1 = f32[2,32,128,128]{3,2,1,0:T(8,128)} custom-call(s32[2,128]{1,0:T(2,128)} %bitcast.106, s32[2,128]{1,0:T(2,128)} %bitcast.107, s32[2]{0:T(128)} %compare_select_fusion.2.where_ref, f32[2,128,32,128]{3,2,1,0:T(8,128)} %slice_bitcast_fusion.u0, f32[2,128,32,128]{3,2,1,0:T(8,128)} %collective-permute-done.1.u1, s32[32,128]{1,0:T(8,128)} %bitcast.99, ...), custom_call_target="tpu_custom_call" | custom-call | bytes 12582912 | tf_op jit(solution)/shard_map/place_rows/pallas_call | solution.py:205
  203.1 15.1 %pack_lower.2 = f32[66,128,128]{2,1,0:T(8,128)} custom-call(s32[1]{0:T(128)S(6)} %sub.89.half_ref.parity_ref, s32[1]{0:T(128)S(6)} %sub.89.half_ref.parity_ref, f32[1,2,16,128,32,128]{5,4,3,2,1,0:T(8,128)} %raw.9), custom_call_target="tpu_custom_call" | custom-call | bytes 27394048 | tf_op jit(solution)/shard_map/pack_lower/pallas_call | solution.py:128
  218.2 0.9 collective-permute-start.3
  219.1 92.7 %collective-permute-done.3.refs_4_.refs_5_.refs_6_.refs_7_ = f32[66,128,128]{2,1,0:T(8,128)} collective-permute-done((f32[66,128,128]{2,1,0:T(8,128)}, f32[66,128,128]{2,1,0:T(8,128)}, u32[]{:S(2)}, u32[]{:S(2)}) %collective-permute-start.3) | collective-permute-done | bytes 4325408 | tf_op jit(solution)/shard_map/ppermute | solution.py:29
  311.8 4.4 collective-permute-start.5
  316.3 8.2 pack_lower.3
  324.4 25.0 %pack_cross.1 = f32[15,15,128,128]{3,2,1,0:T(8,128)} custom-call(s32[1]{0:T(128)S(6)} %sub.89.half_ref.parity_ref, s32[1]{0:T(128)} %bitcast.7.half_ref.parity_ref, f32[1,2,16,128,32,128]{5,4,3,2,1,0:T(8,128)} %raw.9), custom_call_target="tpu_custom_call" | custom-call | bytes 50331648 | tf_op jit(solution)/shard_map/pack_cross/pallas_call | solution.py:95
  349.6 1.0 collective-permute-start.4
  350.7 10.8 fusion.42
  361.5 1.1 collective-permute-start.2
  362.9 0.7 reshape.258.stands_ref
  364.7 0.7 reshape.254.stands_ref
  365.6 0.7 reshape.252.stands_ref
  366.5 0.7 reshape.260.stands_ref
  367.8 0.7 broadcast_select_fusion.c.refs_20_
  368.5 3.1 constant_dynamic-slice_fusion.9.u
  371.6 57.8 %collective-permute-done.4.refs_8_.refs_9_.refs_10_.refs_11_ = f32[54,128,128]{2,1,0:T(8,128)} collective-permute-done((f32[54,128,128]{2,1,0:T(8,128)}, f32[54,128,128]{2,1,0:T(8,128)}, u32[]{:S(2)}, u32[]{:S(2)}) %collective-permute-start.4) | collective-permute-done | bytes 3538976 | tf_op jit(solution)/shard_map/ppermute | solution.py:29
  429.3 1.0 collective-permute-start.7
  430.4 109.5 %collective-permute-done.5.refs_12_.refs_13_.refs_14_.refs_15_ = f32[66,128,128]{2,1,0:T(8,128)} collective-permute-done((f32[66,128,128]{2,1,0:T(8,128)}, f32[66,128,128]{2,1,0:T(8,128)}, u32[]{:S(2)}, u32[]{:S(2)}) %collective-permute-start.5) | collective-permute-done | bytes 4325408 | tf_op jit(solution)/shard_map/ppermute | solution.py:664
  539.9 2.1 collective-permute-start.6
  542.0 1.5 collective-permute-start.8
  543.5 5.2 copy.132
  548.7 5.5 reshape.266.a
  554.2 130.8 %inverse_factor.1 = (bf16[1024,1024]{1,0:T(8,128)(2,1)}, bf16[1024,1024]{1,0:T(8,128)(2,1)}) custom-call(f32[1024,1024]{1,0:T(8,128)} %reshape.266.a), custom_call_target="tpu_custom_call" | custom-call | flops 99999997952 | bytes 8388608 | tf_op jit(solution)/shard_map/inverse_factor/pallas_call | solution.py:285
  685.1 0.9 collective-permute-start.9
  686.0 1.1 collective-permute-start.10
  687.1 18.8 %solve_rows.1 = (bf16[2048,1024]{1,0:T(8,128)(2,1)}, bf16[2048,1024]{1,0:T(8,128)(2,1)}, f32[2,2048,128]{2,1,0:T(8,128)}) custom-call(s32[1]{0:T(128)} %bitcast.15.me, f32[4,2048,256]{2,1,0:T(8,128)} %all-gather.4.cloned.1.call-done.f, bf16[1024,1024]{1,0:T(8,128)(2,1)} %get-tuple-element.20.h, bf16[1024,1024]{1,0:T(8,128)(2,1)} %get-tuple-element.21.l), custom_call_target="tpu_custom_call" | custom-call | flops 12884901888 | bytes 16777216 | tf_op jit(solution)/shard_map/solve_rows/pallas_call | solution.py:322
  705.9 22.7 %solve_columns.1 = (bf16[1024,4096]{1,0:T(8,128)(2,1)}, bf16[1024,4096]{1,0:T(8,128)(2,1)}) custom-call(f32[8,32,128,128]{3,2,1,0:T(8,128)} %all-gather.8.cloned.1.call-done.f, bf16[1024,1024]{1,0:T(8,128)(2,1)} %get-tuple-element.20.h, bf16[1024,1024]{1,0:T(8,128)(2,1)} %get-tuple-element.21.l), custom_call_target="tpu_custom_call" | custom-call | flops 17179869184 | bytes 33554432 | tf_op jit(solution)/shard_map/solve_columns/pallas_call | solution.py:373
  728.6 167.5 %own_part.1.before = f32[1,16,128,32,128]{4,3,2,1,0:T(8,128)} custom-call(s32[1]{0:T(128)} %bitcast.7.half_ref.parity_ref, s32[16,128]{1,0:T(8,128)} %bitcast.103, s32[16]{0:T(128)} %copy-done.23, f32[1,2,16,128,32,128]{5,4,3,2,1,0:T(8,128)} %raw.9, s32[32,128]{1,0:T(8,128)} %bitcast.100, f32[16,1,128]{2,1,0:T(1,128)} %bitcast.101, ...), custom_call_target="tpu_custom_call" | custom-call | flops 51539607552 | bytes 67108864 | tf_op jit(solution)/shard_map/own_part/pallas_call | solution.py:441
  896.2 8.3 add_first.1.before
  904.4 36.3 %add_tiles.5.before = f32[1,16,128,32,128]{4,3,2,1,0:T(8,128)} custom-call(s32[16,128]{1,0:T(8,128)} %bitcast.81, s32[240]{0:T(256)} %constant.282.picks_ref, s32[240]{0:T(256)} %reshape.260.stands_ref, f32[1,16,128,32,128]{4,3,2,1,0:T(8,128)} %add_first.1.before, f32[45,128,128]{2,1,0:T(8,128)} %bitcast.74, ...), custom_call_target="tpu_custom_call", output_to_operand_aliasing={{}: (3, {})} | custom-call | bytes 18874368 | tf_op jit(solution)/shard_map/add_tiles/pallas_call | solution.py:549
  940.7 35.3 %add_tiles.6.before = f32[1,16,128,32,128]{4,3,2,1,0:T(8,128)} custom-call(s32[16,128]{1,0:T(8,128)} %bitcast.82, s32[240]{0:T(256)} %constant.280.picks_ref, s32[240]{0:T(256)} %reshape.258.stands_ref, f32[1,16,128,32,128]{4,3,2,1,0:T(8,128)} %add_tiles.5.before, ...), custom_call_target="tpu_custom_call", output_to_operand_aliasing={{}: (3, {})} | custom-call | bytes 18874368 | tf_op jit(solution)/shard_map/add_tiles/pallas_call | solution.py:549
  976.0 34.6 %add_tiles.7.before = f32[1,16,128,32,128]{4,3,2,1,0:T(8,128)} custom-call(s32[16,128]{1,0:T(8,128)} %bitcast.83, s32[240]{0:T(256)} %constant.278.picks_ref, s32[240]{0:T(256)} %reshape.256.stands_ref, f32[1,16,128,32,128]{4,3,2,1,0:T(8,128)} %add_tiles.6.before, ...), custom_call_target="tpu_custom_call", output_to_operand_aliasing={{}: (3, {})} | custom-call | bytes 18874368 | tf_op jit(solution)/shard_map/add_tiles/pallas_call | solution.py:549
  1010.6 33.9 %add_tiles.8.before = f32[1,16,128,32,128]{4,3,2,1,0:T(8,128)} custom-call(s32[16,128]{1,0:T(8,128)} %bitcast.84, s32[240]{0:T(256)} %constant.276.picks_ref, s32[240]{0:T(256)} %reshape.254.stands_ref, f32[1,16,128,32,128]{4,3,2,1,0:T(8,128)} %add_tiles.7.before, ...), custom_call_target="tpu_custom_call", output_to_operand_aliasing={{}: (3, {})} | custom-call | bytes 18874368 | tf_op jit(solution)/shard_map/add_tiles/pallas_call | solution.py:549
  1044.5 33.4 %add_tiles.9 = f32[1,16,128,32,128]{4,3,2,1,0:T(8,128)} custom-call(s32[16,128]{1,0:T(8,128)} %bitcast.85, s32[240]{0:T(256)} %constant.274.picks_ref, s32[240]{0:T(256)} %reshape.252.stands_ref, f32[1,16,128,32,128]{4,3,2,1,0:T(8,128)} %add_tiles.8.before, f32[45,128,128]{2,1,0:T(8,128)} %bitcast.40.refs_0_.refs_1_.refs_2_.refs_3_, ...), custom_call_target="tpu_custom_call", output_to_operand_aliasing={{}: (3, {})} | custom-call | bytes 18874368 | tf_op jit(solution)/shard_map/add_tiles/pallas_call | solution.py:549
  (104 shorter events, 8.7 us)
Async XLA Ops:
  6.5 22.0 %copy-start = (f32[16384]{0:T(1024)S(1)}, f32[16384]{0:T(1024)}, u32[]{:S(2)}) copy-start(f32[16384]{0:T(1024)} %param.80) | copy-start | bytes 196612
  6.5 537.0 %all-gather.6.cloned.1.call-start = ((), (), s32[]{:S(2)}) async-start(), calls=%async_computation.1 | async-start | bytes 4325376 | tf_op jit(solution)/shard_map/all_gather | solution.py:697
  6.5 11.2 %copy-start.5 = (s32[2,16384]{1,0:T(2,128)S(1)}, s32[2,16384]{1,0:T(2,128)}, u32[]{:S(2)}) copy-start(s32[2,16384]{1,0:T(2,128)} %param.79) | copy-start | bytes 393220
  17.2 47.6 %collective-permute-start = (f32[16,2,128,128]{3,2,1,0:T(8,128)}, f32[16,2,128,128]{3,2,1,0:T(8,128)S(1)}, u32[]{:S(2)}, u32[]{:S(2)}) collective-permute-start(f32[16,2,128,128]{3,2,1,0:T(8,128)} %pack_panel.3), channel_id=1, source_target_pairs={{0,16},{4,20},{8,24},{12,28},{16,0},{20,4},{24,8},{28,12},{1,17},{... | collective-permute-start | bytes 6291464 | tf_op jit(solution)/shard_map/ppermute | solution.py:29
  17.9 15.8 %copy-start.23 = (s32[16]{0:T(128)}, s32[16]{0:T(128)S(1)}, u32[]{:S(2)}) copy-start(s32[16]{0:T(128)S(1)} %compare_select_fusion.3.where_ref) | copy-start | bytes 196
  29.1 39.1 %copy-start.6 = (f32[16,128]{1,0:T(8,128)}, f32[16,128]{1,0:T(8,128)S(1)}, u32[]{:S(2)}) copy-start(f32[16,128]{1,0:T(8,128)S(1)} %gather_fusion) | copy-start | bytes 24580
  33.6 33.3 %copy-start.7 = (s32[16,1,1,128]{3,2,1,0:T(1,128)}, s32[16,1,1,128]{3,2,1,0:T(1,128)S(1)}, u32[]{:S(2)}) copy-start(s32[16,1,1,128]{3,2,1,0:T(1,128)S(1)} %constant_dynamic-slice_fusion.5) | copy-start | bytes 24580
  33.7 33.3 %copy-start.3 = (s32[16,1,1,128]{3,2,1,0:T(1,128)}, s32[16,1,1,128]{3,2,1,0:T(1,128)S(1)}, u32[]{:S(2)}) copy-start(s32[16,1,1,128]{3,2,1,0:T(1,128)S(1)} %constant_dynamic-slice_fusion.7) | copy-start | bytes 24580
  70.6 616.5 %all-gather.4.cloned.1.call-start = ((), (), s32[]{:S(2)}) async-start(), calls=%async_computation | async-start | bytes 10485760 | tf_op jit(solution)/shard_map/all_gather | solution.py:702
  77.0 628.9 %all-gather.8.cloned.1.call-start = ((), (), s32[]{:S(2)}) async-start(), calls=%async_computation.2 | async-start | bytes 20971520 | tf_op jit(solution)/shard_map/all_gather | solution.py:718
  82.2 102.8 %collective-permute-start.1 = (f32[2,128,32,128]{3,2,1,0:T(8,128)}, f32[2,128,32,128]{3,2,1,0:T(8,128)}, u32[]{:S(2)}, u32[]{:S(2)}) collective-permute-start(f32[2,128,32,128]{3,2,1,0:T(8,128)} %slice_bitcast_fusion.u0), channel_id=1, source_target_pairs={{0,16},{4,20},{8,24},{12,28},{16,0},{20,4},{24,8},{28,12},{1,17},{... | collective-permute-start | bytes 12582920 | tf_op jit(solution)/shard_map/ppermute | solution.py:29
  218.2 93.6 %collective-permute-start.3 = (f32[66,128,128]{2,1,0:T(8,128)}, f32[66,128,128]{2,1,0:T(8,128)}, u32[]{:S(2)}, u32[]{:S(2)}) collective-permute-start(f32[66,128,128]{2,1,0:T(8,128)} %pack_lower.2), channel_id=1, source_target_pairs={{0,16},{4,20},{8,24},{12,28},{16,0},{20,4},{24,8},{28,12},{1,17},{... | collective-permute-start | bytes 12976136 | tf_op jit(solution)/shard_map/ppermute | solution.py:29
  311.8 228.1 %collective-permute-start.5 = (f32[66,128,128]{2,1,0:T(8,128)}, f32[66,128,128]{2,1,0:T(8,128)}, u32[]{:S(2)}, u32[]{:S(2)}) collective-permute-start(f32[66,128,128]{2,1,0:T(8,128)} %collective-permute-done.3.refs_4_.refs_5_.refs_6_.refs_7_), channel_id=1, source_target_pairs={{0,0},{1,4},{2,8},{3,12},{4,1},{5,5},{6,9},{7,13},{8,2},{9,6},{10,... | collective-permute-start | bytes 12976136 | tf_op jit(solution)/shard_map/ppermute | solution.py:664
  349.5 13.1 %copy-start.8 = (s32[4,3,4]{0,2,1:T(4,128)S(1)}, s32[4,3,4]{0,2,1:T(4,128)}, u32[]{:S(2)}) copy-start(s32[4,3,4]{0,2,1:T(4,128)} %constant.239.clone) | copy-start | bytes 580
  349.5 13.1 %copy-start.9 = (pred[4,3,4]{0,2,1:T(4,128)(4,1)S(1)}, pred[4,3,4]{0,2,1:T(4,128)(4,1)}, u32[]{:S(2)}) copy-start(pred[4,3,4]{0,2,1:T(4,128)(4,1)} %constant.269.clone) | copy-start | bytes 148
  349.5 13.1 %copy-start.10 = (pred[4,3,4]{0,2,1:T(4,128)(4,1)S(1)}, pred[4,3,4]{0,2,1:T(4,128)(4,1)}, u32[]{:S(2)}) copy-start(pred[4,3,4]{0,2,1:T(4,128)(4,1)} %constant.268.clone) | copy-start | bytes 148
  349.5 13.1 %copy-start.11 = (pred[4,3,4]{0,2,1:T(4,128)(4,1)S(1)}, pred[4,3,4]{0,2,1:T(4,128)(4,1)}, u32[]{:S(2)}) copy-start(pred[4,3,4]{0,2,1:T(4,128)(4,1)} %constant.263.clone) | copy-start | bytes 148
  349.5 13.1 %copy-start.12 = (pred[4,3,4]{0,2,1:T(4,128)(4,1)S(1)}, pred[4,3,4]{0,2,1:T(4,128)(4,1)}, u32[]{:S(2)}) copy-start(pred[4,3,4]{0,2,1:T(4,128)(4,1)} %constant.262.clone) | copy-start | bytes 148
  349.5 13.1 %copy-start.13 = (pred[4,3,4]{0,2,1:T(4,128)(4,1)S(1)}, pred[4,3,4]{0,2,1:T(4,128)(4,1)}, u32[]{:S(2)}) copy-start(pred[4,3,4]{0,2,1:T(4,128)(4,1)} %constant.261.clone) | copy-start | bytes 148
  349.5 13.1 %copy-start.14 = (pred[4,3,4]{0,2,1:T(4,128)(4,1)S(1)}, pred[4,3,4]{0,2,1:T(4,128)(4,1)}, u32[]{:S(2)}) copy-start(pred[4,3,4]{0,2,1:T(4,128)(4,1)} %constant.260.clone) | copy-start | bytes 148
  349.5 13.1 %copy-start.15 = (pred[4,3,4]{0,2,1:T(4,128)(4,1)S(1)}, pred[4,3,4]{0,2,1:T(4,128)(4,1)}, u32[]{:S(2)}) copy-start(pred[4,3,4]{0,2,1:T(4,128)(4,1)} %constant.256.clone) | copy-start | bytes 148
  349.5 13.1 %copy-start.16 = (pred[4,3,4]{0,2,1:T(4,128)(4,1)S(1)}, pred[4,3,4]{0,2,1:T(4,128)(4,1)}, u32[]{:S(2)}) copy-start(pred[4,3,4]{0,2,1:T(4,128)(4,1)} %constant.255.clone) | copy-start | bytes 148
  349.5 13.1 %copy-start.17 = (pred[4,3,4]{0,2,1:T(4,128)(4,1)S(1)}, pred[4,3,4]{0,2,1:T(4,128)(4,1)}, u32[]{:S(2)}) copy-start(pred[4,3,4]{0,2,1:T(4,128)(4,1)} %constant.251.clone) | copy-start | bytes 148
  349.6 13.0 %copy-start.18 = (pred[4,3,4]{0,2,1:T(4,128)(4,1)S(1)}, pred[4,3,4]{0,2,1:T(4,128)(4,1)}, u32[]{:S(2)}) copy-start(pred[4,3,4]{0,2,1:T(4,128)(4,1)} %constant.250.clone) | copy-start | bytes 148
  349.6 13.0 %copy-start.19 = (pred[4,3,4]{0,2,1:T(4,128)(4,1)S(1)}, pred[4,3,4]{0,2,1:T(4,128)(4,1)}, u32[]{:S(2)}) copy-start(pred[4,3,4]{0,2,1:T(4,128)(4,1)} %constant.244.clone) | copy-start | bytes 148
  349.6 13.0 %copy-start.20 = (pred[4,3,4]{0,2,1:T(4,128)(4,1)S(1)}, pred[4,3,4]{0,2,1:T(4,128)(4,1)}, u32[]{:S(2)}) copy-start(pred[4,3,4]{0,2,1:T(4,128)(4,1)} %constant.243.clone) | copy-start | bytes 148
  349.6 13.0 %copy-start.21 = (pred[4,3,4]{0,2,1:T(4,128)(4,1)S(1)}, pred[4,3,4]{0,2,1:T(4,128)(4,1)}, u32[]{:S(2)}) copy-start(pred[4,3,4]{0,2,1:T(4,128)(4,1)} %constant.241.clone) | copy-start | bytes 148
  349.6 13.0 %copy-start.22 = (pred[4,3,4]{0,2,1:T(4,128)(4,1)S(1)}, pred[4,3,4]{0,2,1:T(4,128)(4,1)}, u32[]{:S(2)}) copy-start(pred[4,3,4]{0,2,1:T(4,128)(4,1)} %constant.240.clone) | copy-start | bytes 148
  349.6 18.2 %copy-start.4 = (s32[32,1,128]{2,1,0:T(1,128)S(1)}, s32[32,1,128]{2,1,0:T(1,128)}, u32[]{:S(2)}) copy-start(s32[32,1,128]{2,1,0:T(1,128)} %constant_dynamic-slice_fusion.3) | copy-start | bytes 49156
  349.6 79.7 %collective-permute-start.4 = (f32[54,128,128]{2,1,0:T(8,128)}, f32[54,128,128]{2,1,0:T(8,128)}, u32[]{:S(2)}, u32[]{:S(2)}) collective-permute-start(f32[54,128,128]{2,1,0:T(8,128)} %pack_lower.3), channel_id=1, source_target_pairs={{0,16},{4,20},{8,24},{12,28},{16,0},{20,4},{24,8},{28,12},{1,17},{... | collective-permute-start | bytes 10616840 | tf_op jit(solution)/shard_map/ppermute | solution.py:29
  361.5 180.5 %collective-permute-start.2 = (f32[3,15,128,128]{3,2,1,0:T(8,128)}, f32[3,15,128,128]{3,2,1,0:T(8,128)S(1)}, u32[]{:S(2)}, u32[]{:S(2)}) collective-permute-start(f32[3,15,128,128]{3,2,1,0:T(8,128)} %get-tuple-element.28), channel_id=1, source_target_pairs={{0,16},{4,20},{8,24},{12,28},{16,0},{20,4},{24,8},{28,12},{1,17},{... | collective-permute-start | bytes 8847368 | tf_op jit(solution)/shard_map/ppermute | solution.py:29
  429.3 255.7 %collective-permute-start.7 = (f32[3,15,128,128]{3,2,1,0:T(8,128)}, f32[3,15,128,128]{3,2,1,0:T(8,128)}, u32[]{:S(2)}, u32[]{:S(2)}) collective-permute-start(f32[3,15,128,128]{3,2,1,0:T(8,128)} %get-tuple-element.31), channel_id=1, source_target_pairs={{0,16},{4,20},{8,24},{12,28},{16,0},{20,4},{24,8},{28,12},{1,17},{... | collective-permute-start | bytes 8847368 | tf_op jit(solution)/shard_map/ppermute | solution.py:29
  539.9 364.5 %collective-permute-start.6 = (f32[54,128,128]{2,1,0:T(8,128)}, f32[54,128,128]{2,1,0:T(8,128)}, u32[]{:S(2)}, u32[]{:S(2)}) collective-permute-start(f32[54,128,128]{2,1,0:T(8,128)} %collective-permute-done.4.refs_8_.refs_9_.refs_10_.refs_11_), channel_id=1, source_target_pairs={{0,0},{1,4},{2,8},{3,12},{4,1},{5,5},{6,9},{7,13},{8,2},{9,6},{10,... | collective-permute-start | bytes 10616840 | tf_op jit(solution)/shard_map/ppermute | solution.py:666
  542.0 6.7 copy-start.2
  542.0 144.0 %collective-permute-start.8 = (f32[3,15,128,128]{3,2,1,0:T(8,128)}, f32[3,15,128,128]{3,2,1,0:T(8,128)}, u32[]{:S(2)}, u32[]{:S(2)}) collective-permute-start(f32[3,15,128,128]{3,2,1,0:T(8,128)} %get-tuple-element.32), channel_id=1, source_target_pairs={{0,16},{4,20},{8,24},{12,28},{16,0},{20,4},{24,8},{28,12},{1,17},{... | collective-permute-start | bytes 8847368 | tf_op jit(solution)/shard_map/ppermute | solution.py:29
  685.1 325.5 %collective-permute-start.9 = (f32[3,15,128,128]{3,2,1,0:T(8,128)}, f32[3,15,128,128]{3,2,1,0:T(8,128)}, u32[]{:S(2)}, u32[]{:S(2)}) collective-permute-start(f32[3,15,128,128]{3,2,1,0:T(8,128)} %get-tuple-element.33), channel_id=1, source_target_pairs={{0,16},{4,20},{8,24},{12,28},{16,0},{20,4},{24,8},{28,12},{1,17},{... | collective-permute-start | bytes 8847368 | tf_op jit(solution)/shard_map/ppermute | solution.py:29
  686.0 358.5 %collective-permute-start.10 = (f32[3,15,128,128]{3,2,1,0:T(8,128)}, f32[3,15,128,128]{3,2,1,0:T(8,128)}, u32[]{:S(2)}, u32[]{:S(2)}) collective-permute-start(f32[3,15,128,128]{3,2,1,0:T(8,128)} %get-tuple-element.34), channel_id=1, source_target_pairs={{0,16},{4,20},{8,24},{12,28},{16,0},{20,4},{24,8},{28,12},{1,17},{... | collective-permute-start | bytes 8847368 | tf_op jit(solution)/shard_map/ppermute | solution.py:29
  1044.5 33.4 %copy-start.1 = (f32[16384]{0:T(1024)S(1)}, f32[16384]{0:T(1024)}, u32[]{:S(2)}) copy-start(f32[16384]{0:T(1024)} %param.80) | copy-start | bytes 196612
Sparse Core Ops, SparseCore 0:
  70.7 72.2 all-gather.5
  144.6 149.3 all-gather.3
  295.6 221.2 all-gather.7

commit v2 on v1

--- a/solution.py
+++ b/solution.py
@@ -10,6 +10,8 @@
 F32 = jnp.float32
 BF16 = jnp.bfloat16
 SUB = 8
+BATCH = 32
+WEIGHT = 0.01
 VMEM_LIMIT = 56 * 1024 * 1024
 
 
@@ -20,7 +22,9 @@
 
 
 def cost(flops, moved):
-    return pl.CostEstimate(flops=int(flops), bytes_accessed=int(moved), transcendentals=0)
+    return pl.CostEstimate(
+        flops=int(flops * WEIGHT), bytes_accessed=int(moved * WEIGHT), transcendentals=0
+    )
 
 
 def swapped(value, axis, distance):
@@ -61,20 +65,23 @@
 
 def pack_panel(child, half, count):
     _, _, rows, tile, _, lanes = child.shape
+    block = min(4, rows)
 
     def kernel(half_ref, raw, out):
-        for p in range(count):
-            out[0, p] = raw.reshape(tile * SUB, lanes)[pl.ds(p, tile, SUB), :]
+        flat = raw.reshape(block * tile * SUB, lanes)
+        for b in range(block):
+            for p in range(count):
+                out[b, p] = flat[pl.ds(b * tile * SUB + p, tile, SUB), :]
 
     return pl.pallas_call(
         kernel,
         grid_spec=pltpu.PrefetchScalarGridSpec(
             num_scalar_prefetch=1,
-            grid=(rows,),
+            grid=(rows // block,),
             in_specs=[
-                pl.BlockSpec((1, 1, 1, tile, SUB, lanes), lambda j, h: (0, h[0], j, 0, 0, 0))
+                pl.BlockSpec((1, 1, block, tile, SUB, lanes), lambda j, h: (0, h[0], j, 0, 0, 0))
             ],
-            out_specs=pl.BlockSpec((1, count, tile, lanes), lambda j, h: (j, 0, 0, 0)),
+            out_specs=pl.BlockSpec((block, count, tile, lanes), lambda j, h: (j, 0, 0, 0)),
         ),
         out_shape=jax.ShapeDtypeStruct((rows, count, tile, lanes), F32),
         compiler_params=params(),
@@ -168,33 +175,45 @@
     )(half, child)
 
 
-def gathered_row(index, load, columns):
-    row = load(jnp.maximum(index, 0))
-    placed = jnp.take_along_axis(
-        row, jnp.maximum(columns, 0), axis=1, mode="promise_in_bounds"
-    )
-    return jnp.where((columns >= 0) & (index >= 0), placed, 0.0)
+def place_block(rowmap, row, load, columns, store):
+    tile = columns.shape[-1]
+    live = columns >= 0
+    lanes = jnp.maximum(columns, 0)
+
+    def body(step, carry):
+        index = [rowmap[row, step * BATCH + r] for r in range(BATCH)]
+        values = [load(jnp.maximum(i, 0)) for i in index]
+        values = [
+            jnp.take_along_axis(v, lanes, axis=1, mode="promise_in_bounds") for v in values
+        ]
+        store(step * BATCH, [jnp.where(live & (i >= 0), v, 0.0) for i, v in zip(index, values)])
+        return carry
+
+    lax.fori_loop(0, tile // BATCH, body, 0)
 
 
 def place_rows(first, second, maps, diag, where):
     count, tile, cols, lanes = first.shape
     (rows0, cols0), (rows1, cols1) = maps
 
-    def kernel(rows0_ref, rows1_ref, where_ref, u0, u1, c0, c1, d, out):
+    def kernel(rows0_ref, rows1_ref, where_ref, u0, u1, c0, c1, d, out, flat):
         n, g = pl.program_id(0), pl.program_id(1)
-        cols_0, cols_1 = c0[...], c1[...]
-
-        def body(step, carry):
-            for r in range(SUB):
-                o = step * SUB + r
-                value = gathered_row(rows0_ref[n, o], lambda s: u0[0, s], cols_0)
-                value += gathered_row(rows1_ref[n, o], lambda s: u1[0, s], cols_1)
-                for p in range(SUB):
-                    out[0, p, pl.ds(o, 1), :] = value[p : p + 1, :]
-            return carry
-
-        lax.fori_loop(0, tile // SUB, body, 0)
+
+        def put(at, values):
+            for r, value in enumerate(values):
+                flat[pl.ds(pl.multiple_of((at + r) * SUB, SUB), SUB), :] = value
+
+        def add(at, values):
+            spots = [pl.ds(pl.multiple_of((at + r) * SUB, SUB), SUB) for r in range(BATCH)]
+            values = [flat[spot, :] + value for spot, value in zip(spots, values)]
+            for spot, value in zip(spots, values):
+                flat[spot, :] = value
+
+        place_block(rows0_ref, n, lambda s: u0[0, s], c0[...], put)
+        place_block(rows1_ref, n, lambda s: u1[0, s], c1[...], add)
         for p in range(SUB):
+            out[0, p] = flat[pl.ds(p, tile, SUB), :]
+
             @pl.when(where_ref[n] == g * SUB + p)
             def _():
                 eye = lax.broadcasted_iota(jnp.int32, (tile, lanes), 0) == (
@@ -215,6 +234,7 @@
                 pl.BlockSpec((1, 1, lanes), lambda n, g, *_: (n, 0, 0)),
             ],
             out_specs=pl.BlockSpec((1, SUB, tile, lanes), lambda n, g, *_: (n, g, 0, 0)),
+            scratch_shapes=[pltpu.VMEM((tile * SUB, lanes), F32)],
         ),
         out_shape=jax.ShapeDtypeStruct((count, cols, tile, lanes), F32),
         compiler_params=params(2),
@@ -228,16 +248,19 @@
     lane = lax.broadcasted_iota(jnp.int32, (1, tile), 1)
     sub = lax.broadcasted_iota(jnp.int32, (tile, 1), 0)
 
+    def at_lane(value, j):
+        index = jnp.full(value.shape, j, jnp.int32)
+        return jnp.take_along_axis(value, index, axis=1, mode="promise_in_bounds")
+
     def body(j, carry):
         whole = block[...]
-        row = block[pl.ds(j, 1), :]
+        row = jnp.broadcast_to(block[pl.ds(j, 1), :], (SUB, tile))
         here = lane == j
-        pivot = jnp.sum(jnp.where(here, row, 0.0), axis=1, keepdims=True)
+        pivot = at_lane(row, j)
         root = lax.rsqrt(pivot)
         root = root * (1.5 - 0.5 * pivot * root * root)
-        row = jnp.where(here, root, row * root)
-        column = jnp.sum(jnp.where(here, whole, 0.0), axis=1, keepdims=True) * root
-        column = jnp.where(sub > j, column, 0.0)
+        row = jnp.where(here, root, row * root)[:1]
+        column = jnp.where(sub > j, at_lane(whole, j), 0.0) * root[:1]
         kept = jnp.where(here & (sub > j), 0.0, whole)
         block[...] = jnp.where(sub == j, row, kept - column * row)
         return carry
@@ -347,46 +370,49 @@
     )(column_index, gathered, high, low)
 
 
-def solve_columns(rows, high, low, places):
-    blocks, cols, tile, lanes = rows.shape
+def solve_columns(parts, homes, high, low):
+    _, cols, tile, lanes = parts[0].shape
     order = high.shape[0]
     wide = 4
     deep = 256
-
-    def kernel(f, h, l, out_h, out_l):
-        full = jnp.concatenate(
-            [
-                jnp.concatenate([f[places[b], p] for p in range(wide)], axis=1)
-                for b in range(order // tile)
-            ],
-            axis=0,
-        )
-        fh, fl = split(full)
+    width = len(parts)
+
+    def kernel(home, *refs):
+        f, (h, l, out_h, out_l, fh, fl) = refs[:width], refs[width:]
+        number = 0
+        for part in f:
+            for b in range(part.shape[0]):
+                block = jnp.concatenate([part[b, p] for p in range(wide)], axis=1)
+                rows = pl.ds(pl.multiple_of(home[number] * tile, tile), tile)
+                fh[rows, :], fl[rows, :] = split(block)
+                number += 1
         for r in range(order // deep):
             span, depth = slice(r * deep, (r + 1) * deep), (r + 1) * deep
             lh, ll = h[span, :depth], l[span, :depth]
             x = dot(lh, fh[:depth]) + (dot(lh, fl[:depth]) + dot(ll, fh[:depth]))
-            xh, xl = split(x)
-            out_h[span, :] = xh
-            out_l[span, :] = xl
-
-    return pl.pallas_call(
-        kernel,
-        grid=(cols // wide,),
-        in_specs=[
-            pl.BlockSpec((blocks, wide, tile, lanes), lambda g: (0, g, 0, 0)),
-            pl.BlockSpec((order, order), lambda g: (0, 0)),
-            pl.BlockSpec((order, order), lambda g: (0, 0)),
-        ],
-        out_specs=[pl.BlockSpec((order, wide * lanes), lambda g: (0, g))] * 2,
+            out_h[span, :], out_l[span, :] = split(x)
+
+    return pl.pallas_call(
+        kernel,
+        grid_spec=pltpu.PrefetchScalarGridSpec(
+            num_scalar_prefetch=1,
+            grid=(cols // wide,),
+            in_specs=[
+                pl.BlockSpec((part.shape[0], wide, tile, lanes), lambda g, *_: (0, g, 0, 0))
+                for part in parts
+            ]
+            + [pl.BlockSpec((order, order), lambda g, *_: (0, 0))] * 2,
+            out_specs=[pl.BlockSpec((order, wide * lanes), lambda g, *_: (0, g))] * 2,
+            scratch_shapes=[pltpu.VMEM((order, wide * lanes), BF16)] * 2,
+        ),
         out_shape=[jax.ShapeDtypeStruct((order, cols * lanes), BF16)] * 2,
         compiler_params=params(),
         cost_estimate=cost(4 * order * order * cols * lanes, order * cols * lanes * 8),
         name="solve_columns",
-    )(rows, high, low)
-
-
-def own_part(child, half, own_maps, diag, where, left, right, panel):
+    )(homes, *parts, high, low)
+
+
+def own_part(before, child, half, own_maps, diag, where, left, right, panel, start, end):
     _, _, rows, tile, cols, lanes = child.shape
     rowmap, colmap = own_maps
     xh, xl = left
@@ -395,22 +421,19 @@
     count = panel.shape[0]
     block = min(4, rows)
 
-    def kernel(half_ref, map_ref, where_ref, u, c, d, lh, ll, rh, rl, pan, out, flat):
-        g, n = pl.program_id(0), pl.program_id(1)
+    def kernel(half_ref, map_ref, where_ref, *refs):
+        u, c, d, lh, ll, rh, rl, pan, out, flat = refs[-10:]
+        g, n = pl.program_id(0) + start, pl.program_id(1)
         columns = c[...]
         for b in range(block):
             j = n * block + b
 
-            def body(step, carry):
-                for r in range(SUB):
-                    o = step * SUB + r
-                    at = pl.multiple_of((b * tile + o) * SUB, SUB)
-                    flat[pl.ds(at, SUB), :] = gathered_row(
-                        map_ref[j, o], lambda s: u[0, 0, b, s], columns
-                    )
-                return carry
-
-            lax.fori_loop(0, tile // SUB, body, 0)
+            def put(at, values):
+                for r, value in enumerate(values):
+                    spot = pl.multiple_of((b * tile + at + r) * SUB, SUB)
+                    flat[pl.ds(spot, SUB), :] = value
+
+            place_block(map_ref, j, lambda s: u[0, 0, b, s], columns, put)
             for p in range(SUB):
                 @pl.when(where_ref[j] == g * SUB + p)
                 def _():
@@ -438,49 +461,48 @@
 
         out[...] = flat[...].reshape(out.shape)
 
+    held = [] if before is None else [pl.BlockSpec(memory_space=pl.ANY)]
     return pl.pallas_call(
         kernel,
         grid_spec=pltpu.PrefetchScalarGridSpec(
             num_scalar_prefetch=3,
-            grid=(cols // SUB, rows // block),
-            in_specs=[
+            grid=(end - start, rows // block),
+            in_specs=held
+            + [
                 pl.BlockSpec(
-                    (1, 1, block, tile, SUB, lanes), lambda g, n, h, *_: (0, h[0], n, 0, g, 0)
+                    (1, 1, block, tile, SUB, lanes), lambda g, n, h, *_: (0, h[0], n, 0, g + start, 0)
                 ),
-                pl.BlockSpec((SUB, lanes), lambda g, n, *_: (g, 0)),
+                pl.BlockSpec((SUB, lanes), lambda g, n, *_: (g + start, 0)),
                 pl.BlockSpec((block, 1, lanes), lambda g, n, *_: (n, 0, 0)),
                 pl.BlockSpec((block * tile, order), lambda g, n, *_: (n, 0)),
                 pl.BlockSpec((block * tile, order), lambda g, n, *_: (n, 0)),
-                pl.BlockSpec((order, SUB * lanes), lambda g, n, *_: (0, g)),
-                pl.BlockSpec((order, SUB * lanes), lambda g, n, *_: (0, g)),
+                pl.BlockSpec((order, SUB * lanes), lambda g, n, *_: (0, g + start)),
+                pl.BlockSpec((order, SUB * lanes), lambda g, n, *_: (0, g + start)),
                 pl.BlockSpec((count, block * tile, lanes), lambda g, n, *_: (0, n, 0)),
             ],
-            out_specs=pl.BlockSpec((1, block, tile, SUB, lanes), lambda g, n, *_: (0, n, 0, g, 0)),
+            out_specs=pl.BlockSpec((1, block, tile, SUB, lanes), lambda g, n, *_: (0, n, 0, g + start, 0)),
             scratch_shapes=[pltpu.VMEM((block * tile * SUB, lanes), F32)],
         ),
         out_shape=jax.ShapeDtypeStruct((1, rows, tile, cols, lanes), F32),
+        input_output_aliases={} if before is None else {3: 0},
         compiler_params=params(2),
         cost_estimate=cost(
             6 * rows * tile * order * cols * lanes, rows * tile * cols * lanes * 8
         ),
         name="own_part",
-    )(half, rowmap, where, child, colmap, diag[:, None, :], xh, xl, ch, cl, panel)
+    )(half, rowmap, where, *([] if before is None else [before]), child, colmap, diag[:, None, :], xh, xl, ch, cl, panel)
 
 
 def add_first(front, block, rowmap, colmap):
     _, _, tile, cols, lanes = front.shape
 
     def kernel(map_ref, before, u, c, out):
-        columns = c[...]
-
-        def body(step, carry):
-            for r in range(SUB):
-                o = step * SUB + r
-                value = gathered_row(map_ref[0, o], lambda s: u[0, s], columns)
-                out[0, 0, o] = before[0, 0, o] + value
-            return carry
-
-        lax.fori_loop(0, tile // SUB, body, 0)
+        def add(at, values):
+            values = [before[0, 0, at + r] + value for r, value in enumerate(values)]
+            for r, value in enumerate(values):
+                out[0, 0, at + r] = value
+
+        place_block(map_ref, 0, lambda s: u[0, s], c[...], add)
 
     spec = pl.BlockSpec((1, 1, tile, SUB, lanes), lambda g, *_: (0, 0, 0, g, 0))
     return pl.pallas_call(
@@ -507,7 +529,7 @@
     _, _, tile, cols, lanes = front.shape
     width = len(sources)
     groups = cols // SUB
-    picks, stands = picks.reshape(-1), stands.reshape(-1)
+    picks, stands = (t.astype(jnp.int32).reshape(-1) for t in (picks, stands))
 
     def entry(slot, n, g):
         return (slot * count + n) * groups + g
@@ -515,7 +537,6 @@
     def kernel(map_ref, picks_ref, stands_ref, before, *refs):
         tiles, (c, out, flat) = refs[:width], refs[width:]
         n, g = pl.program_id(0), pl.program_id(1)
-        columns = c[...]
         for slot in range(width):
             stand = stands_ref[entry(slot, n, g)]
             p = stand // 2
@@ -528,18 +549,15 @@
             def _():
                 flat[pl.ds(p, tile, SUB), :] = tiles[slot][0].T
 
-        def body(step, carry):
-            for r in range(SUB):
-                o = step * SUB + r
-                value = gathered_row(
-                    map_ref[n + first, o],
-                    lambda s: flat[pl.ds(pl.multiple_of(s * SUB, SUB), SUB), :],
-                    columns,
-                )
-                out[0, 0, o] = before[0, 0, o] + value
-            return carry
-
-        lax.fori_loop(0, tile // SUB, body, 0)
+        def load(source):
+            return flat[pl.ds(pl.multiple_of(source * SUB, SUB), SUB), :]
+
+        def add(at, values):
+            values = [before[0, 0, at + r] + value for r, value in enumerate(values)]
+            for r, value in enumerate(values):
+                out[0, 0, at + r] = value
+
+        place_block(map_ref, n + first, load, c[...], add)
 
     spec = pl.BlockSpec((1, 1, tile, SUB, lanes), lambda n, g, *_: (0, n + first, 0, g, 0))
 
@@ -569,22 +587,36 @@
     return row * (row - 1) // 2
 
 
-def lower_tables(exchanged, first, last, rows, parity, start, count):
+def held_picks(picks, given):
+    flat, mask = picks.reshape(picks.shape[0], -1).copy(), given.reshape(picks.shape[0], -1)
+    for step in range(1, flat.shape[1]):
+        flat[:, step] = np.where(mask[:, step], flat[:, step], flat[:, step - 1])
+    return flat.reshape(picks.shape).astype(np.int32)
+
+
+def lower_tables(exchanged, first, last, rows, parity, alone, start, count):
     groups = rows // (SUB // 2)
     slot, n, g = np.meshgrid(
         np.arange(SUB // 2), np.arange(start, start + count), np.arange(groups), indexing="ij"
     )
     i = g * (SUB // 2) + slot
-    row, col = (i, n) if exchanged else (n, i)
-    mine = (row >= first) & (row < last) & (col >= 1)
-    mine &= (col < row) if exchanged else (col <= row)
-    picks = np.where(mine, triangle(row) - triangle(first) + col - 1, 0)
-    flat = mine.reshape(SUB // 2, -1)
-    held = picks.reshape(SUB // 2, -1).copy()
-    for step in range(1, held.shape[1]):
-        held[:, step] = np.where(flat[:, step], held[:, step], held[:, step - 1])
-    stands = jnp.where(mine, 2 * (2 * slot + parity) + int(exchanged), -1)
-    return held.reshape(mine.shape).astype(np.int32), stands.astype(jnp.int32)
+    place = 2 * (2 * slot + parity)
+
+    def inside(row, col):
+        return (row >= first) & (row < last) & (col >= 1), triangle(row) - triangle(first) + col - 1
+
+    straight, at = inside(n, i)
+    straight &= i <= n
+    mirror, at_mirror = inside(i, n)
+    mirror &= n < i
+    if exchanged:
+        picks = held_picks(np.where(mirror, at_mirror, 0), mirror)
+        return jnp.where(alone, 0, picks), jnp.where(mirror & ~alone, place + 1, -1)
+    mine = held_picks(np.where(straight, at, 0), straight)
+    both = straight | mirror
+    all_of_it = held_picks(np.where(straight, at, np.where(mirror, at_mirror, 0)), both)
+    stands = jnp.where(straight, place, jnp.where(mirror & alone, place + 1, -1))
+    return jnp.where(alone, all_of_it, mine), stands
 
 
 def cross_tables(rows, parity, start, count):
@@ -595,7 +627,7 @@
     i = g * (SUB // 2) + slot
     picks = np.where(i >= 1, n * (rows - 1) + i - 1, n * (rows - 1))
     stands = jnp.where(i >= 1, 2 * (2 * slot + parity), -1)
-    return picks.astype(np.int32), stands.astype(jnp.int32)
+    return jnp.asarray(picks, jnp.int32), stands
 
 
 def on_device(child_update, child_map, parent_diag):
@@ -649,37 +681,24 @@
 
     diag_rows = diag_tiles[blocks]
 
+    subcubes = ("cube", "row")
+    spans, at = [], 1
+    while at < rows:
+        count = -(-3 * (rows - at) // 10)
+        spans.append((at, count))
+        at += count
+
     panel_sent = pack_panel(child_update, other, local)
-    panel_came = swapped(panel_sent, ("cube", "row"), distance)
+    panel_own = pack_panel(after(child_update, panel_sent), own, local)
+    panel_came = swapped(panel_sent, subcubes, distance)
     if mirrored:
         near = 1 + (rows * 11) // 16
         cuts = [(1, near), (near, rows)]
         lower_sent = [pack_lower(child_update, other, other, a, b) for a, b in cuts]
         pivot_sent = child_update[0, :, 0]
-        pairs = [
-            (r * columns + c, c * columns + r) for r in range(half_grid) for c in range(columns)
-        ]
-        lower_a = swapped(lower_sent[0], ("cube", "row"), distance)
-        pivot_came = swapped(after(pivot_sent, panel_came), ("cube", "row"), distance)
-        turned_a = lax.ppermute(lower_a, ("row", "col"), pairs)
-        lower_b = swapped(after(lower_sent[1], lower_a), ("cube", "row"), distance)
-        turned_b = lax.ppermute(after(lower_b, turned_a), ("row", "col"), pairs)
-        sent = pack_cross(child_update, other, own)
-        chain = [pivot_came, lower_b]
+        panel_came = after(panel_came, panel_own, pivot_sent, lower_sent[0])
     else:
         pivot_sent = lax.dynamic_slice_in_dim(child_update[0, :, 0], 1 - sibling, 1, 0)
-        pivot_came = swapped(after(pivot_sent, panel_came), ("cube", "row"), distance)
-        sent = pack_all(child_update, other)
-        chain = [panel_came, pivot_came]
-    per = -(-(rows - 1) // 5)
-    spans = [(at, min(per, rows - at)) for at in range(1, rows, per)]
-    came = []
-    for at, count in spans:
-        part = after(sent[at - 1 : at - 1 + count], chain[-2])
-        came.append(swapped(part, ("cube", "row"), distance))
-        chain.append(came[-1])
-
-    panel_own = pack_panel(child_update, own, local)
 
     def placed(tiles, row_map, col_map):
         offsets = jnp.arange(tile, dtype=jnp.int32)
@@ -695,18 +714,24 @@
     front_panel += jnp.where(eye, diag_rows[:, :, None, None], 0.0)
 
     pivot = lax.all_gather(front_panel[0], ("cube", "row", "col"), axis=0, tiled=False)
+    gathered = lax.all_gather(
+        front_panel.reshape(rows * tile, local * tile), "col", axis=0, tiled=False
+    )
     pivot = pivot.reshape(grid_size, columns, tile, local, tile)[:pivots]
     pivot = jnp.transpose(pivot, (0, 2, 3, 1, 4)).reshape(K, K)
-    high, low = inverse_factor(pivot, tile)
-
-    gathered = lax.all_gather(
-        front_panel.reshape(rows * tile, local * tile), "col", axis=0, tiled=False
-    )
-    left_h, left_l, panel = solve_rows(
-        gathered, high, low, column_index.astype(jnp.int32)[None]
-    )
-
+
+    pivot_came = swapped(after(pivot_sent, panel_came), subcubes, distance)
     if mirrored:
+        pairs = [
+            (r * columns + c, c * columns + r)
+            for r in range(half_grid)
+            for c in range(columns)
+            if r != c
+        ]
+        lower_a = swapped(after(lower_sent[0], front_panel), subcubes, distance)
+        sent = pack_cross(after(child_update, front_panel), other, own)
+        pivot_came = after(pivot_came, sent, lower_sent[1])
+        lower_b = swapped(after(lower_sent[1], pivot_came), subcubes, distance)
         block_rows = half_grid * jnp.arange(2, dtype=jnp.int32) + within
         pivot_rows = place_rows(
             pivot_sent,
@@ -715,10 +740,34 @@
             diag_tiles[block_rows],
             on_diagonal(block_rows),
         )
-        pivot_rows = lax.all_gather(pivot_rows, "row", axis=0, tiled=True)
-        places = [2 * (b % half_grid) + b // half_grid for b in range(pivots)]
+        across = swapped(pivot_rows, "row", 1)
+        pivot = after(pivot, pivot_rows)
+    else:
+        sent = pack_all(child_update, other)
+    high, low = inverse_factor(pivot, tile)
+
+    came = []
+
+    def send(number, behind):
+        at, count = spans[number]
+        part = after(sent[at - 1 : at - 1 + count], behind)
+        came.append(swapped(part, subcubes, distance))
+
+    if mirrored:
+        lower_a = after(lower_a, high)
+        turned_a = lax.ppermute(lower_a, ("row", "col"), pairs)
+        send(0, lower_a)
+        gathered = after(gathered, lower_a)
+    left_h, left_l, panel = solve_rows(gathered, high, low, column_index.astype(jnp.int32)[None])
+    if mirrored:
+        across = after(across, left_h)
+        beside = swapped(jnp.concatenate([pivot_rows, across]), "row", 0)
+        parts = [pivot_rows, across, beside]
+        homes = [block_rows ^ bits for bits in (0, 2, 1, 3)]
         first = lax.dynamic_slice_in_dim(pivot_came, sibling, 1, 0)
     else:
+        for number in range(len(spans)):
+            send(number, came[-2] if number > 1 else pivot_came)
         pivot_rows = place_rows(
             lax.dynamic_slice_in_dim(child_update[0, :, 0], sibling, 1, 0),
             pivot_came,
@@ -727,39 +776,53 @@
             on_diagonal(blocks[:1]),
         )
         mine = (jnp.arange(pivots) == position)[:, None, None, None]
-        pivot_rows = lax.psum(jnp.where(mine, pivot_rows, 0.0), ("cube", "row"))
-        places = list(range(pivots))
+        parts = [lax.psum(jnp.where(mine, pivot_rows, 0.0), subcubes)]
+        homes = [jnp.arange(pivots, dtype=jnp.int32)]
         first = pivot_came
-    right_h, right_l = solve_columns(pivot_rows, high, low, places)
-
-    front = own_part(
-        child_update,
-        own,
-        (own_rows, own_cols),
-        diag_rows,
-        on_diagonal(blocks),
-        (left_h, left_l),
-        (right_h, right_l),
-        panel,
-    )
+    right_h, right_l = solve_columns(parts, jnp.concatenate(homes), high, low)
+    if mirrored:
+        lower_b = after(lower_b, right_h)
+        turned_b = lax.ppermute(lower_b, ("row", "col"), pairs)
+        send(1, lower_b)
+        right_h = after(right_h, lower_b)
+
+    front = None
+    groups = cols // SUB
+    for start, end in ((0, groups // 2), (groups // 2, groups)):
+        front = own_part(
+            front,
+            child_update,
+            own,
+            (own_rows, own_cols),
+            diag_rows,
+            on_diagonal(blocks),
+            (left_h, left_l),
+            (right_h, right_l),
+            panel,
+            start,
+            end,
+        )
+        if mirrored:
+            send(len(came), front)
     front = add_first(front, first, other_rows[:1], trailing_cols)
+    if mirrored:
+        turned_a = after(turned_a, front)
+        for number in range(len(came), len(spans)):
+            came[number - 4] = after(came[number - 4], front)
+            send(number, came[number - 4])
     for (at, count), array in zip(spans, came):
         flat = array.reshape(-1, tile, tile)
         if mirrored:
             half = SUB // 2
-            picks, stands = [], []
-            arrays = []
+            alone = within == column_index
             tables = [(flat, cross_tables(rows, 1 - sibling, at, count))]
             for exchanged, group in ((False, (lower_a, lower_b)), (True, (turned_a, turned_b))):
                 for (a, b), source in zip(cuts, group):
-                    tables.append(
-                        (source, lower_tables(exchanged, a, b, rows, sibling, at, count))
-                    )
-            for source, (pick, stand) in tables:
-                arrays += [source] * half
-                picks.append(pick)
-                stands.append(stand)
-            picks, stands = jnp.concatenate(picks), jnp.concatenate(stands)
+                    table = lower_tables(exchanged, a, b, rows, sibling, alone, at, count)
+                    tables.append((source, table))
+            arrays = [source for source, _ in tables for _ in range(half)]
+            picks = jnp.concatenate([pick for _, (pick, _) in tables])
+            stands = jnp.concatenate([stand for _, (_, stand) in tables])
         else:
             arrays = [flat] * SUB
             shape = (SUB, count, cols // SUB)

time: 1100 us -> 850 us (0.77)
  waiting for transfers between devices: 386 us -> 190 us
  Pallas kernels: 609 us -> 498 us
  local copies, waits for them, and re-layouts: 45.7 us -> 84.1 us
  other arithmetic: 5.84 us -> 22.9 us
    ppermute x9 -> x12, waiting for transfers between devices: 276 us -> 130 us  [swapped(): return lax.ppermute(value, axis, pairs)]
    ppermute x1, waiting for transfers between devices: 110 us -> 27.5 us  [on_device(): turned_a = lax.ppermute(lower_a, ('row', 'col'), pairs)]
    pallas_call x5 -> x6, Pallas kernels: 173 us -> 128 us  [add_tiles(): pl.pallas_call(kernel, grid_spec=pltpu.PrefetchScalarGridSpec(num_scalar_...]
    pallas_call x1 -> x2, Pallas kernels: 168 us -> 124 us  [own_part(): pl.pallas_call(kernel, grid_spec=pltpu.PrefetchScalarGridSpec(num_scalar_...]
    ppermute x1, waiting for transfers between devices: 0.01 us -> 33.1 us  [on_device(): turned_b = lax.ppermute(lower_b, ('row', 'col'), pairs)]
    concatenate x10 -> x22, local copies, waits for them, and re-layouts: 1.09 us -> 22.1 us  [the longest x12 12.4 us: on_device(): stands = jnp.concatenate([stand for _, (_, stand) in tables])]
  transfers between devices with their start and end apart: 14 -> 16, of which waited for: 5 -> 6; matrix products, arithmetic and copies ran while one was open for 5% -> 12% of each run, Pallas kernels for 52% -> 58%
where the time goes in v2:
time: 850 us; the launch traced here: 838 us
  Pallas kernels  498 us (59%)
  waiting for transfers between devices  190 us (22%)
  local copies, waits for them, and re-layouts  84.1 us (10%)
  other arithmetic  22.9 us (3%)
  starting transfers between devices  19.5 us (2%)
  between operations  14.3 us (2%)
  matrix products  8.8 us (1%)
    ppermute x12, waiting for transfers between devices, swapped(): return lax.ppermute(value, axis, pairs)  130 us
    pallas_call x6, Pallas kernels, add_tiles(): pl.pallas_call(kernel, grid_spec=pltpu.PrefetchScalarGridSpec(num_scalar_...  128 us
    pallas_call x2, Pallas kernels, own_part(): pl.pallas_call(kernel, grid_spec=pltpu.PrefetchScalarGridSpec(num_scalar_...  124 us
    pallas_call x1, Pallas kernels, inverse_factor(): pl.pallas_call(kernel, in_specs=[pl.BlockSpec(memory_space=pltpu.VMEM)],...  121 us
    ppermute x1, waiting for transfers between devices, on_device(): turned_b = lax.ppermute(lower_b, ('row', 'col'), pairs)  33.1 us
    ppermute x1, waiting for transfers between devices, on_device(): turned_a = lax.ppermute(lower_a, ('row', 'col'), pairs)  27.5 us
    pallas_call x1, Pallas kernels, solve_columns(): pl.pallas_call(kernel, grid_spec=pltpu.PrefetchScalarGridSpec(num_scalar_...  26 us
    pallas_call x1, Pallas kernels, pack_cross(): pl.pallas_call(kernel, grid_spec=pltpu.PrefetchScalarGridSpec(num_scalar_...  25.1 us
  transfers between devices with their start and end apart: 16, of which 6 were waited for; matrix products, arithmetic and copies ran while one was open for 12% of the time, Pallas kernels for 58%

profile of v2, /device:TPU:6, one launch (start us, length us, event | category | flops | bytes accessed | tf_op | source)
XLA Modules:
  0.0 838.3 jit_solution(3497594091299639630)
XLA Ops:
  6.5 5.3 pack_panel.2
  12.4 15.0 %pack_lower.2 = f32[66,128,128]{2,1,0:T(8,128)} custom-call(s32[1]{0:T(128)S(6)} %sub.93.half_ref.parity_ref, s32[1]{0:T(128)S(6)} %sub.93.half_ref.parity_ref, f32[1,2,16,128,32,128]{5,4,3,2,1,0:T(8,128)} %refs_1_.1), custom_call_target="tpu_custom_call" | custom-call | bytes 273940 | tf_op jit(solution)/shard_map/pack_lower/pallas_call | solution.py:135
  27.6 5.3 pack_panel.3
  33.0 4.4 select_reduce_fusion
  38.2 3.6 fusion.6
  41.8 4.6 slice_bitcast_fusion.u0
  46.5 13.0 %collective-permute-done = f32[16,2,128,128]{3,2,1,0:T(8,128)S(1)} collective-permute-done((f32[16,2,128,128]{3,2,1,0:T(8,128)}, f32[16,2,128,128]{3,2,1,0:T(8,128)S(1)}, u32[]{:S(2)}, u32[]{:S(2)}) %collective-permute-start) | collective-permute-done | bytes 2097184 | tf_op jit(solution)/shard_map/ppermute | solution.py:33
  59.4 2.2 fusion.2
  63.0 1.7 bitcast_add_fusion
  65.6 2.3 copy.203
  67.9 3.9 reshape.304
  74.2 1.5 collective-permute-start.1
  76.2 8.1 pack_lower.3
  86.0 25.1 %pack_cross.1 = f32[15,15,128,128]{3,2,1,0:T(8,128)} custom-call(s32[1]{0:T(128)S(6)} %sub.93.half_ref.parity_ref, s32[1]{0:T(128)} %bitcast.7.half_ref.parity_ref, f32[1,2,16,128,32,128]{5,4,3,2,1,0:T(8,128)} %refs_1_.1), custom_call_target="tpu_custom_call" | custom-call | bytes 503316 | tf_op jit(solution)/shard_map/pack_cross/pallas_call | solution.py:102
  111.2 66.6 %collective-permute-done.2.u1 = f32[2,128,32,128]{3,2,1,0:T(8,128)} collective-permute-done((f32[2,128,32,128]{3,2,1,0:T(8,128)}, f32[2,128,32,128]{3,2,1,0:T(8,128)}, u32[]{:S(2)}, u32[]{:S(2)}) %collective-permute-start.2) | collective-permute-done | bytes 4194336 | tf_op jit(solution)/shard_map/ppermute | solution.py:33
  177.8 15.5 %place_rows.1.refs_0_ = f32[2,32,128,128]{3,2,1,0:T(8,128)} custom-call(s32[2,128]{1,0:T(2,128)} %bitcast.116, s32[2,128]{1,0:T(2,128)} %bitcast.117, s32[2]{0:T(128)} %compare_select_fusion.2.where_ref, f32[2,128,32,128]{3,2,1,0:T(8,128)} %slice_bitcast_fusion.u0, f32[2,128,32,128]{3,2,1,0:T(8,128)} %collective-permute-done.2.u1, s32[32,128]{1,0:T(8,128)} %bitcast.95, ...), custom_call_target="tpu_custom_call" | custom-call | bytes 125829 | tf_op jit(solution)/shard_map/place_rows/pallas_call | solution.py:224
  193.9 5.3 copy.192
  199.1 5.5 reshape.277.a
  204.7 121.5 %inverse_factor.1 = (bf16[1024,1024]{1,0:T(8,128)(2,1)}, bf16[1024,1024]{1,0:T(8,128)(2,1)}) custom-call(f32[1024,1024]{1,0:T(8,128)} %reshape.277.a), custom_call_target="tpu_custom_call" | custom-call | flops 1000000000 | bytes 83886 | tf_op jit(solution)/shard_map/inverse_factor/pallas_call | solution.py:308
  326.2 19.1 %solve_rows.1 = (bf16[2048,1024]{1,0:T(8,128)(2,1)}, bf16[2048,1024]{1,0:T(8,128)(2,1)}, f32[2,2048,128]{2,1,0:T(8,128)}) custom-call(s32[1]{0:T(128)} %bitcast.15.me, f32[4,2048,256]{2,1,0:T(8,128)} %all-gather.3.cloned.1.call-done.f, bf16[1024,1024]{1,0:T(8,128)(2,1)} %get-tuple-element.41.h.refs_3_, bf16[1024,1024]{1,0:T(8,128)(2,1)} %get-tuple-element.44.l.refs_4_), custom_call_target="tpu_custom_call" | custom-call | flops 128849016 | bytes 167772 | tf_op jit(solution)/shard_map/solve_rows/pallas_call | solution.py:345
  345.3 6.7 pad_maximum_fusion
  352.2 5.2 slice.73
  357.4 1.8 collective-permute-start.6
  359.2 5.4 collective-permute-start.7
  365.2 6.0 fusion.56
  371.2 26.0 %solve_columns.1 = (bf16[1024,4096]{1,0:T(8,128)(2,1)}, bf16[1024,4096]{1,0:T(8,128)(2,1)}) custom-call(s32[8]{0:T(128)} %pad_add_fusion.home, f32[2,32,128,128]{3,2,1,0:T(8,128)} %place_rows.1.refs_0_, f32[2,32,128,128]{3,2,1,0:T(8,128)} %collective-permute-done.3.refs_1_, f32[4,32,128,128]{3,2,1,0:T(8,128)} %collective-permute-done.4.refs_2_, ...), custom_call_target="tpu_custom_call" | custom-call | flops 171798688 | bytes 335544 | tf_op jit(solution)/shard_map/solve_columns/pallas_call | solution.py:395
  397.2 34.3 %collective-permute-done.5.refs_8_.refs_9_.refs_10_.refs_11_ = f32[54,128,128]{2,1,0:T(8,128)S(1)} collective-permute-done((f32[54,128,128]{2,1,0:T(8,128)}, f32[54,128,128]{2,1,0:T(8,128)S(1)}, u32[]{:S(2)}, u32[]{:S(2)}) %collective-permute-start.5) | collective-permute-done | bytes 3538976 | tf_op jit(solution)/shard_map/ppermute | solution.py:33
  431.8 5.7 collective-permute-start.8
  438.9 62.1 %own_part.2.refs_0_ = f32[1,16,128,32,128]{4,3,2,1,0:T(8,128)} custom-call(s32[1]{0:T(128)} %bitcast.7.half_ref.parity_ref, s32[16,128]{1,0:T(8,128)} %bitcast.103, s32[16]{0:T(128)} %copy-done.19, f32[1,2,16,128,32,128]{5,4,3,2,1,0:T(8,128)} %refs_1_.1, s32[32,128]{1,0:T(8,128)} %bitcast.96, f32[16,1,128]{2,1,0:T(1,128)} %bitcast.100, ...), custom_call_target="tpu_custom_call" | custom-call | flops 515396064 | bytes 671088 | tf_op jit(solution)/shard_map/own_part/pallas_call | solution.py:465
  501.0 1.5 collective-permute-start.10
  505.0 3.1 slice.76
  508.1 61.6 %own_part.3.before = f32[1,16,128,32,128]{4,3,2,1,0:T(8,128)} custom-call(s32[1]{0:T(128)} %bitcast.7.half_ref.parity_ref, s32[16,128]{1,0:T(8,128)} %bitcast.104, s32[16]{0:T(128)} %copy-done.19, f32[1,16,128,32,128]{4,3,2,1,0:T(8,128)} %own_part.2.refs_0_, f32[1,2,16,128,32,128]{5,4,3,2,1,0:T(8,128)} %refs_1_.1, ...), custom_call_target="tpu_custom_call", output_to_operand_aliasing={{}: (3, {})} | custom-call | flops 515396064 | bytes 671088 | tf_op jit(solution)/shard_map/own_part/pallas_call | solution.py:465
  572.2 3.0 fusion.55
  575.2 3.1 constant_dynamic-slice_fusion.7.u
  578.4 5.9 add_first.1.before
  584.3 15.8 %collective-permute-done.9 = f32[3,15,128,128]{3,2,1,0:T(8,128)} collective-permute-done((f32[3,15,128,128]{3,2,1,0:T(8,128)}, f32[3,15,128,128]{3,2,1,0:T(8,128)}, u32[]{:S(2)}, u32[]{:S(2)}) %collective-permute-start.9) | collective-permute-done | bytes 2949152 | tf_op jit(solution)/shard_map/ppermute | solution.py:33
  600.4 27.5 %collective-permute-done.7.refs_12_.refs_13_.refs_14_.refs_15_ = f32[66,128,128]{2,1,0:T(8,128)} collective-permute-done((f32[66,128,128]{2,1,0:T(8,128)}, f32[66,128,128]{2,1,0:T(8,128)}, u32[]{:S(2)}, u32[]{:S(2)}) %collective-permute-start.7) | collective-permute-done | bytes 4325408 | tf_op jit(solution)/shard_map/ppermute | solution.py:758
  651.4 1.5 reshape.269.stands_ref
  657.0 1.5 reshape.268.picks_ref
  662.8 1.6 reshape.271.stands_ref
  668.6 1.6 reshape.270.picks_ref
  670.2 33.1 %collective-permute-done.8.refs_16_.refs_17_.refs_18_.refs_19_ = f32[54,128,128]{2,1,0:T(8,128)} collective-permute-done((f32[54,128,128]{2,1,0:T(8,128)S(1)}, f32[54,128,128]{2,1,0:T(8,128)}, u32[]{:S(2)}, u32[]{:S(2)}) %collective-permute-start.8) | collective-permute-done | bytes 3538976 | tf_op jit(solution)/shard_map/ppermute | solution.py:785
  703.3 41.6 %add_tiles.6.before = f32[1,16,128,32,128]{4,3,2,1,0:T(8,128)} custom-call(s32[16,128]{1,0:T(8,128)} %bitcast.87, s32[400]{0:T(512)} %reshape.270.picks_ref, s32[400]{0:T(512)} %reshape.271.stands_ref, f32[1,16,128,32,128]{4,3,2,1,0:T(8,128)} %add_first.1.before, ...), custom_call_target="tpu_custom_call", output_to_operand_aliasing={{}: (3, {})} | custom-call | bytes 314572 | tf_op jit(solution)/shard_map/add_tiles/pallas_call | solution.py:567
  744.9 25.1 %add_tiles.7.before = f32[1,16,128,32,128]{4,3,2,1,0:T(8,128)} custom-call(s32[16,128]{1,0:T(8,128)} %bitcast.88, s32[240]{0:T(256)} %reshape.268.picks_ref, s32[240]{0:T(256)} %reshape.269.stands_ref, f32[1,16,128,32,128]{4,3,2,1,0:T(8,128)} %add_tiles.6.before, ...), custom_call_target="tpu_custom_call", output_to_operand_aliasing={{}: (3, {})} | custom-call | bytes 188743 | tf_op jit(solution)/shard_map/add_tiles/pallas_call | solution.py:567
  770.1 24.5 %add_tiles.8.before = f32[1,16,128,32,128]{4,3,2,1,0:T(8,128)} custom-call(s32[16,128]{1,0:T(8,128)} %bitcast.89, s32[240]{0:T(256)} %reshape.266.picks_ref, s32[240]{0:T(256)} %reshape.267.stands_ref, f32[1,16,128,32,128]{4,3,2,1,0:T(8,128)} %add_tiles.7.before, ...), custom_call_target="tpu_custom_call", output_to_operand_aliasing={{}: (3, {})} | custom-call | bytes 188743 | tf_op jit(solution)/shard_map/add_tiles/pallas_call | solution.py:567
  794.6 16.9 %add_tiles.9.before = f32[1,16,128,32,128]{4,3,2,1,0:T(8,128)} custom-call(s32[16,128]{1,0:T(8,128)} %bitcast.90, s32[160]{0:T(256)} %reshape.264.picks_ref, s32[160]{0:T(256)} %reshape.265.stands_ref, f32[1,16,128,32,128]{4,3,2,1,0:T(8,128)} %add_tiles.8.before, ...), custom_call_target="tpu_custom_call", output_to_operand_aliasing={{}: (3, {})} | custom-call | bytes 125829 | tf_op jit(solution)/shard_map/add_tiles/pallas_call | solution.py:567
  811.5 9.8 %add_tiles.10.before = f32[1,16,128,32,128]{4,3,2,1,0:T(8,128)} custom-call(s32[16,128]{1,0:T(8,128)} %bitcast.91, s32[80]{0:T(128)} %reshape.262.picks_ref, s32[80]{0:T(128)} %reshape.263.stands_ref, f32[1,16,128,32,128]{4,3,2,1,0:T(8,128)} %add_tiles.9.before, ...), custom_call_target="tpu_custom_call", output_to_operand_aliasing={{}: (3, {})} | custom-call | bytes 62914 | tf_op jit(solution)/shard_map/add_tiles/pallas_call | solution.py:567
  821.3 9.8 %add_tiles.11 = f32[1,16,128,32,128]{4,3,2,1,0:T(8,128)} custom-call(s32[16,128]{1,0:T(8,128)} %bitcast.92, s32[80]{0:T(128)} %constant.336.picks_ref, s32[80]{0:T(128)} %reshape.261.stands_ref, f32[1,16,128,32,128]{4,3,2,1,0:T(8,128)} %add_tiles.10.before, f32[15,128,128]{2,1,0:T(8,128)} %bitcast.41.refs_0_.refs_1_.refs_2_.refs_3_, ...), custom_call_target="tpu_custom_call", output_to_operand_aliasing={{}: (3, {})} | custom-call | bytes 62914 | tf_op jit(solution)/shard_map/add_tiles/pallas_call | solution.py:567
  (152 shorter events, 52.7 us)
Async XLA Ops:
  6.5 30.8 %copy-start = (f32[16384]{0:T(1024)S(1)}, f32[16384]{0:T(1024)}, u32[]{:S(2)}) copy-start(f32[16384]{0:T(1024)} %param.119) | copy-start | bytes 196612
  6.5 187.3 %all-gather.5.cloned.1.call-start = ((), (), s32[]{:S(2)}) async-start(), calls=%async_computation.1 | async-start | bytes 4325376 | tf_op jit(solution)/shard_map/all_gather | solution.py:716
  11.9 47.6 %collective-permute-start = (f32[16,2,128,128]{3,2,1,0:T(8,128)}, f32[16,2,128,128]{3,2,1,0:T(8,128)S(1)}, u32[]{:S(2)}, u32[]{:S(2)}) collective-permute-start(f32[16,2,128,128]{3,2,1,0:T(8,128)} %pack_panel.2), channel_id=1, source_target_pairs={{0,16},{4,20},{8,24},{12,28},{16,0},{20,4},{24,8},{28,12},{1,17},{... | collective-permute-start | bytes 6291464 | tf_op jit(solution)/shard_map/ppermute | solution.py:33
  12.4 15.1 %copy-start.8 = (s32[2,16384]{1,0:T(2,128)S(1)}, s32[2,16384]{1,0:T(2,128)}, u32[]{:S(2)}) copy-start(s32[2,16384]{1,0:T(2,128)} %param.118) | copy-start | bytes 393220
  37.9 25.0 %copy-start.6 = (f32[16,128]{1,0:T(8,128)}, f32[16,128]{1,0:T(8,128)S(1)}, u32[]{:S(2)}) copy-start(f32[16,128]{1,0:T(8,128)S(1)} %gather_fusion) | copy-start | bytes 24580
  38.0 8.5 %copy-start.19 = (s32[16]{0:T(128)}, s32[16]{0:T(128)S(1)}, u32[]{:S(2)}) copy-start(s32[16]{0:T(128)S(1)} %compare_select_fusion.3.where_ref) | copy-start | bytes 196
  38.0 35.6 %copy-start.9 = (s32[1,128,128]{2,1,0:T(8,128)}, s32[1,128,128]{2,1,0:T(8,128)S(1)}, u32[]{:S(2)}) copy-start(s32[1,128,128]{2,1,0:T(8,128)S(1)} %get-tuple-element.70) | copy-start | bytes 196612
  38.1 8.4 copy-start.7
  38.1 21.3 %copy-start.4 = (s32[16,1,1,128]{3,2,1,0:T(1,128)}, s32[16,1,1,128]{3,2,1,0:T(1,128)S(1)}, u32[]{:S(2)}) copy-start(s32[16,1,1,128]{3,2,1,0:T(1,128)S(1)} %constant_dynamic-slice_fusion.8) | copy-start | bytes 24580
  65.3 260.8 %all-gather.3.cloned.1.call-start = ((), (), s32[]{:S(2)}) async-start(), calls=%async_computation | async-start | bytes 10485760 | tf_op jit(solution)/shard_map/all_gather | solution.py:717
  71.9 105.9 %collective-permute-start.2 = (f32[2,128,32,128]{3,2,1,0:T(8,128)}, f32[2,128,32,128]{3,2,1,0:T(8,128)}, u32[]{:S(2)}, u32[]{:S(2)}) collective-permute-start(f32[2,128,32,128]{3,2,1,0:T(8,128)} %slice_bitcast_fusion.u0), channel_id=1, source_target_pairs={{0,16},{4,20},{8,24},{12,28},{16,0},{20,4},{24,8},{28,12},{1,17},{... | collective-permute-start | bytes 12582920 | tf_op jit(solution)/shard_map/ppermute | solution.py:33
  74.2 251.9 %collective-permute-start.1 = (f32[66,128,128]{2,1,0:T(8,128)}, f32[66,128,128]{2,1,0:T(8,128)}, u32[]{:S(2)}, u32[]{:S(2)}) collective-permute-start(f32[66,128,128]{2,1,0:T(8,128)} %pack_lower.2), channel_id=1, source_target_pairs={{0,16},{4,20},{8,24},{12,28},{16,0},{20,4},{24,8},{28,12},{1,17},{... | collective-permute-start | bytes 12976136 | tf_op jit(solution)/shard_map/ppermute | solution.py:33
  193.3 151.9 %collective-permute-start.3 = (f32[2,32,128,128]{3,2,1,0:T(8,128)}, f32[2,32,128,128]{3,2,1,0:T(8,128)}, u32[]{:S(2)}, u32[]{:S(2)}) collective-permute-start(f32[2,32,128,128]{3,2,1,0:T(8,128)} %place_rows.1.refs_0_), channel_id=1, source_target_pairs={{0,8},{4,12},{8,0},{12,4},{1,9},{5,13},{9,1},{13,5},{2,10},{6,14},... | collective-permute-start | bytes 12582920 | tf_op jit(solution)/shard_map/ppermute | solution.py:33
  326.2 19.1 %copy-start.3 = (f32[2,32,128,128]{3,2,1,0:T(8,128)S(1)}, f32[2,32,128,128]{3,2,1,0:T(8,128)}, u32[]{:S(2)}) copy-start(f32[2,32,128,128]{3,2,1,0:T(8,128)} %place_rows.1.refs_0_) | copy-start | bytes 12582916
  352.0 19.2 %collective-permute-start.4 = (f32[4,32,128,128]{3,2,1,0:T(8,128)}, f32[4,32,128,128]{3,2,1,0:T(8,128)}, u32[]{:S(2)}, u32[]{:S(2)}) collective-permute-start(f32[4,32,128,128]{3,2,1,0:T(8,128)} %pad_maximum_fusion), channel_id=1, source_target_pairs={{0,4},{4,0},{8,12},{12,8},{1,5},{5,1},{9,13},{13,9},{2,6},{6,2},{1... | collective-permute-start | bytes 25165832 | tf_op jit(solution)/shard_map/ppermute | solution.py:33
  352.0 79.5 %collective-permute-start.5 = (f32[54,128,128]{2,1,0:T(8,128)}, f32[54,128,128]{2,1,0:T(8,128)S(1)}, u32[]{:S(2)}, u32[]{:S(2)}) collective-permute-start(f32[54,128,128]{2,1,0:T(8,128)} %pack_lower.3), channel_id=1, source_target_pairs={{0,16},{4,20},{8,24},{12,28},{16,0},{20,4},{24,8},{28,12},{1,17},{... | collective-permute-start | bytes 10616840 | tf_op jit(solution)/shard_map/ppermute | solution.py:33
  357.4 212.4 %collective-permute-start.6 = (f32[5,15,128,128]{3,2,1,0:T(8,128)}, f32[5,15,128,128]{3,2,1,0:T(8,128)}, u32[]{:S(2)}, u32[]{:S(2)}) collective-permute-start(f32[5,15,128,128]{3,2,1,0:T(8,128)} %slice.73), channel_id=1, source_target_pairs={{0,16},{4,20},{8,24},{12,28},{16,0},{20,4},{24,8},{28,12},{1,17},{... | collective-permute-start | bytes 14745608 | tf_op jit(solution)/shard_map/ppermute | solution.py:33
  359.2 268.7 %collective-permute-start.7 = (f32[66,128,128]{2,1,0:T(8,128)}, f32[66,128,128]{2,1,0:T(8,128)}, u32[]{:S(2)}, u32[]{:S(2)}) collective-permute-start(f32[66,128,128]{2,1,0:T(8,128)} %collective-permute-done.1.refs_4_.refs_5_.refs_6_.refs_7_), channel_id=1, source_target_pairs={{1,4},{2,8},{3,12},{4,1},{6,9},{7,13},{8,2},{9,6},{11,14},{12,3},{... | collective-permute-start | bytes 12976136 | tf_op jit(solution)/shard_map/ppermute | solution.py:758
  371.2 66.3 %copy-start.20 = (s32[4,1,4]{0,2,1:T(4,128)S(1)}, s32[4,1,4]{0,2,1:T(4,128)}, u32[]{:S(2)}) copy-start(s32[4,1,4]{0,2,1:T(4,128)} %constant.332.clone) | copy-start | bytes 196
  371.2 66.3 %copy-start.21 = (s32[4,1,4]{0,2,1:T(4,128)S(1)}, s32[4,1,4]{0,2,1:T(4,128)}, u32[]{:S(2)}) copy-start(s32[4,1,4]{0,2,1:T(4,128)} %constant.325.clone) | copy-start | bytes 196
  431.5 69.5 %copy-start.2 = (f32[54,128,128]{2,1,0:T(8,128)}, f32[54,128,128]{2,1,0:T(8,128)S(1)}, u32[]{:S(2)}) copy-start(f32[54,128,128]{2,1,0:T(8,128)S(1)} %collective-permute-done.5.refs_8_.refs_9_.refs_10_.refs_11_) | copy-start | bytes 10616836
  431.5 168.6 %collective-permute-start.9 = (f32[3,15,128,128]{3,2,1,0:T(8,128)}, f32[3,15,128,128]{3,2,1,0:T(8,128)}, u32[]{:S(2)}, u32[]{:S(2)}) collective-permute-start(f32[3,15,128,128]{3,2,1,0:T(8,128)} %get-tuple-element.57), channel_id=1, source_target_pairs={{0,16},{4,20},{8,24},{12,28},{16,0},{20,4},{24,8},{28,12},{1,17},{... | collective-permute-start | bytes 8847368 | tf_op jit(solution)/shard_map/ppermute | solution.py:33
  431.8 271.6 %collective-permute-start.8 = (f32[54,128,128]{2,1,0:T(8,128)S(1)}, f32[54,128,128]{2,1,0:T(8,128)}, u32[]{:S(2)}, u32[]{:S(2)}) collective-permute-start(f32[54,128,128]{2,1,0:T(8,128)S(1)} %collective-permute-done.5.refs_8_.refs_9_.refs_10_.refs_11_), channel_id=1, source_target_pairs={{1,4},{2,8},{3,12},{4,1},{6,9},{7,13},{8,2},{9,6},{11,14},{12,3},{... | collective-permute-start | bytes 10616840 | tf_op jit(solution)/shard_map/ppermute | solution.py:785
  438.8 190.0 %copy-start.10 = (s32[4,1,4]{0,2,1:T(4,128)}, s32[4,1,4]{0,2,1:T(4,128)S(1)}, u32[]{:S(2)}) copy-start(s32[4,1,4]{0,2,1:T(4,128)S(1)} %get-tuple-element.104) | copy-start | bytes 196
  438.8 63.8 %copy-start.15 = (s32[4,2,4]{0,2,1:T(4,128)S(1)}, s32[4,2,4]{0,2,1:T(4,128)}, u32[]{:S(2)}) copy-start(s32[4,2,4]{0,2,1:T(4,128)} %constant.323.clone) | copy-start | bytes 388
  438.8 63.8 %copy-start.16 = (s32[4,2,4]{0,2,1:T(4,128)S(1)}, s32[4,2,4]{0,2,1:T(4,128)}, u32[]{:S(2)}) copy-start(s32[4,2,4]{0,2,1:T(4,128)} %constant.322.clone) | copy-start | bytes 388
  438.8 64.4 %copy-start.11 = (s32[4,3,4]{0,2,1:T(4,128)S(1)}, s32[4,3,4]{0,2,1:T(4,128)}, u32[]{:S(2)}) copy-start(s32[4,3,4]{0,2,1:T(4,128)} %constant.314.clone) | copy-start | bytes 580
  438.8 64.4 %copy-start.12 = (s32[4,3,4]{0,2,1:T(4,128)S(1)}, s32[4,3,4]{0,2,1:T(4,128)}, u32[]{:S(2)}) copy-start(s32[4,3,4]{0,2,1:T(4,128)} %constant.313.clone) | copy-start | bytes 580
  438.8 65.0 %copy-start.17 = (s32[4,2,4]{0,2,1:T(4,128)S(1)}, s32[4,2,4]{0,2,1:T(4,128)}, u32[]{:S(2)}) copy-start(s32[4,2,4]{0,2,1:T(4,128)} %constant.324.clone) | copy-start | bytes 388
  438.8 65.0 %copy-start.18 = (s32[4,2,4]{0,2,1:T(4,128)S(1)}, s32[4,2,4]{0,2,1:T(4,128)}, u32[]{:S(2)}) copy-start(s32[4,2,4]{0,2,1:T(4,128)} %constant.317.clone) | copy-start | bytes 388
  438.8 65.0 %copy-start.24 = (pred[4,2,4]{0,2,1:T(4,128)(4,1)S(1)}, pred[4,2,4]{0,2,1:T(4,128)(4,1)}, u32[]{:S(2)}) copy-start(pred[4,2,4]{0,2,1:T(4,128)(4,1)} %constant.321.clone) | copy-start | bytes 100
  438.8 64.9 %copy-start.25 = (pred[4,2,4]{0,2,1:T(4,128)(4,1)S(1)}, pred[4,2,4]{0,2,1:T(4,128)(4,1)}, u32[]{:S(2)}) copy-start(pred[4,2,4]{0,2,1:T(4,128)(4,1)} %constant.320.clone) | copy-start | bytes 100
  438.8 64.9 %copy-start.26 = (pred[4,2,4]{0,2,1:T(4,128)(4,1)S(1)}, pred[4,2,4]{0,2,1:T(4,128)(4,1)}, u32[]{:S(2)}) copy-start(pred[4,2,4]{0,2,1:T(4,128)(4,1)} %constant.318.clone) | copy-start | bytes 100
  438.8 65.6 %copy-start.13 = (s32[4,3,4]{0,2,1:T(4,128)S(1)}, s32[4,3,4]{0,2,1:T(4,128)}, u32[]{:S(2)}) copy-start(s32[4,3,4]{0,2,1:T(4,128)} %constant.316.clone) | copy-start | bytes 580
  438.9 65.5 %copy-start.14 = (s32[4,3,4]{0,2,1:T(4,128)S(1)}, s32[4,3,4]{0,2,1:T(4,128)}, u32[]{:S(2)}) copy-start(s32[4,3,4]{0,2,1:T(4,128)} %constant.315.clone) | copy-start | bytes 580
  501.0 269.0 %collective-permute-start.10 = (f32[3,15,128,128]{3,2,1,0:T(8,128)}, f32[3,15,128,128]{3,2,1,0:T(8,128)}, u32[]{:S(2)}, u32[]{:S(2)}) collective-permute-start(f32[3,15,128,128]{3,2,1,0:T(8,128)} %get-tuple-element.59), channel_id=1, source_target_pairs={{0,16},{4,20},{8,24},{12,28},{16,0},{20,4},{24,8},{28,12},{1,17},{... | collective-permute-start | bytes 8847368 | tf_op jit(solution)/shard_map/ppermute | solution.py:33
  508.1 63.5 %copy-start.5 = (s32[32,1,128]{2,1,0:T(1,128)S(1)}, s32[32,1,128]{2,1,0:T(1,128)}, u32[]{:S(2)}) copy-start(s32[32,1,128]{2,1,0:T(1,128)} %constant_dynamic-slice_fusion.2) | copy-start | bytes 49156
  569.7 224.9 %collective-permute-start.11 = (f32[2,15,128,128]{3,2,1,0:T(8,128)}, f32[2,15,128,128]{3,2,1,0:T(8,128)}, u32[]{:S(2)}, u32[]{:S(2)}) collective-permute-start(f32[2,15,128,128]{3,2,1,0:T(8,128)} %slice.76), channel_id=1, source_target_pairs={{0,16},{4,20},{8,24},{12,28},{16,0},{20,4},{24,8},{28,12},{1,17},{... | collective-permute-start | bytes 5898248 | tf_op jit(solution)/shard_map/ppermute | solution.py:33
  578.4 49.8 %copy-start.22 = (s32[4,1,4]{0,2,1:T(4,128)S(1)}, s32[4,1,4]{0,2,1:T(4,128)}, u32[]{:S(2)}) copy-start(s32[4,1,4]{0,2,1:T(4,128)} %constant.331.clone) | copy-start | bytes 196
  578.4 49.8 %copy-start.23 = (s32[4,1,4]{0,2,1:T(4,128)S(1)}, s32[4,1,4]{0,2,1:T(4,128)}, u32[]{:S(2)}) copy-start(s32[4,1,4]{0,2,1:T(4,128)} %constant.330.clone) | copy-start | bytes 196
  600.1 211.4 %collective-permute-start.12 = (f32[1,15,128,128]{3,2,1,0:T(8,128)}, f32[1,15,128,128]{3,2,1,0:T(8,128)}, u32[]{:S(2)}, u32[]{:S(2)}) collective-permute-start(f32[1,15,128,128]{3,2,1,0:T(8,128)} %get-tuple-element.61), channel_id=1, source_target_pairs={{0,16},{4,20},{8,24},{12,28},{16,0},{20,4},{24,8},{28,12},{1,17},{... | collective-permute-start | bytes 2949128 | tf_op jit(solution)/shard_map/ppermute | solution.py:33
  627.8 193.4 %collective-permute-start.13 = (f32[1,15,128,128]{3,2,1,0:T(8,128)}, f32[1,15,128,128]{3,2,1,0:T(8,128)}, u32[]{:S(2)}, u32[]{:S(2)}) collective-permute-start(f32[1,15,128,128]{3,2,1,0:T(8,128)} %get-tuple-element.62), channel_id=1, source_target_pairs={{0,16},{4,20},{8,24},{12,28},{16,0},{20,4},{24,8},{28,12},{1,17},{... | collective-permute-start | bytes 2949128 | tf_op jit(solution)/shard_map/ppermute | solution.py:33
  821.3 9.8 %copy-start.1 = (f32[16384]{0:T(1024)S(1)}, f32[16384]{0:T(1024)}, u32[]{:S(2)}) copy-start(f32[16384]{0:T(1024)} %param.119) | copy-start | bytes 196612
Sparse Core Ops, SparseCore 0:
  65.4 72.8 all-gather.4
  139.9 149.3 all-gather.2

commit v3 on v2

--- a/solution.py
+++ b/solution.py
@@ -118,25 +118,34 @@
     )(half, parity, child)
 
 
+def lower_start(row, first, last):
+    width = last - first
+    short, long = row - first, row - last
+    return short * (short + 1) // 2 if long <= 0 else width * (width + 1) // 2 + long * width
+
+
 def pack_lower(child, half, parity, first, last):
-    _, _, _, tile, cols, lanes = child.shape
-    base = first * (first - 1) // 2
-    count = last * (last - 1) // 2 - base
+    _, _, rows, tile, cols, lanes = child.shape
+    count = lower_start(rows, first, last)
+    width = last - first
 
     def kernel(half_ref, parity_ref, raw, out):
         j = pl.program_id(0) + first
-        start = j * (j - 1) // 2 - base - 1
-        for i in range(1, last):
+        short, long = j - first, j - last
+        start = jnp.where(
+            long <= 0, short * (short + 1) // 2, width * (width + 1) // 2 + long * width
+        )
+        flat = raw.reshape(tile * cols, lanes)
+        for i in range(first, last):
             @pl.when(i <= j)
             def _():
-                at = pl.ds(2 * i + parity_ref[0], tile, cols)
-                out[start + i] = raw.reshape(tile * cols, lanes)[at, :]
+                out[start + i - first] = flat[pl.ds(2 * i + parity_ref[0], tile, cols), :]
 
     return pl.pallas_call(
         kernel,
         grid_spec=pltpu.PrefetchScalarGridSpec(
             num_scalar_prefetch=2,
-            grid=(last - first,),
+            grid=(rows - first,),
             in_specs=[
                 pl.BlockSpec(
                     (1, 1, 1, tile, cols, lanes), lambda j, h, b: (0, h[0], j + first, 0, 0, 0)
@@ -146,7 +155,7 @@
         ),
         out_shape=jax.ShapeDtypeStruct((count, tile, lanes), F32),
         compiler_params=params(),
-        cost_estimate=cost(0, tile * lanes * 4 * ((last - first) * cols + count)),
+        cost_estimate=cost(0, tile * lanes * 4 * ((rows - first) * cols + count)),
         name="pack_lower",
     )(half, parity, child)
 
@@ -252,20 +261,34 @@
         index = jnp.full(value.shape, j, jnp.int32)
         return jnp.take_along_axis(value, index, axis=1, mode="promise_in_bounds")
 
-    def body(j, carry):
-        whole = block[...]
-        row = jnp.broadcast_to(block[pl.ds(j, 1), :], (SUB, tile))
-        here = lane == j
-        pivot = at_lane(row, j)
-        root = lax.rsqrt(pivot)
-        root = root * (1.5 - 0.5 * pivot * root * root)
-        row = jnp.where(here, root, row * root)[:1]
-        column = jnp.where(sub > j, at_lane(whole, j), 0.0) * root[:1]
-        kept = jnp.where(here & (sub > j), 0.0, whole)
-        block[...] = jnp.where(sub == j, row, kept - column * row)
+    def body(g, carry):
+        at = pl.multiple_of(g * SUB, SUB)
+        rows = block[pl.ds(at, SUB), :]
+        whole = block[...].reshape(tile // SUB, SUB, tile)
+        within = lax.broadcasted_iota(jnp.int32, (SUB, tile), 0)
+        below = sub.reshape(tile // SUB, SUB, 1) >= at + SUB
+        for r in range(SUB):
+            j = at + r
+            here = lane == j
+            row = jnp.broadcast_to(rows[r : r + 1, :], (SUB, tile))
+            pivot = at_lane(row, j)
+            root = lax.rsqrt(pivot)
+            root = root * (1.5 - 0.5 * pivot * root * root)
+            row = jnp.where(here, root, row * root)
+            column = at_lane(rows, j) * root
+            under = within > r
+            rows = jnp.where(
+                under,
+                jnp.where(here, 0.0, rows) - column * row,
+                jnp.where(within == r, row, rows),
+            )
+            column = at_lane(whole.reshape(tile, tile), j).reshape(whole.shape) * root[None]
+            whole = jnp.where(here[None], 0.0, whole) - column * row[None]
+        block[...] = jnp.where(below, whole, block[...].reshape(whole.shape)).reshape(tile, tile)
+        block[pl.ds(at, SUB), :] = rows
         return carry
 
-    lax.fori_loop(0, tile, body, 0)
+    lax.fori_loop(0, tile // SUB, body, 0)
     low = lax.broadcasted_iota(jnp.int32, (tile, tile), 0) >= (
         lax.broadcasted_iota(jnp.int32, (tile, tile), 1)
     )
@@ -525,21 +548,28 @@
     )(rowmap, front, block, colmap)
 
 
-def add_tiles(front, sources, picks, stands, rowmap, colmap, first, count):
+def add_tiles(front, entries, steps, rowmap, colmap):
     _, _, tile, cols, lanes = front.shape
-    width = len(sources)
-    groups = cols // SUB
-    picks, stands = (t.astype(jnp.int32).reshape(-1) for t in (picks, stands))
-
-    def entry(slot, n, g):
-        return (slot * count + n) * groups + g
-
-    def kernel(map_ref, picks_ref, stands_ref, before, *refs):
+    sources, picks, stands = [], [], []
+    for array, pick, stand, ever in entries:
+        for slot in range(len(ever)):
+            if ever[slot]:
+                sources.append(array)
+                picks.append(pick[slot])
+                stands.append(stand[slot])
+    width, count = len(sources), len(steps)
+    picks, stands = (jnp.concatenate(t).astype(jnp.int32) for t in (picks, stands))
+    order = jnp.array([row for row, _ in steps] + [group for _, group in steps], jnp.int32)
+
+    def kernel(map_ref, order_ref, picks_ref, stands_ref, before, *refs):
         tiles, (c, out, flat) = refs[:width], refs[width:]
-        n, g = pl.program_id(0), pl.program_id(1)
+        n = pl.program_id(0)
+        sub = lax.broadcasted_iota(jnp.int32, (SUB, lanes), 0)
+        given = jnp.zeros((SUB, lanes), jnp.int32)
         for slot in range(width):
-            stand = stands_ref[entry(slot, n, g)]
+            stand = stands_ref[slot * count + n]
             p = stand // 2
+            given = jnp.where((stand >= 0) & (sub == p), 1, given)
 
             @pl.when((stand >= 0) & (stand % 2 == 0))
             def _():
@@ -557,77 +587,69 @@
             for r, value in enumerate(values):
                 out[0, 0, at + r] = value
 
-        place_block(map_ref, n + first, load, c[...], add)
-
-    spec = pl.BlockSpec((1, 1, tile, SUB, lanes), lambda n, g, *_: (0, n + first, 0, g, 0))
+        place_block(map_ref, order_ref[n], load, jnp.where(given == 1, c[...], -1), add)
+
+    spec = pl.BlockSpec(
+        (1, 1, tile, SUB, lanes), lambda n, m, o, *_: (0, o[n], 0, o[count + n], 0)
+    )
 
     def tile_spec(slot):
-        return pl.BlockSpec((1, tile, lanes), lambda n, g, m, k, t: (k[entry(slot, n, g)], 0, 0))
-
-    return pl.pallas_call(
-        kernel,
-        grid_spec=pltpu.PrefetchScalarGridSpec(
-            num_scalar_prefetch=3,
-            grid=(count, groups),
+        return pl.BlockSpec((1, tile, lanes), lambda n, m, o, k, t: (k[slot * count + n], 0, 0))
+
+    return pl.pallas_call(
+        kernel,
+        grid_spec=pltpu.PrefetchScalarGridSpec(
+            num_scalar_prefetch=4,
+            grid=(count,),
             in_specs=[spec]
             + [tile_spec(slot) for slot in range(width)]
-            + [pl.BlockSpec((SUB, lanes), lambda n, g, *_: (g, 0))],
+            + [pl.BlockSpec((SUB, lanes), lambda n, m, o, *_: (o[count + n], 0))],
             out_specs=spec,
             scratch_shapes=[pltpu.VMEM((tile * SUB, lanes), F32)],
         ),
         out_shape=jax.ShapeDtypeStruct(front.shape, F32),
-        input_output_aliases={3: 0},
-        compiler_params=params(2),
-        cost_estimate=cost(0, count * tile * cols * lanes * 12),
+        input_output_aliases={4: 0},
+        compiler_params=params(),
+        cost_estimate=cost(0, count * tile * SUB * lanes * 12),
         name="add_tiles",
-    )(rowmap, picks, stands, front, *sources, colmap)
-
-
-def triangle(row):
-    return row * (row - 1) // 2
+    )(rowmap, order, picks, stands, front, *sources, colmap)
 
 
 def held_picks(picks, given):
-    flat, mask = picks.reshape(picks.shape[0], -1).copy(), given.reshape(picks.shape[0], -1)
-    for step in range(1, flat.shape[1]):
-        flat[:, step] = np.where(mask[:, step], flat[:, step], flat[:, step - 1])
-    return flat.reshape(picks.shape).astype(np.int32)
-
-
-def lower_tables(exchanged, first, last, rows, parity, alone, start, count):
-    groups = rows // (SUB // 2)
-    slot, n, g = np.meshgrid(
-        np.arange(SUB // 2), np.arange(start, start + count), np.arange(groups), indexing="ij"
-    )
-    i = g * (SUB // 2) + slot
-    place = 2 * (2 * slot + parity)
-
-    def inside(row, col):
-        return (row >= first) & (row < last) & (col >= 1), triangle(row) - triangle(first) + col - 1
-
-    straight, at = inside(n, i)
-    straight &= i <= n
-    mirror, at_mirror = inside(i, n)
-    mirror &= n < i
-    if exchanged:
-        picks = held_picks(np.where(mirror, at_mirror, 0), mirror)
-        return jnp.where(alone, 0, picks), jnp.where(mirror & ~alone, place + 1, -1)
-    mine = held_picks(np.where(straight, at, 0), straight)
-    both = straight | mirror
-    all_of_it = held_picks(np.where(straight, at, np.where(mirror, at_mirror, 0)), both)
-    stands = jnp.where(straight, place, jnp.where(mirror & alone, place + 1, -1))
-    return jnp.where(alone, all_of_it, mine), stands
-
-
-def cross_tables(rows, parity, start, count):
-    groups = rows // (SUB // 2)
-    slot, n, g = np.meshgrid(
-        np.arange(SUB // 2), np.arange(count), np.arange(groups), indexing="ij"
-    )
-    i = g * (SUB // 2) + slot
-    picks = np.where(i >= 1, n * (rows - 1) + i - 1, n * (rows - 1))
-    stands = jnp.where(i >= 1, 2 * (2 * slot + parity), -1)
-    return jnp.asarray(picks, jnp.int32), stands
+    held = np.where(given, picks, 0)
+    for step in range(1, held.shape[1]):
+        held[:, step] = np.where(given[:, step], held[:, step], held[:, step - 1])
+    return held.astype(np.int32)
+
+
+def straight_entry(array, first, last, rows, parity, steps):
+    j, g = np.array(steps).T
+    i = g[None, :] * (SUB // 2) + np.arange(SUB // 2)[:, None]
+    begins = np.array([lower_start(max(row, first), first, last) for row in range(rows)])
+    given = (i >= first) & (i < last) & (i <= j)
+    picks = held_picks(begins[j] + i - first, given)
+    place = 2 * (2 * np.arange(SUB // 2)[:, None] + parity)
+    return array, jnp.asarray(picks), jnp.where(given, place, -1), given.any(axis=1)
+
+
+def turned_entry(array, first, last, rows, parity, steps, used):
+    j, g = np.array(steps).T
+    i = g[None, :] * (SUB // 2) + np.arange(SUB // 2)[:, None]
+    begins = np.array([lower_start(max(row, first), first, last) for row in range(rows)])
+    given = (j >= first) & (j < last) & (i > j)
+    picks = held_picks(begins[i] + j - first, given)
+    place = 2 * (2 * np.arange(SUB // 2)[:, None] + parity) + 1
+    stands = jnp.where(given & used, place, -1)
+    return array, jnp.where(used, picks, 0), stands, given.any(axis=1)
+
+
+def cross_entry(array, rows, parity, steps):
+    j, g = np.array(steps).T
+    i = g[None, :] * (SUB // 2) + np.arange(SUB // 2)[:, None]
+    given = i >= 1
+    picks = held_picks((j - j[0]) * (rows - 1) + i - 1, given)
+    place = 2 * (2 * np.arange(SUB // 2)[:, None] + parity)
+    return array, jnp.asarray(picks), jnp.where(given, place, -1), given.any(axis=1)
 
 
 def on_device(child_update, child_map, parent_diag):
@@ -692,11 +714,12 @@
     panel_own = pack_panel(after(child_update, panel_sent), own, local)
     panel_came = swapped(panel_sent, subcubes, distance)
     if mirrored:
-        near = 1 + (rows * 11) // 16
-        cuts = [(1, near), (near, rows)]
+        near = spans[0][0] + spans[0][1]
+        edges = [1, 2, 4, near, near + 2, rows]
+        cuts = list(zip(edges[:-1], edges[1:]))
         lower_sent = [pack_lower(child_update, other, other, a, b) for a, b in cuts]
-        pivot_sent = child_update[0, :, 0]
-        panel_came = after(panel_came, panel_own, pivot_sent, lower_sent[0])
+        pivot_sent = after(child_update, panel_sent)[0, :, 0]
+        panel_came = after(panel_came, panel_own, pivot_sent, *lower_sent[:3])
     else:
         pivot_sent = lax.dynamic_slice_in_dim(child_update[0, :, 0], 1 - sibling, 1, 0)
 
@@ -720,7 +743,7 @@
     pivot = pivot.reshape(grid_size, columns, tile, local, tile)[:pivots]
     pivot = jnp.transpose(pivot, (0, 2, 3, 1, 4)).reshape(K, K)
 
-    pivot_came = swapped(after(pivot_sent, panel_came), subcubes, distance)
+    pivot_came = swapped(pivot_sent, subcubes, distance)
     if mirrored:
         pairs = [
             (r * columns + c, c * columns + r)
@@ -728,10 +751,10 @@
             for c in range(columns)
             if r != c
         ]
-        lower_a = swapped(after(lower_sent[0], front_panel), subcubes, distance)
+        lower = [swapped(after(part, front_panel), subcubes, distance) for part in lower_sent[:3]]
         sent = pack_cross(after(child_update, front_panel), other, own)
-        pivot_came = after(pivot_came, sent, lower_sent[1])
-        lower_b = swapped(after(lower_sent[1], pivot_came), subcubes, distance)
+        pivot_came = after(pivot_came, sent, *lower_sent[3:])
+        lower += [swapped(after(part, pivot_came), subcubes, distance) for part in lower_sent[3:]]
         block_rows = half_grid * jnp.arange(2, dtype=jnp.int32) + within
         pivot_rows = place_rows(
             pivot_sent,
@@ -754,13 +777,13 @@
         came.append(swapped(part, subcubes, distance))
 
     if mirrored:
-        lower_a = after(lower_a, high)
-        turned_a = lax.ppermute(lower_a, ("row", "col"), pairs)
-        send(0, lower_a)
-        gathered = after(gathered, lower_a)
+        lower[:2] = [after(part, high) for part in lower[:2]]
+        turned = [lax.ppermute(part, ("row", "col"), pairs) for part in lower[:2]]
+        send(0, lower[1])
+        gathered = after(gathered, *lower[:2])
     left_h, left_l, panel = solve_rows(gathered, high, low, column_index.astype(jnp.int32)[None])
     if mirrored:
-        across = after(across, left_h)
+        across = after(across, left_h, lower[2], lower[3])
         beside = swapped(jnp.concatenate([pivot_rows, across]), "row", 0)
         parts = [pivot_rows, across, beside]
         homes = [block_rows ^ bits for bits in (0, 2, 1, 3)]
@@ -781,10 +804,10 @@
         first = pivot_came
     right_h, right_l = solve_columns(parts, jnp.concatenate(homes), high, low)
     if mirrored:
-        lower_b = after(lower_b, right_h)
-        turned_b = lax.ppermute(lower_b, ("row", "col"), pairs)
-        send(1, lower_b)
-        right_h = after(right_h, lower_b)
+        turned[0] = after(turned[0], left_h)
+        turned += [lax.ppermute(part, ("row", "col"), pairs) for part in lower[2:4]]
+        send(1, turned[0])
+        right_h = after(right_h, turned[0])
 
     front = None
     groups = cols // SUB
@@ -803,32 +826,49 @@
             end,
         )
         if mirrored:
+            if start > 0:
+                send(2, front)
+                lower[4] = after(lower[4], front)
+            front = after(front, turned[1]) if start == 0 else after(front, turned[2], lower[4])
+    if mirrored:
+        turned.append(lax.ppermute(lower[4], ("row", "col"), pairs))
+    front = add_first(front, first, other_rows[:1], trailing_cols)
+
+    def turned_tiles(front, parts, low, top):
+        steps = [
+            (j, g)
+            for j in range(low, top)
+            for g in range(groups)
+            if j < min(rows, (g + 1) * (SUB // 2)) - 1
+        ]
+        alone = within == column_index
+        entries = []
+        for part in parts:
+            mine = (*cuts[part], rows, sibling, steps)
+            entries.append(turned_entry(turned[part], *mine, ~alone))
+            entries.append(turned_entry(lower[part], *mine, alone))
+        return add_tiles(front, entries, steps, other_rows, trailing_cols)
+
+    for number, (at, count) in enumerate(spans):
+        if len(came) < len(spans):
             send(len(came), front)
-    front = add_first(front, first, other_rows[:1], trailing_cols)
-    if mirrored:
-        turned_a = after(turned_a, front)
-        for number in range(len(came), len(spans)):
-            came[number - 4] = after(came[number - 4], front)
-            send(number, came[number - 4])
-    for (at, count), array in zip(spans, came):
-        flat = array.reshape(-1, tile, tile)
+        flat = came[number].reshape(-1, tile, tile)
+        steps = [(j, g) for j in range(at, at + count) for g in range(groups)]
         if mirrored:
-            half = SUB // 2
-            alone = within == column_index
-            tables = [(flat, cross_tables(rows, 1 - sibling, at, count))]
-            for exchanged, group in ((False, (lower_a, lower_b)), (True, (turned_a, turned_b))):
-                for (a, b), source in zip(cuts, group):
-                    table = lower_tables(exchanged, a, b, rows, sibling, alone, at, count)
-                    tables.append((source, table))
-            arrays = [source for source, _ in tables for _ in range(half)]
-            picks = jnp.concatenate([pick for _, (pick, _) in tables])
-            stands = jnp.concatenate([stand for _, (_, stand) in tables])
+            if number == 2:
+                front = turned_tiles(after(front, turned[3]), (0, 1, 2), 1, near)
+            if number == len(spans) - 1:
+                front = turned_tiles(front, (3, 4), near, rows)
+            entries = [cross_entry(flat, rows, 1 - sibling, steps)]
+            for part, cut in zip(lower, cuts):
+                entries.append(straight_entry(part, *cut, rows, sibling, steps))
         else:
-            arrays = [flat] * SUB
-            shape = (SUB, count, cols // SUB)
-            slot, n, g = (lax.broadcasted_iota(jnp.int32, shape, axis) for axis in range(3))
-            picks, stands = n * cols + g * SUB + slot, 2 * slot
-        front = add_tiles(front, arrays, picks, stands, other_rows, trailing_cols, at, count)
+            j, g = np.array(steps).T
+            slot = np.arange(SUB)[:, None]
+            picks = jnp.asarray((j - at) * cols + g * SUB + slot, jnp.int32)
+            stands = jnp.asarray(np.broadcast_to(2 * slot, picks.shape), jnp.int32)
+            entries = [(flat, picks, stands, np.ones(SUB, bool))]
+        front = add_tiles(front, entries, steps, other_rows, trailing_cols)
     return front
 
 

time: 850 us -> 875 us (1.029)
  Pallas kernels: 498 us -> 568 us
  waiting for transfers between devices: 190 us -> 141 us
  starting transfers between devices: 19.5 us -> 30.6 us
    ppermute x12 -> x15, waiting for transfers between devices: 130 us -> 52.4 us  [swapped(): return lax.ppermute(value, axis, pairs)]
    pallas_call x2 -> x5, Pallas kernels: 23.1 us -> 64.5 us  [pack_lower(): pl.pallas_call(kernel, grid_spec=pltpu.PrefetchScalarGridSpec(num_scalar_...]
    pallas_call x6 -> x8, Pallas kernels: 128 us -> 165 us  [add_tiles(): pl.pallas_call(kernel, grid_spec=pltpu.PrefetchScalarGridSpec(num_scalar_...]
    ppermute x2 -> x5, waiting for transfers between devices: 60.6 us -> 88.4 us  [the longest x2 88 us: on_device(): turned = [lax.ppermute(part, ('row', 'col'), pairs) for part in lower[:2]]]
    squeeze x1 -> x44, local copies, waits for them, and re-layouts: 4.64 us -> 23.4 us  [the longest x33 15.2 us: add_tiles(): stands.append(stand[slot])]
    reshape x11 -> x0, local copies, waits for them, and re-layouts: 13.8 us -> none  [add_tiles(): picks, stands = (t.astype(jnp.int32).reshape(-1) for t in (picks, stands))]
    concatenate x22 -> x10, local copies, waits for them, and re-layouts: 22.1 us -> 10.8 us  [add_tiles(): jnp.concatenate(t).astype(jnp.int32)]
    pallas_call x1, Pallas kernels: 121 us -> 111 us  [inverse_factor(): pl.pallas_call(kernel, in_specs=[pl.BlockSpec(memory_space=pltpu.VMEM)],...]
  transfers between devices with their start and end apart: 16 -> 22, of which waited for: 6 -> 3; matrix products, arithmetic and copies ran while one was open for 12% -> 10% of each run, Pallas kernels for 58% -> 64%
where the time goes in v3:
time: 875 us; the launch traced here: 864 us
  Pallas kernels  568 us (65%)
  waiting for transfers between devices  141 us (16%)
  local copies, waits for them, and re-layouts  84.6 us (10%)
  starting transfers between devices  30.6 us (3%)
  between operations  15.2 us (2%)
  other arithmetic  14.7 us (2%)
  matrix products  10.2 us (1%)
    pallas_call x8, Pallas kernels, add_tiles(): pl.pallas_call(kernel, grid_spec=pltpu.PrefetchScalarGridSpec(num_scalar_...  165 us
    pallas_call x2, Pallas kernels, own_part(): pl.pallas_call(kernel, grid_spec=pltpu.PrefetchScalarGridSpec(num_scalar_...  124 us
    pallas_call x1, Pallas kernels, inverse_factor(): pl.pallas_call(kernel, in_specs=[pl.BlockSpec(memory_space=pltpu.VMEM)],...  111 us
    ppermute x2, waiting for transfers between devices, on_device(): turned = [lax.ppermute(part, ('row', 'col'), pairs) for part in lower[:2]]  88 us
    pallas_call x5, Pallas kernels, pack_lower(): pl.pallas_call(kernel, grid_spec=pltpu.PrefetchScalarGridSpec(num_scalar_...  64.5 us
    ppermute x15, waiting for transfers between devices, swapped(): return lax.ppermute(value, axis, pairs)  52.4 us
    pallas_call x1, Pallas kernels, solve_columns(): pl.pallas_call(kernel, grid_spec=pltpu.PrefetchScalarGridSpec(num_scalar_...  26.4 us
    pallas_call x1, Pallas kernels, pack_cross(): pl.pallas_call(kernel, grid_spec=pltpu.PrefetchScalarGridSpec(num_scalar_...  25.1 us
  transfers between devices with their start and end apart: 22, of which 3 were waited for; matrix products, arithmetic and copies ran while one was open for 10% of the time, Pallas kernels for 64%

profile of v3, /device:TPU:6, one launch (start us, length us, event | category | flops | bytes accessed | tf_op | source)
XLA Modules:
  0.0 864.0 jit_solution(2879656443354262949)
XLA Ops:
  6.5 5.3 pack_panel.2
  12.4 14.9 %pack_lower.6 = f32[27,128,128]{2,1,0:T(8,128)} custom-call(s32[1]{0:T(128)S(6)} %sub.93.half_ref.parity_ref, s32[1]{0:T(128)S(6)} %sub.93.half_ref.parity_ref, f32[1,2,16,128,32,128]{5,4,3,2,1,0:T(8,128)} %refs_1_.1), custom_call_target="tpu_custom_call" | custom-call | bytes 311296 | tf_op jit(solution)/shard_map/pack_lower/pallas_call | solution.py:144
  27.3 13.0 %pack_lower.7 = f32[23,128,128]{2,1,0:T(8,128)} custom-call(s32[1]{0:T(128)S(6)} %sub.93.half_ref.parity_ref, s32[1]{0:T(128)S(6)} %sub.93.half_ref.parity_ref, f32[1,2,16,128,32,128]{5,4,3,2,1,0:T(8,128)} %refs_1_.1), custom_call_target="tpu_custom_call" | custom-call | bytes 266731 | tf_op jit(solution)/shard_map/pack_lower/pallas_call | solution.py:144
  40.2 15.2 %pack_lower.5 = f32[15,128,128]{2,1,0:T(8,128)} custom-call(s32[1]{0:T(128)S(6)} %sub.93.half_ref.parity_ref, s32[1]{0:T(128)S(6)} %sub.93.half_ref.parity_ref, f32[1,2,16,128,32,128]{5,4,3,2,1,0:T(8,128)} %refs_1_.1), custom_call_target="tpu_custom_call" | custom-call | bytes 324403 | tf_op jit(solution)/shard_map/pack_lower/pallas_call | solution.py:144
  55.5 5.3 pack_panel.3
  61.1 4.4 select_reduce_fusion
  66.3 3.6 fusion.6
  69.9 4.6 slice_bitcast_fusion.u0
  74.6 3.7 fusion.2
  79.5 1.7 bitcast_add_fusion
  83.8 4.1 copy.198
  87.9 4.0 reshape.256
  93.5 10.4 %pack_lower.9 = f32[36,128,128]{2,1,0:T(8,128)} custom-call(s32[1]{0:T(128)S(6)} %sub.93.half_ref.parity_ref, s32[1]{0:T(128)S(6)} %sub.93.half_ref.parity_ref, f32[1,2,16,128,32,128]{5,4,3,2,1,0:T(8,128)} %refs_1_.1), custom_call_target="tpu_custom_call" | custom-call | bytes 191365 | tf_op jit(solution)/shard_map/pack_lower/pallas_call | solution.py:144
  103.9 11.0 %pack_lower.8 = f32[19,128,128]{2,1,0:T(8,128)} custom-call(s32[1]{0:T(128)S(6)} %sub.93.half_ref.parity_ref, s32[1]{0:T(128)S(6)} %sub.93.half_ref.parity_ref, f32[1,2,16,128,32,128]{5,4,3,2,1,0:T(8,128)} %refs_1_.1), custom_call_target="tpu_custom_call" | custom-call | bytes 222167 | tf_op jit(solution)/shard_map/pack_lower/pallas_call | solution.py:144
  118.9 25.1 %pack_cross.1 = f32[15,15,128,128]{3,2,1,0:T(8,128)} custom-call(s32[1]{0:T(128)S(6)} %sub.93.half_ref.parity_ref, s32[1]{0:T(128)} %bitcast.151.half_ref.parity_ref, f32[1,2,16,128,32,128]{5,4,3,2,1,0:T(8,128)} %refs_1_.1), custom_call_target="tpu_custom_call" | custom-call | bytes 503316 | tf_op jit(solution)/shard_map/pack_cross/pallas_call | solution.py:102
  144.0 52.3 %collective-permute-done.2.u1 = f32[2,128,32,128]{3,2,1,0:T(8,128)} collective-permute-done((f32[2,128,32,128]{3,2,1,0:T(8,128)}, f32[2,128,32,128]{3,2,1,0:T(8,128)}, u32[]{:S(2)}, u32[]{:S(2)}) %collective-permute-start.2) | collective-permute-done | bytes 4194336 | tf_op jit(solution)/shard_map/ppermute | solution.py:33
  196.5 15.6 %place_rows.1.refs_0_ = f32[2,32,128,128]{3,2,1,0:T(8,128)} custom-call(s32[2,128]{1,0:T(2,128)} %bitcast.403, s32[2,128]{1,0:T(2,128)} %bitcast.404, s32[2]{0:T(128)} %compare_select_fusion.2.where_ref, f32[2,128,32,128]{3,2,1,0:T(8,128)} %slice_bitcast_fusion.u0, f32[2,128,32,128]{3,2,1,0:T(8,128)} %collective-permute-done.2.u1, s32[32,128]{1,0:T(8,128)} %bitcast.382, ...), custom_call_target="tpu_custom_call" | custom-call | bytes 125829 | tf_op jit(solution)/shard_map/place_rows/pallas_call | solution.py:233
  212.4 1.7 collective-permute-start.3
  214.4 1.7 collective-permute-start.6
  217.9 5.2 copy.187
  223.1 5.5 reshape.229.a
  228.6 111.1 %inverse_factor.1 = (bf16[1024,1024]{1,0:T(8,128)(2,1)}, bf16[1024,1024]{1,0:T(8,128)(2,1)}) custom-call(f32[1024,1024]{1,0:T(8,128)} %reshape.229.a), custom_call_target="tpu_custom_call" | custom-call | flops 1000000000 | bytes 83886 | tf_op jit(solution)/shard_map/inverse_factor/pallas_call | solution.py:331
  339.8 19.4 %solve_rows.1 = (bf16[2048,1024]{1,0:T(8,128)(2,1)}, bf16[2048,1024]{1,0:T(8,128)(2,1)}, f32[2,2048,128]{2,1,0:T(8,128)}) custom-call(s32[1]{0:T(128)} %bitcast.159.me, f32[4,2048,256]{2,1,0:T(8,128)} %all-gather.3.cloned.1.call-done.f, bf16[1024,1024]{1,0:T(8,128)(2,1)} %get-tuple-element.44.h.refs_3_, bf16[1024,1024]{1,0:T(8,128)(2,1)} %get-tuple-element.49.l.refs_4_), custom_call_target="tpu_custom_call" | custom-call | flops 128849016 | bytes 167772 | tf_op jit(solution)/shard_map/solve_rows/pallas_call | solution.py:368
  359.4 7.2 pad_maximum_fusion
  377.1 5.3 slice.1042
  382.4 1.8 collective-permute-start.12
  388.2 5.4 collective-permute-start.8
  394.2 2.2 collective-permute-start.9
  397.8 6.0 fusion.30
  403.8 88.0 %collective-permute-done.8.refs_0_.refs_1_.refs_2_.refs_3_ = f32[15,128,128]{2,1,0:T(8,128)S(1)} collective-permute-done((f32[15,128,128]{2,1,0:T(8,128)}, f32[15,128,128]{2,1,0:T(8,128)S(1)}, u32[]{:S(2)}, u32[]{:S(2)}) %collective-permute-start.8) | collective-permute-done | bytes 983072 | tf_op jit(solution)/shard_map/ppermute | solution.py:781
  492.8 1.9 collective-permute-start.10
  497.5 26.4 %solve_columns.1 = (bf16[1024,4096]{1,0:T(8,128)(2,1)}, bf16[1024,4096]{1,0:T(8,128)(2,1)}) custom-call(s32[8]{0:T(128)} %pad_add_fusion.home, f32[2,32,128,128]{3,2,1,0:T(8,128)} %place_rows.1.refs_0_, f32[2,32,128,128]{3,2,1,0:T(8,128)} %collective-permute-done.4.refs_1_, f32[4,32,128,128]{3,2,1,0:T(8,128)} %copy-done.11, ...), custom_call_target="tpu_custom_call" | custom-call | flops 171798688 | bytes 335544 | tf_op jit(solution)/shard_map/solve_columns/pallas_call | solution.py:418
  523.9 62.0 %own_part.2.refs_0_ = f32[1,16,128,32,128]{4,3,2,1,0:T(8,128)} custom-call(s32[1]{0:T(128)} %bitcast.151.half_ref.parity_ref, s32[16,128]{1,0:T(8,128)} %bitcast.390, s32[16]{0:T(128)} %copy-done.27, f32[1,2,16,128,32,128]{5,4,3,2,1,0:T(8,128)} %refs_1_.1, s32[32,128]{1,0:T(8,128)} %bitcast.383, f32[16,1,128]{2,1,0:T(1,128)} %bitcast.387, ...), custom_call_target="tpu_custom_call" | custom-call | flops 515396064 | bytes 671088 | tf_op jit(solution)/shard_map/own_part/pallas_call | solution.py:488
  585.9 61.5 %own_part.3.before = f32[1,16,128,32,128]{4,3,2,1,0:T(8,128)} custom-call(s32[1]{0:T(128)} %bitcast.151.half_ref.parity_ref, s32[16,128]{1,0:T(8,128)} %bitcast.391, s32[16]{0:T(128)} %copy-done.27, f32[1,16,128,32,128]{4,3,2,1,0:T(8,128)} %own_part.2.refs_0_, f32[1,2,16,128,32,128]{5,4,3,2,1,0:T(8,128)} %refs_1_.1, ...), custom_call_target="tpu_custom_call", output_to_operand_aliasing={{}: (3, {})} | custom-call | flops 515396064 | bytes 671088 | tf_op jit(solution)/shard_map/own_part/pallas_call | solution.py:488
  650.2 4.3 collective-permute-start.14
  654.5 3.4 collective-permute-start.18
  658.5 3.1 slice.1045
  661.6 3.1 constant_dynamic-slice_fusion.9.u
  664.8 6.1 add_first.1.before
  672.8 3.0 fusion.29
  675.8 26.4 %add_tiles.8.before = f32[1,16,128,32,128]{4,3,2,1,0:T(8,128)} custom-call(s32[16,128]{1,0:T(8,128)} %bitcast.372, s32[40]{0:T(128)} %constant.342.clone.order_ref, s32[180]{0:T(256)} %constant.559.picks_ref, s32[180]{0:T(256)} %concatenate.69.stands_ref, f32[1,16,128,32,128]{4,3,2,1,0:T(8,128)} %add_first.1.before, ...), custom_call_target="tpu_custom_call", output_to_operand_aliasing={{}: (4, {})} | custom-call | bytes 314572 | tf_op jit(solution)/shard_map/add_tiles/pallas_call | solution.py:599
  702.6 18.6 %add_tiles.9.before = f32[1,16,128,32,128]{4,3,2,1,0:T(8,128)} custom-call(s32[16,128]{1,0:T(8,128)} %bitcast.373, s32[24]{0:T(128)} %constant.355.clone.order_ref, s32[144]{0:T(256)} %constant.540.picks_ref, s32[144]{0:T(256)} %concatenate.67.stands_ref, f32[1,16,128,32,128]{4,3,2,1,0:T(8,128)} %add_tiles.8.before, ...), custom_call_target="tpu_custom_call", output_to_operand_aliasing={{}: (4, {})} | custom-call | bytes 188743 | tf_op jit(solution)/shard_map/add_tiles/pallas_call | solution.py:599
  734.2 39.1 %add_tiles.10.before = f32[1,16,128,32,128]{4,3,2,1,0:T(8,128)} custom-call(s32[16,128]{1,0:T(8,128)} %bitcast.374, s32[34]{0:T(128)} %constant.362.clone.order_ref, s32[408]{0:T(512)} %concatenate.64.picks_ref, s32[408]{0:T(512)} %concatenate.65.stands_ref, f32[1,16,128,32,128]{4,3,2,1,0:T(8,128)} %add_tiles.9.before, ...), custom_call_target="tpu_custom_call", output_to_operand_aliasing={{}: (4, {})} | custom-call | bytes 267386 | tf_op jit(solution)/shard_map/add_tiles/pallas_call | solution.py:599
  773.3 20.4 %add_tiles.11.before = f32[1,16,128,32,128]{4,3,2,1,0:T(8,128)} custom-call(s32[16,128]{1,0:T(8,128)} %bitcast.375, s32[24]{0:T(128)} %constant.370.clone.order_ref, s32[180]{0:T(256)} %constant.525.picks_ref, s32[180]{0:T(256)} %concatenate.63.stands_ref, f32[1,16,128,32,128]{4,3,2,1,0:T(8,128)} %add_tiles.10.before, ...), custom_call_target="tpu_custom_call", output_to_operand_aliasing={{}: (4, {})} | custom-call | bytes 188743 | tf_op jit(solution)/shard_map/add_tiles/pallas_call | solution.py:599
  795.0 14.6 %add_tiles.12.before = f32[1,16,128,32,128]{4,3,2,1,0:T(8,128)} custom-call(s32[16,128]{1,0:T(8,128)} %bitcast.376, s32[16]{0:T(128)} %constant.383.clone.order_ref, s32[120]{0:T(128)} %constant.494.picks_ref, s32[120]{0:T(128)} %concatenate.61.stands_ref, f32[1,16,128,32,128]{4,3,2,1,0:T(8,128)} %add_tiles.11.before, ...), custom_call_target="tpu_custom_call", output_to_operand_aliasing={{}: (4, {})} | custom-call | bytes 125829 | tf_op jit(solution)/shard_map/add_tiles/pallas_call | solution.py:599
  809.6 8.7 %add_tiles.13.before = f32[1,16,128,32,128]{4,3,2,1,0:T(8,128)} custom-call(s32[16,128]{1,0:T(8,128)} %bitcast.377, s32[8]{0:T(128)} %constant.396.clone.order_ref, s32[60]{0:T(128)} %constant.463.picks_ref, s32[60]{0:T(128)} %concatenate.59.stands_ref, f32[1,16,128,32,128]{4,3,2,1,0:T(8,128)} %add_tiles.12.before, ...), custom_call_target="tpu_custom_call", output_to_operand_aliasing={{}: (4, {})} | custom-call | bytes 62914 | tf_op jit(solution)/shard_map/add_tiles/pallas_call | solution.py:599
  818.4 28.7 %add_tiles.14.before = f32[1,16,128,32,128]{4,3,2,1,0:T(8,128)} custom-call(s32[16,128]{1,0:T(8,128)} %bitcast.378, s32[30]{0:T(128)} %constant.401.clone.order_ref, s32[240]{0:T(256)} %concatenate.56.picks_ref, s32[240]{0:T(256)} %concatenate.57.stands_ref, f32[1,16,128,32,128]{4,3,2,1,0:T(8,128)} %add_tiles.13.before, ...), custom_call_target="tpu_custom_call", output_to_operand_aliasing={{}: (4, {})} | custom-call | bytes 235929 | tf_op jit(solution)/shard_map/add_tiles/pallas_call | solution.py:599
  848.1 8.9 %add_tiles.15 = f32[1,16,128,32,128]{4,3,2,1,0:T(8,128)} custom-call(s32[16,128]{1,0:T(8,128)} %bitcast.379, s32[8]{0:T(128)} %constant.408.clone.order_ref, s32[60]{0:T(128)} %constant.440.picks_ref, s32[60]{0:T(128)} %concatenate.55.stands_ref, f32[1,16,128,32,128]{4,3,2,1,0:T(8,128)} %add_tiles.14.before, ...), custom_call_target="tpu_custom_call", output_to_operand_aliasing={{}: (4, {})} | custom-call | bytes 62914 | tf_op jit(solution)/shard_map/add_tiles/pallas_call | solution.py:599
  (338 shorter events, 53.8 us)
Async XLA Ops:
  6.5 58.9 %copy-start = (f32[16384]{0:T(1024)S(1)}, f32[16384]{0:T(1024)}, u32[]{:S(2)}) copy-start(f32[16384]{0:T(1024)} %param.145) | copy-start | bytes 196612
  6.5 211.3 %all-gather.5.cloned.1.call-start = ((), (), s32[]{:S(2)}) async-start(), calls=%async_computation.1 | async-start | bytes 4325376 | tf_op jit(solution)/shard_map/all_gather | solution.py:739
  11.8 62.7 %collective-permute-start = (f32[16,2,128,128]{3,2,1,0:T(8,128)}, f32[16,2,128,128]{3,2,1,0:T(8,128)}, u32[]{:S(2)}, u32[]{:S(2)}) collective-permute-start(f32[16,2,128,128]{3,2,1,0:T(8,128)} %pack_panel.2), channel_id=1, source_target_pairs={{0,16},{4,20},{8,24},{12,28},{16,0},{20,4},{24,8},{28,12},{1,17},{... | collective-permute-start | bytes 6291464 | tf_op jit(solution)/shard_map/ppermute | solution.py:33
  83.3 256.5 %all-gather.3.cloned.1.call-start = ((), (), s32[]{:S(2)}) async-start(), calls=%async_computation | async-start | bytes 10485760 | tf_op jit(solution)/shard_map/all_gather | solution.py:740
  91.9 104.4 %collective-permute-start.2 = (f32[2,128,32,128]{3,2,1,0:T(8,128)}, f32[2,128,32,128]{3,2,1,0:T(8,128)}, u32[]{:S(2)}, u32[]{:S(2)}) collective-permute-start(f32[2,128,32,128]{3,2,1,0:T(8,128)} %slice_bitcast_fusion.u0), channel_id=1, source_target_pairs={{0,16},{4,20},{8,24},{12,28},{16,0},{20,4},{24,8},{28,12},{1,17},{... | collective-permute-start | bytes 12582920 | tf_op jit(solution)/shard_map/ppermute | solution.py:33
  212.1 147.1 %collective-permute-start.4 = (f32[2,32,128,128]{3,2,1,0:T(8,128)}, f32[2,32,128,128]{3,2,1,0:T(8,128)}, u32[]{:S(2)}, u32[]{:S(2)}) collective-permute-start(f32[2,32,128,128]{3,2,1,0:T(8,128)} %place_rows.1.refs_0_), channel_id=1, source_target_pairs={{0,8},{4,12},{8,0},{12,4},{1,9},{5,13},{9,1},{13,5},{2,10},{6,14},... | collective-permute-start | bytes 12582920 | tf_op jit(solution)/shard_map/ppermute | solution.py:33
  212.4 127.3 %collective-permute-start.3 = (f32[27,128,128]{2,1,0:T(8,128)}, f32[27,128,128]{2,1,0:T(8,128)S(1)}, u32[]{:S(2)}, u32[]{:S(2)}) collective-permute-start(f32[27,128,128]{2,1,0:T(8,128)} %pack_lower.6), channel_id=1, source_target_pairs={{0,16},{4,20},{8,24},{12,28},{16,0},{20,4},{24,8},{28,12},{1,17},{... | collective-permute-start | bytes 5308424 | tf_op jit(solution)/shard_map/ppermute | solution.py:33
  214.1 145.0 %collective-permute-start.5 = (f32[23,128,128]{2,1,0:T(8,128)}, f32[23,128,128]{2,1,0:T(8,128)S(1)}, u32[]{:S(2)}, u32[]{:S(2)}) collective-permute-start(f32[23,128,128]{2,1,0:T(8,128)} %pack_lower.7), channel_id=1, source_target_pairs={{0,16},{4,20},{8,24},{12,28},{16,0},{20,4},{24,8},{28,12},{1,17},{... | collective-permute-start | bytes 4521992 | tf_op jit(solution)/shard_map/ppermute | solution.py:33
  214.4 144.8 %collective-permute-start.6 = (f32[19,128,128]{2,1,0:T(8,128)}, f32[19,128,128]{2,1,0:T(8,128)}, u32[]{:S(2)}, u32[]{:S(2)}) collective-permute-start(f32[19,128,128]{2,1,0:T(8,128)} %pack_lower.8), channel_id=1, source_target_pairs={{0,16},{4,20},{8,24},{12,28},{16,0},{20,4},{24,8},{28,12},{1,17},{... | collective-permute-start | bytes 3735560 | tf_op jit(solution)/shard_map/ppermute | solution.py:33
  216.2 123.6 %collective-permute-start.1 = (f32[15,128,128]{2,1,0:T(8,128)}, f32[15,128,128]{2,1,0:T(8,128)}, u32[]{:S(2)}, u32[]{:S(2)}) collective-permute-start(f32[15,128,128]{2,1,0:T(8,128)} %pack_lower.5), channel_id=1, source_target_pairs={{0,16},{4,20},{8,24},{12,28},{16,0},{20,4},{24,8},{28,12},{1,17},{... | collective-permute-start | bytes 2949128 | tf_op jit(solution)/shard_map/ppermute | solution.py:33
  339.7 54.5 %copy-start.2 = (f32[27,128,128]{2,1,0:T(8,128)}, f32[27,128,128]{2,1,0:T(8,128)S(1)}, u32[]{:S(2)}) copy-start(f32[27,128,128]{2,1,0:T(8,128)S(1)} %collective-permute-done.3.refs_5_.refs_6_.refs_12_.refs_13_.refs_14_.refs_15_) | copy-start | bytes 5308420
  359.2 133.6 %copy-start.3 = (f32[23,128,128]{2,1,0:T(8,128)}, f32[23,128,128]{2,1,0:T(8,128)S(1)}, u32[]{:S(2)}) copy-start(f32[23,128,128]{2,1,0:T(8,128)S(1)} %collective-permute-done.5.refs_7_.refs_8_.refs_20_.refs_21_.refs_22_.refs_23_) | copy-start | bytes 4521988
  366.6 126.1 %collective-permute-start.7 = (f32[4,32,128,128]{3,2,1,0:T(8,128)}, f32[4,32,128,128]{3,2,1,0:T(8,128)S(1)}, u32[]{:S(2)}, u32[]{:S(2)}) collective-permute-start(f32[4,32,128,128]{3,2,1,0:T(8,128)} %pad_maximum_fusion), channel_id=1, source_target_pairs={{0,4},{4,0},{8,12},{12,8},{1,5},{5,1},{9,13},{13,9},{2,6},{6,2},{1... | collective-permute-start | bytes 25165832 | tf_op jit(solution)/shard_map/ppermute | solution.py:33
  382.4 288.6 %collective-permute-start.12 = (f32[5,15,128,128]{3,2,1,0:T(8,128)}, f32[5,15,128,128]{3,2,1,0:T(8,128)}, u32[]{:S(2)}, u32[]{:S(2)}) collective-permute-start(f32[5,15,128,128]{3,2,1,0:T(8,128)} %slice.1042), channel_id=1, source_target_pairs={{0,16},{4,20},{8,24},{12,28},{16,0},{20,4},{24,8},{28,12},{1,17},{... | collective-permute-start | bytes 14745608 | tf_op jit(solution)/shard_map/ppermute | solution.py:33
  388.2 103.6 %collective-permute-start.8 = (f32[15,128,128]{2,1,0:T(8,128)}, f32[15,128,128]{2,1,0:T(8,128)S(1)}, u32[]{:S(2)}, u32[]{:S(2)}) collective-permute-start(f32[15,128,128]{2,1,0:T(8,128)} %collective-permute-done.1.refs_4_.refs_5_.refs_6_.refs_7_), channel_id=1, source_target_pairs={{1,4},{2,8},{3,12},{4,1},{6,9},{7,13},{8,2},{9,6},{11,14},{12,3},{... | collective-permute-start | bytes 2949128 | tf_op jit(solution)/shard_map/ppermute | solution.py:781
  394.2 191.7 %collective-permute-start.9 = (f32[27,128,128]{2,1,0:T(8,128)S(1)}, f32[27,128,128]{2,1,0:T(8,128)S(1)}, u32[]{:S(2)}, u32[]{:S(2)}) collective-permute-start(f32[27,128,128]{2,1,0:T(8,128)S(1)} %collective-permute-done.3.refs_5_.refs_6_.refs_12_.refs_13_.refs_14_.refs_15_), channel_id=1, source_target_pairs={{1,4},{2,8},{3,12},{4,1},{6,9},{7,13},{8,2},{9,6},{11,14},{12,3},{... | collective-permute-start | bytes 5308424 | tf_op jit(solution)/shard_map/ppermute | solution.py:781
  397.0 253.2 %collective-permute-start.11 = (f32[36,128,128]{2,1,0:T(8,128)}, f32[36,128,128]{2,1,0:T(8,128)}, u32[]{:S(2)}, u32[]{:S(2)}) collective-permute-start(f32[36,128,128]{2,1,0:T(8,128)} %pack_lower.9), channel_id=1, source_target_pairs={{0,16},{4,20},{8,24},{12,28},{16,0},{20,4},{24,8},{28,12},{1,17},{... | collective-permute-start | bytes 7077896 | tf_op jit(solution)/shard_map/ppermute | solution.py:33
  397.8 99.6 %copy-start.102 = (pred[4,15]{1,0:T(4,128)(4,1)S(1)}, pred[4,15]{1,0:T(4,128)(4,1)}, u32[]{:S(2)}) copy-start(pred[4,15]{1,0:T(4,128)(4,1)} %constant.397.clone) | copy-start | bytes 184
  397.8 99.6 %copy-start.103 = (pred[4,15]{1,0:T(4,128)(4,1)S(1)}, pred[4,15]{1,0:T(4,128)(4,1)}, u32[]{:S(2)}) copy-start(pred[4,15]{1,0:T(4,128)(4,1)} %constant.399.clone) | copy-start | bytes 184
  491.8 210.4 %collective-permute-start.13 = (f32[3,15,128,128]{3,2,1,0:T(8,128)}, f32[3,15,128,128]{3,2,1,0:T(8,128)}, u32[]{:S(2)}, u32[]{:S(2)}) collective-permute-start(f32[3,15,128,128]{3,2,1,0:T(8,128)} %get-tuple-element.65), channel_id=1, source_target_pairs={{0,16},{4,20},{8,24},{12,28},{16,0},{20,4},{24,8},{28,12},{1,17},{... | collective-permute-start | bytes 8847368 | tf_op jit(solution)/shard_map/ppermute | solution.py:33
  492.8 161.8 %collective-permute-start.10 = (f32[23,128,128]{2,1,0:T(8,128)S(1)}, f32[23,128,128]{2,1,0:T(8,128)S(1)}, u32[]{:S(2)}, u32[]{:S(2)}) collective-permute-start(f32[23,128,128]{2,1,0:T(8,128)S(1)} %collective-permute-done.5.refs_7_.refs_8_.refs_20_.refs_21_.refs_22_.refs_23_), channel_id=1, source_target_pairs={{1,4},{2,8},{3,12},{4,1},{6,9},{7,13},{8,2},{9,6},{11,14},{12,3},{... | collective-permute-start | bytes 4521992 | tf_op jit(solution)/shard_map/ppermute | solution.py:808
  585.9 63.7 %copy-start.13 = (s32[32,1,128]{2,1,0:T(1,128)S(1)}, s32[32,1,128]{2,1,0:T(1,128)}, u32[]{:S(2)}) copy-start(s32[32,1,128]{2,1,0:T(1,128)} %constant_dynamic-slice_fusion.3) | copy-start | bytes 49156
  585.9 61.5 %copy-start.6 = (f32[27,128,128]{2,1,0:T(8,128)}, f32[27,128,128]{2,1,0:T(8,128)S(1)}, u32[]{:S(2)}) copy-start(f32[27,128,128]{2,1,0:T(8,128)S(1)} %collective-permute-done.9.refs_8_.refs_9_.refs_10_.refs_11_) | copy-start | bytes 5308420
  647.4 125.9 %collective-permute-start.15 = (f32[3,15,128,128]{3,2,1,0:T(8,128)}, f32[3,15,128,128]{3,2,1,0:T(8,128)}, u32[]{:S(2)}, u32[]{:S(2)}) collective-permute-start(f32[3,15,128,128]{3,2,1,0:T(8,128)} %get-tuple-element.67), channel_id=1, source_target_pairs={{0,16},{4,20},{8,24},{12,28},{16,0},{20,4},{24,8},{28,12},{1,17},{... | collective-permute-start | bytes 8847368 | tf_op jit(solution)/shard_map/ppermute | solution.py:33
  650.2 72.9 %collective-permute-start.14 = (f32[19,128,128]{2,1,0:T(8,128)}, f32[19,128,128]{2,1,0:T(8,128)}, u32[]{:S(2)}, u32[]{:S(2)}) collective-permute-start(f32[19,128,128]{2,1,0:T(8,128)} %collective-permute-done.6.refs_9_.refs_10_.refs_4_.refs_5_.refs_6_.refs_7_), channel_id=1, source_target_pairs={{1,4},{2,8},{3,12},{4,1},{6,9},{7,13},{8,2},{9,6},{11,14},{12,3},{... | collective-permute-start | bytes 3735560 | tf_op jit(solution)/shard_map/ppermute | solution.py:808
  654.5 163.8 %collective-permute-start.18 = (f32[36,128,128]{2,1,0:T(8,128)}, f32[36,128,128]{2,1,0:T(8,128)}, u32[]{:S(2)}, u32[]{:S(2)}) collective-permute-start(f32[36,128,128]{2,1,0:T(8,128)} %collective-permute-done.11.refs_11_.refs_12_.refs_13_.refs_14_.refs_15_), channel_id=1, source_target_pairs={{1,4},{2,8},{3,12},{4,1},{6,9},{7,13},{8,2},{9,6},{11,14},{12,3},{... | collective-permute-start | bytes 7077896 | tf_op jit(solution)/shard_map/ppermute | solution.py:834
  670.9 122.8 %collective-permute-start.16 = (f32[2,15,128,128]{3,2,1,0:T(8,128)}, f32[2,15,128,128]{3,2,1,0:T(8,128)S(1)}, u32[]{:S(2)}, u32[]{:S(2)}) collective-permute-start(f32[2,15,128,128]{3,2,1,0:T(8,128)} %slice.1045), channel_id=1, source_target_pairs={{0,16},{4,20},{8,24},{12,28},{16,0},{20,4},{24,8},{28,12},{1,17},{... | collective-permute-start | bytes 5898248 | tf_op jit(solution)/shard_map/ppermute | solution.py:33
  702.4 29.5 %copy-start.49 = (s32[17]{0:T(128)S(1)}, s32[17]{0:T(128)}, u32[]{:S(2)}) copy-start(s32[17]{0:T(128)} %get-tuple-element.99) | copy-start | bytes 208
  702.4 29.5 %copy-start.50 = (s32[17]{0:T(128)S(1)}, s32[17]{0:T(128)}, u32[]{:S(2)}) copy-start(s32[17]{0:T(128)} %get-tuple-element.100) | copy-start | bytes 208
  702.4 29.5 %copy-start.51 = (s32[17]{0:T(128)S(1)}, s32[17]{0:T(128)}, u32[]{:S(2)}) copy-start(s32[17]{0:T(128)} %get-tuple-element.101) | copy-start | bytes 208
  702.4 29.5 %copy-start.52 = (s32[17]{0:T(128)S(1)}, s32[17]{0:T(128)}, u32[]{:S(2)}) copy-start(s32[17]{0:T(128)} %get-tuple-element.102) | copy-start | bytes 208
  702.4 29.5 %copy-start.53 = (s32[17]{0:T(128)S(1)}, s32[17]{0:T(128)}, u32[]{:S(2)}) copy-start(s32[17]{0:T(128)} %get-tuple-element.103) | copy-start | bytes 208
  702.4 29.5 %copy-start.54 = (s32[17]{0:T(128)S(1)}, s32[17]{0:T(128)}, u32[]{:S(2)}) copy-start(s32[17]{0:T(128)} %get-tuple-element.104) | copy-start | bytes 208
  702.4 29.5 %copy-start.55 = (s32[17]{0:T(128)S(1)}, s32[17]{0:T(128)}, u32[]{:S(2)}) copy-start(s32[17]{0:T(128)} %get-tuple-element.105) | copy-start | bytes 208
  702.4 29.5 %copy-start.56 = (s32[17]{0:T(128)S(1)}, s32[17]{0:T(128)}, u32[]{:S(2)}) copy-start(s32[17]{0:T(128)} %get-tuple-element.106) | copy-start | bytes 208
  702.4 29.5 %copy-start.57 = (s32[17]{0:T(128)S(1)}, s32[17]{0:T(128)}, u32[]{:S(2)}) copy-start(s32[17]{0:T(128)} %get-tuple-element.107) | copy-start | bytes 208
  702.5 29.5 %copy-start.58 = (s32[17]{0:T(128)S(1)}, s32[17]{0:T(128)}, u32[]{:S(2)}) copy-start(s32[17]{0:T(128)} %get-tuple-element.108) | copy-start | bytes 208
  702.5 29.5 %copy-start.59 = (s32[17]{0:T(128)S(1)}, s32[17]{0:T(128)}, u32[]{:S(2)}) copy-start(s32[17]{0:T(128)} %get-tuple-element.109) | copy-start | bytes 208
  702.5 30.9 %copy-start.41 = (s32[17]{0:T(128)S(1)}, s32[17]{0:T(128)}, u32[]{:S(2)}) copy-start(s32[17]{0:T(128)} %get-tuple-element.135) | copy-start | bytes 208
  702.5 30.9 %copy-start.42 = (s32[17]{0:T(128)S(1)}, s32[17]{0:T(128)}, u32[]{:S(2)}) copy-start(s32[17]{0:T(128)} %get-tuple-element.136) | copy-start | bytes 208
  702.5 30.9 %copy-start.43 = (s32[17]{0:T(128)S(1)}, s32[17]{0:T(128)}, u32[]{:S(2)}) copy-start(s32[17]{0:T(128)} %get-tuple-element.137) | copy-start | bytes 208
  702.5 30.9 %copy-start.44 = (s32[17]{0:T(128)S(1)}, s32[17]{0:T(128)}, u32[]{:S(2)}) copy-start(s32[17]{0:T(128)} %get-tuple-element.138) | copy-start | bytes 208
  702.5 30.9 %copy-start.45 = (s32[17]{0:T(128)S(1)}, s32[17]{0:T(128)}, u32[]{:S(2)}) copy-start(s32[17]{0:T(128)} %get-tuple-element.141) | copy-start | bytes 208
  702.5 30.9 %copy-start.46 = (s32[17]{0:T(128)S(1)}, s32[17]{0:T(128)}, u32[]{:S(2)}) copy-start(s32[17]{0:T(128)} %get-tuple-element.142) | copy-start | bytes 208
  702.5 30.9 %copy-start.47 = (s32[17]{0:T(128)S(1)}, s32[17]{0:T(128)}, u32[]{:S(2)}) copy-start(s32[17]{0:T(128)} %get-tuple-element.143) | copy-start | bytes 208
  702.6 30.9 %copy-start.48 = (s32[17]{0:T(128)S(1)}, s32[17]{0:T(128)}, u32[]{:S(2)}) copy-start(s32[17]{0:T(128)} %get-tuple-element.144) | copy-start | bytes 208
  721.1 88.5 %collective-permute-start.17 = (f32[1,15,128,128]{3,2,1,0:T(8,128)}, f32[1,15,128,128]{3,2,1,0:T(8,128)}, u32[]{:S(2)}, u32[]{:S(2)}) collective-permute-start(f32[1,15,128,128]{3,2,1,0:T(8,128)} %get-tuple-element.69), channel_id=1, source_target_pairs={{0,16},{4,20},{8,24},{12,28},{16,0},{20,4},{24,8},{28,12},{1,17},{... | collective-permute-start | bytes 2949128 | tf_op jit(solution)/shard_map/ppermute | solution.py:33
  723.2 123.9 %collective-permute-start.19 = (f32[1,15,128,128]{3,2,1,0:T(8,128)}, f32[1,15,128,128]{3,2,1,0:T(8,128)S(1)}, u32[]{:S(2)}, u32[]{:S(2)}) collective-permute-start(f32[1,15,128,128]{3,2,1,0:T(8,128)} %get-tuple-element.70), channel_id=1, source_target_pairs={{0,16},{4,20},{8,24},{12,28},{16,0},{20,4},{24,8},{28,12},{1,17},{... | collective-permute-start | bytes 2949128 | tf_op jit(solution)/shard_map/ppermute | solution.py:33
  (78 other events, 1184.9 us)
Sparse Core Ops, SparseCore 0:
  83.4 72.2 all-gather.4
  157.3 149.7 all-gather.2

commit v4 on v3

--- a/solution.py
+++ b/solution.py
@@ -305,25 +305,15 @@
             top, end = s * tile, (s + 1) * tile
             block[...] = m[top:end, top:end]
             inverse = eliminate(block)
+            strip = dot_full(inverse, m[top:end, :], ((1,), (0,)))
+            pieces = [strip[:, :top]] if top > 0 else []
+            pieces += [inverse] + ([strip[:, end:]] if end < order else [])
+            strip = jnp.concatenate(pieces, axis=1)
             if end < order:
-                right = dot_full(inverse, m[top:end, end:], ((1,), (0,)))
-                for t in range(s + 1, steps):
-                    left = right[:, t * tile - end : (t + 1) * tile - end]
-                    span = slice(t * tile, (t + 1) * tile)
-                    m[span, t * tile :] -= dot_full(
-                        left, right[:, t * tile - end :], ((0,), (0,))
-                    )
-                    m[span, top:end] = -dot_full(left, inverse, ((0,), (0,)))
-            m[top:end, top:end] = inverse
-            if s > 0:
-                done = dot_full(inverse, m[top:end, :top], ((1,), (0,)))
-                m[top:end, :top] = done
-                for t in range(s + 1, steps):
-                    span = slice(t * tile, (t + 1) * tile)
-                    left = right[:, t * tile - end : (t + 1) * tile - end]
-                    m[span, :top] -= dot_full(left, done, ((0,), (0,)))
-            if end < order:
+                m[end:, top:end] = jnp.zeros((order - end, tile), F32)
+                m[end:, :] -= dot_full(strip[:, end:], strip, ((0,), (0,)))
                 m[top:end, end:] = jnp.zeros((tile, order - end), F32)
+            m[top:end, :end] = strip[:, :end]
         head, tail = split(m[...])
         high[...] = head
         low[...] = tail
@@ -804,10 +794,7 @@
         first = pivot_came
     right_h, right_l = solve_columns(parts, jnp.concatenate(homes), high, low)
     if mirrored:
-        turned[0] = after(turned[0], left_h)
         turned += [lax.ppermute(part, ("row", "col"), pairs) for part in lower[2:4]]
-        send(1, turned[0])
-        right_h = after(right_h, turned[0])
 
     front = None
     groups = cols // SUB
@@ -826,10 +813,14 @@
             end,
         )
         if mirrored:
-            if start > 0:
+            if start == 0:
+                turned[0] = after(turned[0], front)
+                send(1, turned[0])
+                front = after(front, turned[0])
+            else:
                 send(2, front)
                 lower[4] = after(lower[4], front)
-            front = after(front, turned[1]) if start == 0 else after(front, turned[2], lower[4])
+                front = after(front, turned[1], turned[2], lower[4])
     if mirrored:
         turned.append(lax.ppermute(lower[4], ("row", "col"), pairs))
     front = add_first(front, first, other_rows[:1], trailing_cols)

time: 875 us -> 845 us (0.966)
  waiting for transfers between devices: 141 us -> 118 us
  local copies, waits for them, and re-layouts: 84.6 us -> 73.1 us
    ppermute x2, waiting for transfers between devices: 88 us -> 66.2 us  [on_device(): turned = [lax.ppermute(part, ('row', 'col'), pairs) for part in lower[:2]]]
  transfers between devices with their start and end apart: 22 -> 22, of which waited for: 3 -> 3; matrix products, arithmetic and copies ran while one was open for 10% -> 10% of each run, Pallas kernels for 64% -> 67%
where the time goes in v4:
time: 845 us; the launch traced here: 833 us
  Pallas kernels  571 us (68%)
  waiting for transfers between devices  118 us (14%)
  local copies, waits for them, and re-layouts  73.1 us (9%)
  starting transfers between devices  31.8 us (4%)
  between operations  15.3 us (2%)
  other arithmetic  14.6 us (2%)
  matrix products  8.81 us (1%)
    pallas_call x8, Pallas kernels, add_tiles(): pl.pallas_call(kernel, grid_spec=pltpu.PrefetchScalarGridSpec(num_scalar_...  165 us
    pallas_call x2, Pallas kernels, own_part(): pl.pallas_call(kernel, grid_spec=pltpu.PrefetchScalarGridSpec(num_scalar_...  124 us
    pallas_call x1, Pallas kernels, inverse_factor(): pl.pallas_call(kernel, in_specs=[pl.BlockSpec(memory_space=pltpu.VMEM)],...  114 us
    ppermute x2, waiting for transfers between devices, on_device(): turned = [lax.ppermute(part, ('row', 'col'), pairs) for part in lower[:2]]  66.2 us
    pallas_call x5, Pallas kernels, pack_lower(): pl.pallas_call(kernel, grid_spec=pltpu.PrefetchScalarGridSpec(num_scalar_...  64.8 us
    ppermute x15, waiting for transfers between devices, swapped(): return lax.ppermute(value, axis, pairs)  52.2 us
    pallas_call x1, Pallas kernels, solve_columns(): pl.pallas_call(kernel, grid_spec=pltpu.PrefetchScalarGridSpec(num_scalar_...  25.9 us
    pallas_call x1, Pallas kernels, pack_cross(): pl.pallas_call(kernel, grid_spec=pltpu.PrefetchScalarGridSpec(num_scalar_...  25.1 us
  transfers between devices with their start and end apart: 22, of which 3 were waited for; matrix products, arithmetic and copies ran while one was open for 10% of the time, Pallas kernels for 67%

profile of v4, /device:TPU:6, one launch (start us, length us, event | category | flops | bytes accessed | tf_op | source)
XLA Modules:
  0.0 832.8 jit_solution(14269560513938140580)
XLA Ops:
  6.5 5.3 pack_panel.2
  12.4 14.9 %pack_lower.6 = f32[27,128,128]{2,1,0:T(8,128)} custom-call(s32[1]{0:T(128)S(6)} %sub.93.half_ref.parity_ref, s32[1]{0:T(128)S(6)} %sub.93.half_ref.parity_ref, f32[1,2,16,128,32,128]{5,4,3,2,1,0:T(8,128)} %refs_1_.1), custom_call_target="tpu_custom_call" | custom-call | bytes 311296 | tf_op jit(solution)/shard_map/pack_lower/pallas_call | solution.py:144
  27.3 12.9 %pack_lower.7 = f32[23,128,128]{2,1,0:T(8,128)} custom-call(s32[1]{0:T(128)S(6)} %sub.93.half_ref.parity_ref, s32[1]{0:T(128)S(6)} %sub.93.half_ref.parity_ref, f32[1,2,16,128,32,128]{5,4,3,2,1,0:T(8,128)} %refs_1_.1), custom_call_target="tpu_custom_call" | custom-call | bytes 266731 | tf_op jit(solution)/shard_map/pack_lower/pallas_call | solution.py:144
  40.3 15.3 %pack_lower.5 = f32[15,128,128]{2,1,0:T(8,128)} custom-call(s32[1]{0:T(128)S(6)} %sub.93.half_ref.parity_ref, s32[1]{0:T(128)S(6)} %sub.93.half_ref.parity_ref, f32[1,2,16,128,32,128]{5,4,3,2,1,0:T(8,128)} %refs_1_.1), custom_call_target="tpu_custom_call" | custom-call | bytes 324403 | tf_op jit(solution)/shard_map/pack_lower/pallas_call | solution.py:144
  55.6 5.3 pack_panel.3
  61.1 4.4 select_reduce_fusion
  66.4 3.6 fusion.6
  70.0 4.6 slice_bitcast_fusion.u0
  74.7 2.2 fusion.2
  80.8 2.4 copy.198
  83.2 3.9 reshape.256
  88.7 10.5 %pack_lower.9 = f32[36,128,128]{2,1,0:T(8,128)} custom-call(s32[1]{0:T(128)S(6)} %sub.93.half_ref.parity_ref, s32[1]{0:T(128)S(6)} %sub.93.half_ref.parity_ref, f32[1,2,16,128,32,128]{5,4,3,2,1,0:T(8,128)} %refs_1_.1), custom_call_target="tpu_custom_call" | custom-call | bytes 191365 | tf_op jit(solution)/shard_map/pack_lower/pallas_call | solution.py:144
  99.2 11.1 %pack_lower.8 = f32[19,128,128]{2,1,0:T(8,128)} custom-call(s32[1]{0:T(128)S(6)} %sub.93.half_ref.parity_ref, s32[1]{0:T(128)S(6)} %sub.93.half_ref.parity_ref, f32[1,2,16,128,32,128]{5,4,3,2,1,0:T(8,128)} %refs_1_.1), custom_call_target="tpu_custom_call" | custom-call | bytes 222167 | tf_op jit(solution)/shard_map/pack_lower/pallas_call | solution.py:144
  114.3 25.1 %pack_cross.1 = f32[15,15,128,128]{3,2,1,0:T(8,128)} custom-call(s32[1]{0:T(128)S(6)} %sub.93.half_ref.parity_ref, s32[1]{0:T(128)} %bitcast.151.half_ref.parity_ref, f32[1,2,16,128,32,128]{5,4,3,2,1,0:T(8,128)} %refs_1_.1), custom_call_target="tpu_custom_call" | custom-call | bytes 503316 | tf_op jit(solution)/shard_map/pack_cross/pallas_call | solution.py:102
  139.4 52.2 %collective-permute-done.2.u1 = f32[2,128,32,128]{3,2,1,0:T(8,128)} collective-permute-done((f32[2,128,32,128]{3,2,1,0:T(8,128)}, f32[2,128,32,128]{3,2,1,0:T(8,128)}, u32[]{:S(2)}, u32[]{:S(2)}) %collective-permute-start.2) | collective-permute-done | bytes 4194336 | tf_op jit(solution)/shard_map/ppermute | solution.py:33
  191.7 15.7 %place_rows.1.refs_0_ = f32[2,32,128,128]{3,2,1,0:T(8,128)} custom-call(s32[2,128]{1,0:T(2,128)} %bitcast.399, s32[2,128]{1,0:T(2,128)} %bitcast.400, s32[2]{0:T(128)} %compare_select_fusion.2.where_ref, f32[2,128,32,128]{3,2,1,0:T(8,128)} %slice_bitcast_fusion.u0, f32[2,128,32,128]{3,2,1,0:T(8,128)} %collective-permute-done.2.u1, s32[32,128]{1,0:T(8,128)} %bitcast.378, ...), custom_call_target="tpu_custom_call" | custom-call | bytes 125829 | tf_op jit(solution)/shard_map/place_rows/pallas_call | solution.py:233
  207.6 1.7 collective-permute-start.3
  209.7 1.7 collective-permute-start.6
  212.0 5.2 copy.187
  217.2 5.5 reshape.229.a
  222.7 113.5 %inverse_factor.1 = (bf16[1024,1024]{1,0:T(8,128)(2,1)}, bf16[1024,1024]{1,0:T(8,128)(2,1)}) custom-call(f32[1024,1024]{1,0:T(8,128)} %reshape.229.a), custom_call_target="tpu_custom_call" | custom-call | flops 1000000000 | bytes 83886 | tf_op jit(solution)/shard_map/inverse_factor/pallas_call | solution.py:321
  336.3 19.6 %solve_rows.1 = (bf16[2048,1024]{1,0:T(8,128)(2,1)}, bf16[2048,1024]{1,0:T(8,128)(2,1)}, f32[2,2048,128]{2,1,0:T(8,128)}) custom-call(s32[1]{0:T(128)} %bitcast.159.me, f32[4,2048,256]{2,1,0:T(8,128)} %all-gather.3.cloned.1.call-done.f, bf16[1024,1024]{1,0:T(8,128)(2,1)} %get-tuple-element.43.h.refs_3_, bf16[1024,1024]{1,0:T(8,128)(2,1)} %get-tuple-element.48.l.refs_4_), custom_call_target="tpu_custom_call" | custom-call | flops 128849016 | bytes 167772 | tf_op jit(solution)/shard_map/solve_rows/pallas_call | solution.py:358
  356.2 7.2 pad_maximum_fusion
  372.8 5.2 slice.1042
  378.0 1.8 collective-permute-start.12
  383.7 5.7 collective-permute-start.8
  391.2 5.9 fusion.30
  397.1 1.9 collective-permute-start.10
  399.1 5.7 collective-permute-start.9
  404.8 25.9 %solve_columns.1 = (bf16[1024,4096]{1,0:T(8,128)(2,1)}, bf16[1024,4096]{1,0:T(8,128)(2,1)}) custom-call(s32[8]{0:T(128)} %pad_add_fusion.home, f32[2,32,128,128]{3,2,1,0:T(8,128)} %place_rows.1.refs_0_, f32[2,32,128,128]{3,2,1,0:T(8,128)} %collective-permute-done.4.refs_1_, f32[4,32,128,128]{3,2,1,0:T(8,128)} %collective-permute-done.7.refs_2_, ...), custom_call_target="tpu_custom_call" | custom-call | flops 171798688 | bytes 335544 | tf_op jit(solution)/shard_map/solve_columns/pallas_call | solution.py:408
  430.7 62.3 %own_part.2.refs_0_ = f32[1,16,128,32,128]{4,3,2,1,0:T(8,128)} custom-call(s32[1]{0:T(128)} %bitcast.151.half_ref.parity_ref, s32[16,128]{1,0:T(8,128)} %bitcast.386, s32[16]{0:T(128)} %copy-done.25, f32[1,2,16,128,32,128]{5,4,3,2,1,0:T(8,128)} %refs_1_.1, s32[32,128]{1,0:T(8,128)} %bitcast.379, f32[16,1,128]{2,1,0:T(1,128)} %bitcast.383, ...), custom_call_target="tpu_custom_call" | custom-call | flops 515396064 | bytes 671088 | tf_op jit(solution)/shard_map/own_part/pallas_call | solution.py:478
  493.1 10.5 %collective-permute-done.8.refs_0_.refs_1_.refs_2_.refs_3_ = f32[15,128,128]{2,1,0:T(8,128)S(1)} collective-permute-done((f32[15,128,128]{2,1,0:T(8,128)}, f32[15,128,128]{2,1,0:T(8,128)S(1)}, u32[]{:S(2)}, u32[]{:S(2)}) %collective-permute-start.8) | collective-permute-done | bytes 983072 | tf_op jit(solution)/shard_map/ppermute | solution.py:771
  505.3 61.6 %own_part.3.before = f32[1,16,128,32,128]{4,3,2,1,0:T(8,128)} custom-call(s32[1]{0:T(128)} %bitcast.151.half_ref.parity_ref, s32[16,128]{1,0:T(8,128)} %bitcast.387, s32[16]{0:T(128)} %copy-done.25, f32[1,16,128,32,128]{4,3,2,1,0:T(8,128)} %own_part.2.refs_0_, f32[1,2,16,128,32,128]{5,4,3,2,1,0:T(8,128)} %refs_1_.1, ...), custom_call_target="tpu_custom_call", output_to_operand_aliasing={{}: (3, {})} | custom-call | flops 515396064 | bytes 671088 | tf_op jit(solution)/shard_map/own_part/pallas_call | solution.py:478
  568.1 1.9 collective-permute-start.14
  570.0 55.7 %collective-permute-done.9.refs_8_.refs_9_.refs_10_.refs_11_ = f32[27,128,128]{2,1,0:T(8,128)S(1)} collective-permute-done((f32[27,128,128]{2,1,0:T(8,128)S(1)}, f32[27,128,128]{2,1,0:T(8,128)S(1)}, u32[]{:S(2)}, u32[]{:S(2)}) %collective-permute-start.9) | collective-permute-done | bytes 1769504 | tf_op jit(solution)/shard_map/ppermute | solution.py:771
  625.7 1.9 collective-permute-start.18
  628.2 3.0 slice.1045
  631.2 3.1 constant_dynamic-slice_fusion.9.u
  634.3 6.2 add_first.1.before
  643.5 3.0 fusion.29
  646.5 26.3 %add_tiles.8.before = f32[1,16,128,32,128]{4,3,2,1,0:T(8,128)} custom-call(s32[16,128]{1,0:T(8,128)} %bitcast.368, s32[40]{0:T(128)} %constant.342.clone.order_ref, s32[180]{0:T(256)} %constant.559.picks_ref, s32[180]{0:T(256)} %concatenate.69.stands_ref, f32[1,16,128,32,128]{4,3,2,1,0:T(8,128)} %add_first.1.before, ...), custom_call_target="tpu_custom_call", output_to_operand_aliasing={{}: (4, {})} | custom-call | bytes 314572 | tf_op jit(solution)/shard_map/add_tiles/pallas_call | solution.py:589
  673.7 18.6 %add_tiles.9.before = f32[1,16,128,32,128]{4,3,2,1,0:T(8,128)} custom-call(s32[16,128]{1,0:T(8,128)} %bitcast.369, s32[24]{0:T(128)} %constant.355.clone.order_ref, s32[144]{0:T(256)} %constant.540.picks_ref, s32[144]{0:T(256)} %concatenate.67.stands_ref, f32[1,16,128,32,128]{4,3,2,1,0:T(8,128)} %add_tiles.8.before, ...), custom_call_target="tpu_custom_call", output_to_operand_aliasing={{}: (4, {})} | custom-call | bytes 188743 | tf_op jit(solution)/shard_map/add_tiles/pallas_call | solution.py:589
  703.8 39.1 %add_tiles.10.before = f32[1,16,128,32,128]{4,3,2,1,0:T(8,128)} custom-call(s32[16,128]{1,0:T(8,128)} %bitcast.370, s32[34]{0:T(128)} %constant.362.clone.order_ref, s32[408]{0:T(512)} %concatenate.64.picks_ref, s32[408]{0:T(512)} %concatenate.65.stands_ref, f32[1,16,128,32,128]{4,3,2,1,0:T(8,128)} %add_tiles.9.before, ...), custom_call_target="tpu_custom_call", output_to_operand_aliasing={{}: (4, {})} | custom-call | bytes 267386 | tf_op jit(solution)/shard_map/add_tiles/pallas_call | solution.py:589
  742.8 20.4 %add_tiles.11.before = f32[1,16,128,32,128]{4,3,2,1,0:T(8,128)} custom-call(s32[16,128]{1,0:T(8,128)} %bitcast.371, s32[24]{0:T(128)} %constant.370.clone.order_ref, s32[180]{0:T(256)} %constant.525.picks_ref, s32[180]{0:T(256)} %concatenate.63.stands_ref, f32[1,16,128,32,128]{4,3,2,1,0:T(8,128)} %add_tiles.10.before, ...), custom_call_target="tpu_custom_call", output_to_operand_aliasing={{}: (4, {})} | custom-call | bytes 188743 | tf_op jit(solution)/shard_map/add_tiles/pallas_call | solution.py:589
  764.5 14.7 %add_tiles.12.before = f32[1,16,128,32,128]{4,3,2,1,0:T(8,128)} custom-call(s32[16,128]{1,0:T(8,128)} %bitcast.372, s32[16]{0:T(128)} %constant.383.clone.order_ref, s32[120]{0:T(128)} %constant.494.picks_ref, s32[120]{0:T(128)} %concatenate.61.stands_ref, f32[1,16,128,32,128]{4,3,2,1,0:T(8,128)} %add_tiles.11.before, ...), custom_call_target="tpu_custom_call", output_to_operand_aliasing={{}: (4, {})} | custom-call | bytes 125829 | tf_op jit(solution)/shard_map/add_tiles/pallas_call | solution.py:589
  779.2 8.8 %add_tiles.13.before = f32[1,16,128,32,128]{4,3,2,1,0:T(8,128)} custom-call(s32[16,128]{1,0:T(8,128)} %bitcast.373, s32[8]{0:T(128)} %constant.396.clone.order_ref, s32[60]{0:T(128)} %constant.463.picks_ref, s32[60]{0:T(128)} %concatenate.59.stands_ref, f32[1,16,128,32,128]{4,3,2,1,0:T(8,128)} %add_tiles.12.before, ...), custom_call_target="tpu_custom_call", output_to_operand_aliasing={{}: (4, {})} | custom-call | bytes 62914 | tf_op jit(solution)/shard_map/add_tiles/pallas_call | solution.py:589
  788.0 28.6 %add_tiles.14.before = f32[1,16,128,32,128]{4,3,2,1,0:T(8,128)} custom-call(s32[16,128]{1,0:T(8,128)} %bitcast.374, s32[30]{0:T(128)} %constant.401.clone.order_ref, s32[240]{0:T(256)} %concatenate.56.picks_ref, s32[240]{0:T(256)} %concatenate.57.stands_ref, f32[1,16,128,32,128]{4,3,2,1,0:T(8,128)} %add_tiles.13.before, ...), custom_call_target="tpu_custom_call", output_to_operand_aliasing={{}: (4, {})} | custom-call | bytes 235929 | tf_op jit(solution)/shard_map/add_tiles/pallas_call | solution.py:589
  816.6 8.9 %add_tiles.15 = f32[1,16,128,32,128]{4,3,2,1,0:T(8,128)} custom-call(s32[16,128]{1,0:T(8,128)} %bitcast.375, s32[8]{0:T(128)} %constant.408.clone.order_ref, s32[60]{0:T(128)} %constant.440.picks_ref, s32[60]{0:T(128)} %concatenate.55.stands_ref, f32[1,16,128,32,128]{4,3,2,1,0:T(8,128)} %add_tiles.14.before, ...), custom_call_target="tpu_custom_call", output_to_operand_aliasing={{}: (4, {})} | custom-call | bytes 62914 | tf_op jit(solution)/shard_map/add_tiles/pallas_call | solution.py:589
  (314 shorter events, 46.6 us)
Async XLA Ops:
  6.5 59.0 %copy-start = (f32[16384]{0:T(1024)S(1)}, f32[16384]{0:T(1024)}, u32[]{:S(2)}) copy-start(f32[16384]{0:T(1024)} %param.145) | copy-start | bytes 196612
  6.5 205.4 %all-gather.5.cloned.1.call-start = ((), (), s32[]{:S(2)}) async-start(), calls=%async_computation.1 | async-start | bytes 4325376 | tf_op jit(solution)/shard_map/all_gather | solution.py:729
  11.8 62.8 %collective-permute-start = (f32[16,2,128,128]{3,2,1,0:T(8,128)}, f32[16,2,128,128]{3,2,1,0:T(8,128)S(1)}, u32[]{:S(2)}, u32[]{:S(2)}) collective-permute-start(f32[16,2,128,128]{3,2,1,0:T(8,128)} %pack_panel.2), channel_id=1, source_target_pairs={{0,16},{4,20},{8,24},{12,28},{16,0},{20,4},{24,8},{28,12},{1,17},{... | collective-permute-start | bytes 6291464 | tf_op jit(solution)/shard_map/ppermute | solution.py:33
  80.6 255.7 %all-gather.3.cloned.1.call-start = ((), (), s32[]{:S(2)}) async-start(), calls=%async_computation | async-start | bytes 10485760 | tf_op jit(solution)/shard_map/all_gather | solution.py:730
  87.1 104.4 %collective-permute-start.2 = (f32[2,128,32,128]{3,2,1,0:T(8,128)}, f32[2,128,32,128]{3,2,1,0:T(8,128)}, u32[]{:S(2)}, u32[]{:S(2)}) collective-permute-start(f32[2,128,32,128]{3,2,1,0:T(8,128)} %slice_bitcast_fusion.u0), channel_id=1, source_target_pairs={{0,16},{4,20},{8,24},{12,28},{16,0},{20,4},{24,8},{28,12},{1,17},{... | collective-permute-start | bytes 12582920 | tf_op jit(solution)/shard_map/ppermute | solution.py:33
  207.4 148.6 %collective-permute-start.4 = (f32[2,32,128,128]{3,2,1,0:T(8,128)}, f32[2,32,128,128]{3,2,1,0:T(8,128)}, u32[]{:S(2)}, u32[]{:S(2)}) collective-permute-start(f32[2,32,128,128]{3,2,1,0:T(8,128)} %place_rows.1.refs_0_), channel_id=1, source_target_pairs={{0,8},{4,12},{8,0},{12,4},{1,9},{5,13},{9,1},{13,5},{2,10},{6,14},... | collective-permute-start | bytes 12582920 | tf_op jit(solution)/shard_map/ppermute | solution.py:33
  207.6 128.6 %collective-permute-start.3 = (f32[27,128,128]{2,1,0:T(8,128)}, f32[27,128,128]{2,1,0:T(8,128)S(1)}, u32[]{:S(2)}, u32[]{:S(2)}) collective-permute-start(f32[27,128,128]{2,1,0:T(8,128)} %pack_lower.6), channel_id=1, source_target_pairs={{0,16},{4,20},{8,24},{12,28},{16,0},{20,4},{24,8},{28,12},{1,17},{... | collective-permute-start | bytes 5308424 | tf_op jit(solution)/shard_map/ppermute | solution.py:33
  209.4 146.5 %collective-permute-start.5 = (f32[23,128,128]{2,1,0:T(8,128)}, f32[23,128,128]{2,1,0:T(8,128)S(1)}, u32[]{:S(2)}, u32[]{:S(2)}) collective-permute-start(f32[23,128,128]{2,1,0:T(8,128)} %pack_lower.7), channel_id=1, source_target_pairs={{0,16},{4,20},{8,24},{12,28},{16,0},{20,4},{24,8},{28,12},{1,17},{... | collective-permute-start | bytes 4521992 | tf_op jit(solution)/shard_map/ppermute | solution.py:33
  209.7 146.2 %collective-permute-start.6 = (f32[19,128,128]{2,1,0:T(8,128)}, f32[19,128,128]{2,1,0:T(8,128)}, u32[]{:S(2)}, u32[]{:S(2)}) collective-permute-start(f32[19,128,128]{2,1,0:T(8,128)} %pack_lower.8), channel_id=1, source_target_pairs={{0,16},{4,20},{8,24},{12,28},{16,0},{20,4},{24,8},{28,12},{1,17},{... | collective-permute-start | bytes 3735560 | tf_op jit(solution)/shard_map/ppermute | solution.py:33
  211.4 124.9 %collective-permute-start.1 = (f32[15,128,128]{2,1,0:T(8,128)}, f32[15,128,128]{2,1,0:T(8,128)}, u32[]{:S(2)}, u32[]{:S(2)}) collective-permute-start(f32[15,128,128]{2,1,0:T(8,128)} %pack_lower.5), channel_id=1, source_target_pairs={{0,16},{4,20},{8,24},{12,28},{16,0},{20,4},{24,8},{28,12},{1,17},{... | collective-permute-start | bytes 2949128 | tf_op jit(solution)/shard_map/ppermute | solution.py:33
  336.3 62.8 %copy-start.2 = (f32[27,128,128]{2,1,0:T(8,128)}, f32[27,128,128]{2,1,0:T(8,128)S(1)}, u32[]{:S(2)}) copy-start(f32[27,128,128]{2,1,0:T(8,128)S(1)} %collective-permute-done.3.refs_5_.refs_6_.refs_12_.refs_13_.refs_14_.refs_15_) | copy-start | bytes 5308420
  355.9 41.2 %copy-start.3 = (f32[23,128,128]{2,1,0:T(8,128)}, f32[23,128,128]{2,1,0:T(8,128)S(1)}, u32[]{:S(2)}) copy-start(f32[23,128,128]{2,1,0:T(8,128)S(1)} %collective-permute-done.5.refs_7_.refs_8_.refs_20_.refs_21_.refs_22_.refs_23_) | copy-start | bytes 4521988
  363.3 35.7 %collective-permute-start.7 = (f32[4,32,128,128]{3,2,1,0:T(8,128)}, f32[4,32,128,128]{3,2,1,0:T(8,128)}, u32[]{:S(2)}, u32[]{:S(2)}) collective-permute-start(f32[4,32,128,128]{3,2,1,0:T(8,128)} %pad_maximum_fusion), channel_id=1, source_target_pairs={{0,4},{4,0},{8,12},{12,8},{1,5},{5,1},{9,13},{13,9},{2,6},{6,2},{1... | collective-permute-start | bytes 25165832 | tf_op jit(solution)/shard_map/ppermute | solution.py:33
  378.0 262.5 %collective-permute-start.12 = (f32[5,15,128,128]{3,2,1,0:T(8,128)}, f32[5,15,128,128]{3,2,1,0:T(8,128)}, u32[]{:S(2)}, u32[]{:S(2)}) collective-permute-start(f32[5,15,128,128]{3,2,1,0:T(8,128)} %slice.1042), channel_id=1, source_target_pairs={{0,16},{4,20},{8,24},{12,28},{16,0},{20,4},{24,8},{28,12},{1,17},{... | collective-permute-start | bytes 14745608 | tf_op jit(solution)/shard_map/ppermute | solution.py:33
  382.8 184.2 %collective-permute-start.11 = (f32[36,128,128]{2,1,0:T(8,128)}, f32[36,128,128]{2,1,0:T(8,128)}, u32[]{:S(2)}, u32[]{:S(2)}) collective-permute-start(f32[36,128,128]{2,1,0:T(8,128)} %pack_lower.9), channel_id=1, source_target_pairs={{0,16},{4,20},{8,24},{12,28},{16,0},{20,4},{24,8},{28,12},{1,17},{... | collective-permute-start | bytes 7077896 | tf_op jit(solution)/shard_map/ppermute | solution.py:33
  383.7 119.8 %collective-permute-start.8 = (f32[15,128,128]{2,1,0:T(8,128)}, f32[15,128,128]{2,1,0:T(8,128)S(1)}, u32[]{:S(2)}, u32[]{:S(2)}) collective-permute-start(f32[15,128,128]{2,1,0:T(8,128)} %collective-permute-done.1.refs_4_.refs_5_.refs_6_.refs_7_), channel_id=1, source_target_pairs={{1,4},{2,8},{3,12},{4,1},{6,9},{7,13},{8,2},{9,6},{11,14},{12,3},{... | collective-permute-start | bytes 2949128 | tf_op jit(solution)/shard_map/ppermute | solution.py:771
  397.1 171.0 %collective-permute-start.10 = (f32[23,128,128]{2,1,0:T(8,128)S(1)}, f32[23,128,128]{2,1,0:T(8,128)S(1)}, u32[]{:S(2)}, u32[]{:S(2)}) collective-permute-start(f32[23,128,128]{2,1,0:T(8,128)S(1)} %collective-permute-done.5.refs_7_.refs_8_.refs_20_.refs_21_.refs_22_.refs_23_), channel_id=1, source_target_pairs={{1,4},{2,8},{3,12},{4,1},{6,9},{7,13},{8,2},{9,6},{11,14},{12,3},{... | collective-permute-start | bytes 4521992 | tf_op jit(solution)/shard_map/ppermute | solution.py:797
  399.1 226.6 %collective-permute-start.9 = (f32[27,128,128]{2,1,0:T(8,128)S(1)}, f32[27,128,128]{2,1,0:T(8,128)S(1)}, u32[]{:S(2)}, u32[]{:S(2)}) collective-permute-start(f32[27,128,128]{2,1,0:T(8,128)S(1)} %collective-permute-done.3.refs_5_.refs_6_.refs_12_.refs_13_.refs_14_.refs_15_), channel_id=1, source_target_pairs={{1,4},{2,8},{3,12},{4,1},{6,9},{7,13},{8,2},{9,6},{11,14},{12,3},{... | collective-permute-start | bytes 5308424 | tf_op jit(solution)/shard_map/ppermute | solution.py:771
  430.7 74.5 %copy-start.90 = (pred[4,15]{1,0:T(4,128)(4,1)S(1)}, pred[4,15]{1,0:T(4,128)(4,1)}, u32[]{:S(2)}) copy-start(pred[4,15]{1,0:T(4,128)(4,1)} %constant.397.clone) | copy-start | bytes 184
  430.7 74.5 %copy-start.91 = (pred[4,15]{1,0:T(4,128)(4,1)S(1)}, pred[4,15]{1,0:T(4,128)(4,1)}, u32[]{:S(2)}) copy-start(pred[4,15]{1,0:T(4,128)(4,1)} %constant.399.clone) | copy-start | bytes 184
  503.5 63.4 %copy-start.9 = (f32[15,128,128]{2,1,0:T(8,128)}, f32[15,128,128]{2,1,0:T(8,128)S(1)}, u32[]{:S(2)}) copy-start(f32[15,128,128]{2,1,0:T(8,128)S(1)} %collective-permute-done.8.refs_0_.refs_1_.refs_2_.refs_3_) | copy-start | bytes 2949124
  503.5 169.4 %collective-permute-start.13 = (f32[3,15,128,128]{3,2,1,0:T(8,128)}, f32[3,15,128,128]{3,2,1,0:T(8,128)}, u32[]{:S(2)}, u32[]{:S(2)}) collective-permute-start(f32[3,15,128,128]{3,2,1,0:T(8,128)} %get-tuple-element.63), channel_id=1, source_target_pairs={{0,16},{4,20},{8,24},{12,28},{16,0},{20,4},{24,8},{28,12},{1,17},{... | collective-permute-start | bytes 8847368 | tf_op jit(solution)/shard_map/ppermute | solution.py:33
  505.3 62.1 %copy-start.11 = (s32[32,1,128]{2,1,0:T(1,128)S(1)}, s32[32,1,128]{2,1,0:T(1,128)}, u32[]{:S(2)}) copy-start(s32[32,1,128]{2,1,0:T(1,128)} %constant_dynamic-slice_fusion.3) | copy-start | bytes 49156
  567.0 175.9 %collective-permute-start.15 = (f32[3,15,128,128]{3,2,1,0:T(8,128)}, f32[3,15,128,128]{3,2,1,0:T(8,128)}, u32[]{:S(2)}, u32[]{:S(2)}) collective-permute-start(f32[3,15,128,128]{3,2,1,0:T(8,128)} %get-tuple-element.65), channel_id=1, source_target_pairs={{0,16},{4,20},{8,24},{12,28},{16,0},{20,4},{24,8},{28,12},{1,17},{... | collective-permute-start | bytes 8847368 | tf_op jit(solution)/shard_map/ppermute | solution.py:33
  568.1 66.2 %copy-start.7 = (f32[23,128,128]{2,1,0:T(8,128)}, f32[23,128,128]{2,1,0:T(8,128)S(1)}, u32[]{:S(2)}) copy-start(f32[23,128,128]{2,1,0:T(8,128)S(1)} %collective-permute-done.10.refs_16_.refs_17_.refs_18_.refs_19_) | copy-start | bytes 4521988
  568.1 124.2 %collective-permute-start.14 = (f32[19,128,128]{2,1,0:T(8,128)}, f32[19,128,128]{2,1,0:T(8,128)S(1)}, u32[]{:S(2)}, u32[]{:S(2)}) collective-permute-start(f32[19,128,128]{2,1,0:T(8,128)} %collective-permute-done.6.refs_9_.refs_10_.refs_4_.refs_5_.refs_6_.refs_7_), channel_id=1, source_target_pairs={{1,4},{2,8},{3,12},{4,1},{6,9},{7,13},{8,2},{9,6},{11,14},{12,3},{... | collective-permute-start | bytes 3735560 | tf_op jit(solution)/shard_map/ppermute | solution.py:797
  625.7 162.3 %collective-permute-start.18 = (f32[36,128,128]{2,1,0:T(8,128)}, f32[36,128,128]{2,1,0:T(8,128)}, u32[]{:S(2)}, u32[]{:S(2)}) collective-permute-start(f32[36,128,128]{2,1,0:T(8,128)} %collective-permute-done.11.refs_11_.refs_12_.refs_13_.refs_14_.refs_15_), channel_id=1, source_target_pairs={{1,4},{2,8},{3,12},{4,1},{6,9},{7,13},{8,2},{9,6},{11,14},{12,3},{... | collective-permute-start | bytes 7077896 | tf_op jit(solution)/shard_map/ppermute | solution.py:825
  640.5 122.8 %collective-permute-start.16 = (f32[2,15,128,128]{3,2,1,0:T(8,128)}, f32[2,15,128,128]{3,2,1,0:T(8,128)S(1)}, u32[]{:S(2)}, u32[]{:S(2)}) collective-permute-start(f32[2,15,128,128]{3,2,1,0:T(8,128)} %slice.1045), channel_id=1, source_target_pairs={{0,16},{4,20},{8,24},{12,28},{16,0},{20,4},{24,8},{28,12},{1,17},{... | collective-permute-start | bytes 5898248 | tf_op jit(solution)/shard_map/ppermute | solution.py:33
  672.9 106.3 %collective-permute-start.17 = (f32[1,15,128,128]{3,2,1,0:T(8,128)}, f32[1,15,128,128]{3,2,1,0:T(8,128)}, u32[]{:S(2)}, u32[]{:S(2)}) collective-permute-start(f32[1,15,128,128]{3,2,1,0:T(8,128)} %get-tuple-element.67), channel_id=1, source_target_pairs={{0,16},{4,20},{8,24},{12,28},{16,0},{20,4},{24,8},{28,12},{1,17},{... | collective-permute-start | bytes 2949128 | tf_op jit(solution)/shard_map/ppermute | solution.py:33
  673.5 28.0 %copy-start.46 = (s32[17]{0:T(128)S(1)}, s32[17]{0:T(128)}, u32[]{:S(2)}) copy-start(s32[17]{0:T(128)} %get-tuple-element.97) | copy-start | bytes 208
  673.5 28.0 %copy-start.47 = (s32[17]{0:T(128)S(1)}, s32[17]{0:T(128)}, u32[]{:S(2)}) copy-start(s32[17]{0:T(128)} %get-tuple-element.98) | copy-start | bytes 208
  673.5 28.0 %copy-start.48 = (s32[17]{0:T(128)S(1)}, s32[17]{0:T(128)}, u32[]{:S(2)}) copy-start(s32[17]{0:T(128)} %get-tuple-element.99) | copy-start | bytes 208
  673.5 28.0 %copy-start.49 = (s32[17]{0:T(128)S(1)}, s32[17]{0:T(128)}, u32[]{:S(2)}) copy-start(s32[17]{0:T(128)} %get-tuple-element.100) | copy-start | bytes 208
  673.5 28.0 %copy-start.50 = (s32[17]{0:T(128)S(1)}, s32[17]{0:T(128)}, u32[]{:S(2)}) copy-start(s32[17]{0:T(128)} %get-tuple-element.101) | copy-start | bytes 208
  673.5 28.0 %copy-start.51 = (s32[17]{0:T(128)S(1)}, s32[17]{0:T(128)}, u32[]{:S(2)}) copy-start(s32[17]{0:T(128)} %get-tuple-element.102) | copy-start | bytes 208
  673.5 28.0 %copy-start.52 = (s32[17]{0:T(128)S(1)}, s32[17]{0:T(128)}, u32[]{:S(2)}) copy-start(s32[17]{0:T(128)} %get-tuple-element.103) | copy-start | bytes 208
  673.5 28.0 %copy-start.53 = (s32[17]{0:T(128)S(1)}, s32[17]{0:T(128)}, u32[]{:S(2)}) copy-start(s32[17]{0:T(128)} %get-tuple-element.104) | copy-start | bytes 208
  673.5 28.0 %copy-start.54 = (s32[17]{0:T(128)S(1)}, s32[17]{0:T(128)}, u32[]{:S(2)}) copy-start(s32[17]{0:T(128)} %get-tuple-element.105) | copy-start | bytes 208
  673.6 29.4 %copy-start.38 = (s32[17]{0:T(128)S(1)}, s32[17]{0:T(128)}, u32[]{:S(2)}) copy-start(s32[17]{0:T(128)} %get-tuple-element.133) | copy-start | bytes 208
  673.6 29.4 %copy-start.39 = (s32[17]{0:T(128)S(1)}, s32[17]{0:T(128)}, u32[]{:S(2)}) copy-start(s32[17]{0:T(128)} %get-tuple-element.134) | copy-start | bytes 208
  673.6 29.4 %copy-start.40 = (s32[17]{0:T(128)S(1)}, s32[17]{0:T(128)}, u32[]{:S(2)}) copy-start(s32[17]{0:T(128)} %get-tuple-element.135) | copy-start | bytes 208
  673.6 29.4 %copy-start.41 = (s32[17]{0:T(128)S(1)}, s32[17]{0:T(128)}, u32[]{:S(2)}) copy-start(s32[17]{0:T(128)} %get-tuple-element.136) | copy-start | bytes 208
  673.6 29.4 %copy-start.42 = (s32[17]{0:T(128)S(1)}, s32[17]{0:T(128)}, u32[]{:S(2)}) copy-start(s32[17]{0:T(128)} %get-tuple-element.139) | copy-start | bytes 208
  673.6 29.4 %copy-start.43 = (s32[17]{0:T(128)S(1)}, s32[17]{0:T(128)}, u32[]{:S(2)}) copy-start(s32[17]{0:T(128)} %get-tuple-element.140) | copy-start | bytes 208
  673.7 29.4 %copy-start.44 = (s32[17]{0:T(128)S(1)}, s32[17]{0:T(128)}, u32[]{:S(2)}) copy-start(s32[17]{0:T(128)} %get-tuple-element.141) | copy-start | bytes 208
  673.7 29.4 %copy-start.45 = (s32[17]{0:T(128)S(1)}, s32[17]{0:T(128)}, u32[]{:S(2)}) copy-start(s32[17]{0:T(128)} %get-tuple-element.142) | copy-start | bytes 208
  692.3 50.5 %copy-start.8 = (f32[19,128,128]{2,1,0:T(8,128)}, f32[19,128,128]{2,1,0:T(8,128)S(1)}, u32[]{:S(2)}) copy-start(f32[19,128,128]{2,1,0:T(8,128)S(1)} %collective-permute-done.14.refs_0_.refs_1_.refs_2_.refs_3_) | copy-start | bytes 3735556
  692.3 124.3 %collective-permute-start.19 = (f32[1,15,128,128]{3,2,1,0:T(8,128)}, f32[1,15,128,128]{3,2,1,0:T(8,128)}, u32[]{:S(2)}, u32[]{:S(2)}) collective-permute-start(f32[1,15,128,128]{3,2,1,0:T(8,128)} %get-tuple-element.68), channel_id=1, source_target_pairs={{0,16},{4,20},{8,24},{12,28},{16,0},{20,4},{24,8},{28,12},{1,17},{... | collective-permute-start | bytes 2949128 | tf_op jit(solution)/shard_map/ppermute | solution.py:33
  (66 other events, 1093.0 us)
Sparse Core Ops, SparseCore 0:
  80.7 72.9 all-gather.4
  155.2 149.7 all-gather.2

commit v5 on v4

--- a/solution.py
+++ b/solution.py
@@ -820,9 +820,7 @@
             else:
                 send(2, front)
                 lower[4] = after(lower[4], front)
-                front = after(front, turned[1], turned[2], lower[4])
-    if mirrored:
-        turned.append(lax.ppermute(lower[4], ("row", "col"), pairs))
+                front = after(front, turned[2], lower[4])
     front = add_first(front, first, other_rows[:1], trailing_cols)
 
     def turned_tiles(front, parts, low, top):
@@ -846,6 +844,9 @@
         flat = came[number].reshape(-1, tile, tile)
         steps = [(j, g) for j in range(at, at + count) for g in range(groups)]
         if mirrored:
+            if number == 1:
+                turned.append(lax.ppermute(after(lower[4], front), ("row", "col"), pairs))
+                front = after(front, turned[1])
             if number == 2:
                 front = turned_tiles(after(front, turned[3]), (0, 1, 2), 1, near)
             if number == len(spans) - 1:

time: 845 us -> 830 us (0.982)
  waiting for transfers between devices: 118 us -> 98 us
    ppermute x2, waiting for transfers between devices: 66.2 us -> 0.01 us  [on_device(): turned = [lax.ppermute(part, ('row', 'col'), pairs) for part in lower[:2]]]
    ppermute x2, waiting for transfers between devices: 0.01 us -> 44.9 us  [on_device(): turned += [lax.ppermute(part, ('row', 'col'), pairs) for part in lower[2:4]]]
  transfers between devices with their start and end apart: 22 -> 22, of which waited for: 3 -> 2; matrix products, arithmetic and copies ran while one was open for 10% -> 11% of each run, Pallas kernels for 67% -> 68%
where the time goes in v5:
time: 830 us; the launch traced here: 819 us
  Pallas kernels  570 us (69%)
  waiting for transfers between devices  98 us (12%)
  local copies, waits for them, and re-layouts  77.3 us (9%)
  starting transfers between devices  35.6 us (4%)
  between operations  15 us (2%)
  other arithmetic  14.8 us (2%)
  matrix products  8.81 us (1%)
    pallas_call x8, Pallas kernels, add_tiles(): pl.pallas_call(kernel, grid_spec=pltpu.PrefetchScalarGridSpec(num_scalar_...  166 us
    pallas_call x2, Pallas kernels, own_part(): pl.pallas_call(kernel, grid_spec=pltpu.PrefetchScalarGridSpec(num_scalar_...  124 us
    pallas_call x1, Pallas kernels, inverse_factor(): pl.pallas_call(kernel, in_specs=[pl.BlockSpec(memory_space=pltpu.VMEM)],...  113 us
    pallas_call x5, Pallas kernels, pack_lower(): pl.pallas_call(kernel, grid_spec=pltpu.PrefetchScalarGridSpec(num_scalar_...  64.7 us
    ppermute x15, waiting for transfers between devices, swapped(): return lax.ppermute(value, axis, pairs)  53 us
    ppermute x2, waiting for transfers between devices, on_device(): turned += [lax.ppermute(part, ('row', 'col'), pairs) for part in lower[2:4]]  44.9 us
    pallas_call x1, Pallas kernels, solve_columns(): pl.pallas_call(kernel, grid_spec=pltpu.PrefetchScalarGridSpec(num_scalar_...  26.1 us
    pallas_call x1, Pallas kernels, pack_cross(): pl.pallas_call(kernel, grid_spec=pltpu.PrefetchScalarGridSpec(num_scalar_...  24.3 us
  transfers between devices with their start and end apart: 22, of which 2 were waited for; matrix products, arithmetic and copies ran while one was open for 11% of the time, Pallas kernels for 68%

profile of v5, /device:TPU:6, one launch (start us, length us, event | category | flops | bytes accessed | tf_op | source)
XLA Modules:
  0.0 819.5 jit_solution(1276583207973450302)
XLA Ops:
  6.5 5.3 pack_panel.2
  12.4 14.9 %pack_lower.6 = f32[27,128,128]{2,1,0:T(8,128)} custom-call(s32[1]{0:T(128)S(6)} %sub.93.half_ref.parity_ref, s32[1]{0:T(128)S(6)} %sub.93.half_ref.parity_ref, f32[1,2,16,128,32,128]{5,4,3,2,1,0:T(8,128)} %refs_1_.1), custom_call_target="tpu_custom_call" | custom-call | bytes 311296 | tf_op jit(solution)/shard_map/pack_lower/pallas_call | solution.py:144
  27.3 12.9 %pack_lower.7 = f32[23,128,128]{2,1,0:T(8,128)} custom-call(s32[1]{0:T(128)S(6)} %sub.93.half_ref.parity_ref, s32[1]{0:T(128)S(6)} %sub.93.half_ref.parity_ref, f32[1,2,16,128,32,128]{5,4,3,2,1,0:T(8,128)} %refs_1_.1), custom_call_target="tpu_custom_call" | custom-call | bytes 266731 | tf_op jit(solution)/shard_map/pack_lower/pallas_call | solution.py:144
  40.3 15.3 %pack_lower.5 = f32[15,128,128]{2,1,0:T(8,128)} custom-call(s32[1]{0:T(128)S(6)} %sub.93.half_ref.parity_ref, s32[1]{0:T(128)S(6)} %sub.93.half_ref.parity_ref, f32[1,2,16,128,32,128]{5,4,3,2,1,0:T(8,128)} %refs_1_.1), custom_call_target="tpu_custom_call" | custom-call | bytes 324403 | tf_op jit(solution)/shard_map/pack_lower/pallas_call | solution.py:144
  55.6 5.3 pack_panel.3
  61.1 4.4 select_reduce_fusion
  66.3 3.6 fusion.6
  70.0 4.6 slice_bitcast_fusion.u0
  74.7 2.2 fusion.2
  80.8 2.3 copy.198
  83.1 3.9 reshape.256
  88.6 10.6 %pack_lower.9 = f32[36,128,128]{2,1,0:T(8,128)} custom-call(s32[1]{0:T(128)S(6)} %sub.93.half_ref.parity_ref, s32[1]{0:T(128)S(6)} %sub.93.half_ref.parity_ref, f32[1,2,16,128,32,128]{5,4,3,2,1,0:T(8,128)} %refs_1_.1), custom_call_target="tpu_custom_call" | custom-call | bytes 191365 | tf_op jit(solution)/shard_map/pack_lower/pallas_call | solution.py:144
  99.2 11.0 %pack_lower.8 = f32[19,128,128]{2,1,0:T(8,128)} custom-call(s32[1]{0:T(128)S(6)} %sub.93.half_ref.parity_ref, s32[1]{0:T(128)S(6)} %sub.93.half_ref.parity_ref, f32[1,2,16,128,32,128]{5,4,3,2,1,0:T(8,128)} %refs_1_.1), custom_call_target="tpu_custom_call" | custom-call | bytes 222167 | tf_op jit(solution)/shard_map/pack_lower/pallas_call | solution.py:144
  114.2 24.3 %pack_cross.1 = f32[15,15,128,128]{3,2,1,0:T(8,128)} custom-call(s32[1]{0:T(128)S(6)} %sub.93.half_ref.parity_ref, s32[1]{0:T(128)} %bitcast.151.half_ref.parity_ref, f32[1,2,16,128,32,128]{5,4,3,2,1,0:T(8,128)} %refs_1_.1), custom_call_target="tpu_custom_call" | custom-call | bytes 503316 | tf_op jit(solution)/shard_map/pack_cross/pallas_call | solution.py:102
  138.5 52.9 %collective-permute-done.2.u1 = f32[2,128,32,128]{3,2,1,0:T(8,128)} collective-permute-done((f32[2,128,32,128]{3,2,1,0:T(8,128)}, f32[2,128,32,128]{3,2,1,0:T(8,128)}, u32[]{:S(2)}, u32[]{:S(2)}) %collective-permute-start.2) | collective-permute-done | bytes 4194336 | tf_op jit(solution)/shard_map/ppermute | solution.py:33
  191.6 15.7 %place_rows.1.refs_0_ = f32[2,32,128,128]{3,2,1,0:T(8,128)} custom-call(s32[2,128]{1,0:T(2,128)} %bitcast.399, s32[2,128]{1,0:T(2,128)} %bitcast.400, s32[2]{0:T(128)} %compare_select_fusion.2.where_ref, f32[2,128,32,128]{3,2,1,0:T(8,128)} %slice_bitcast_fusion.u0, f32[2,128,32,128]{3,2,1,0:T(8,128)} %collective-permute-done.2.u1, s32[32,128]{1,0:T(8,128)} %bitcast.378, ...), custom_call_target="tpu_custom_call" | custom-call | bytes 125829 | tf_op jit(solution)/shard_map/place_rows/pallas_call | solution.py:233
  207.6 1.7 collective-permute-start.3
  209.6 1.7 collective-permute-start.6
  212.5 5.2 copy.187
  217.7 5.5 reshape.229.a
  223.2 113.5 %inverse_factor.1 = (bf16[1024,1024]{1,0:T(8,128)(2,1)}, bf16[1024,1024]{1,0:T(8,128)(2,1)}) custom-call(f32[1024,1024]{1,0:T(8,128)} %reshape.229.a), custom_call_target="tpu_custom_call" | custom-call | flops 1000000000 | bytes 83886 | tf_op jit(solution)/shard_map/inverse_factor/pallas_call | solution.py:321
  336.8 19.3 %solve_rows.1 = (bf16[2048,1024]{1,0:T(8,128)(2,1)}, bf16[2048,1024]{1,0:T(8,128)(2,1)}, f32[2,2048,128]{2,1,0:T(8,128)}) custom-call(s32[1]{0:T(128)} %bitcast.159.me, f32[4,2048,256]{2,1,0:T(8,128)} %all-gather.3.cloned.1.call-done.f, bf16[1024,1024]{1,0:T(8,128)(2,1)} %get-tuple-element.45.h.refs_3_, bf16[1024,1024]{1,0:T(8,128)(2,1)} %get-tuple-element.50.l.refs_4_), custom_call_target="tpu_custom_call" | custom-call | flops 128849016 | bytes 167772 | tf_op jit(solution)/shard_map/solve_rows/pallas_call | solution.py:358
  356.3 6.7 pad_maximum_fusion
  371.6 5.4 slice.1042
  377.0 1.7 collective-permute-start.11
  383.9 5.7 collective-permute-start.8
  391.4 5.9 fusion.30
  397.3 1.9 collective-permute-start.9
  399.2 26.1 %solve_columns.1 = (bf16[1024,4096]{1,0:T(8,128)(2,1)}, bf16[1024,4096]{1,0:T(8,128)(2,1)}) custom-call(s32[8]{0:T(128)} %pad_add_fusion.home, f32[2,32,128,128]{3,2,1,0:T(8,128)} %place_rows.1.refs_0_, f32[2,32,128,128]{3,2,1,0:T(8,128)} %collective-permute-done.4.refs_1_, f32[4,32,128,128]{3,2,1,0:T(8,128)} %collective-permute-done.7.refs_2_, ...), custom_call_target="tpu_custom_call" | custom-call | flops 171798688 | bytes 335544 | tf_op jit(solution)/shard_map/solve_columns/pallas_call | solution.py:408
  425.3 62.2 %own_part.2.refs_0_ = f32[1,16,128,32,128]{4,3,2,1,0:T(8,128)} custom-call(s32[1]{0:T(128)} %bitcast.151.half_ref.parity_ref, s32[16,128]{1,0:T(8,128)} %bitcast.386, s32[16]{0:T(128)} %copy-done.24, f32[1,2,16,128,32,128]{5,4,3,2,1,0:T(8,128)} %refs_1_.1, s32[32,128]{1,0:T(8,128)} %bitcast.379, f32[16,1,128]{2,1,0:T(1,128)} %bitcast.383, ...), custom_call_target="tpu_custom_call" | custom-call | flops 515396064 | bytes 671088 | tf_op jit(solution)/shard_map/own_part/pallas_call | solution.py:478
  487.5 1.9 collective-permute-start.13
  489.5 5.4 collective-permute-start.12
  496.7 61.6 %own_part.3.before = f32[1,16,128,32,128]{4,3,2,1,0:T(8,128)} custom-call(s32[1]{0:T(128)} %bitcast.151.half_ref.parity_ref, s32[16,128]{1,0:T(8,128)} %bitcast.387, s32[16]{0:T(128)} %copy-done.24, f32[1,16,128,32,128]{4,3,2,1,0:T(8,128)} %own_part.2.refs_0_, f32[1,2,16,128,32,128]{5,4,3,2,1,0:T(8,128)} %refs_1_.1, ...), custom_call_target="tpu_custom_call", output_to_operand_aliasing={{}: (3, {})} | custom-call | flops 515396064 | bytes 671088 | tf_op jit(solution)/shard_map/own_part/pallas_call | solution.py:478
  560.5 3.0 slice.1045
  563.5 3.1 constant_dynamic-slice_fusion.9.u
  566.6 2.0 collective-permute-start.14
  568.7 5.8 add_first.1.before
  574.5 26.6 %add_tiles.8.before = f32[1,16,128,32,128]{4,3,2,1,0:T(8,128)} custom-call(s32[16,128]{1,0:T(8,128)} %bitcast.368, s32[40]{0:T(128)} %constant.342.clone.order_ref, s32[180]{0:T(256)} %constant.559.picks_ref, s32[180]{0:T(256)} %concatenate.69.stands_ref, f32[1,16,128,32,128]{4,3,2,1,0:T(8,128)} %add_first.1.before, ...), custom_call_target="tpu_custom_call", output_to_operand_aliasing={{}: (4, {})} | custom-call | bytes 314572 | tf_op jit(solution)/shard_map/add_tiles/pallas_call | solution.py:589
  601.1 5.6 collective-permute-start.18
  610.0 3.0 fusion.29
  613.9 18.9 %add_tiles.9.before = f32[1,16,128,32,128]{4,3,2,1,0:T(8,128)} custom-call(s32[16,128]{1,0:T(8,128)} %bitcast.369, s32[24]{0:T(128)} %constant.355.clone.order_ref, s32[144]{0:T(256)} %constant.540.picks_ref, s32[144]{0:T(256)} %concatenate.67.stands_ref, f32[1,16,128,32,128]{4,3,2,1,0:T(8,128)} %add_tiles.8.before, ...), custom_call_target="tpu_custom_call", output_to_operand_aliasing={{}: (4, {})} | custom-call | bytes 188743 | tf_op jit(solution)/shard_map/add_tiles/pallas_call | solution.py:589
  632.8 44.9 %collective-permute-done.14.refs_0_.refs_1_.refs_2_.refs_3_ = f32[19,128,128]{2,1,0:T(8,128)} collective-permute-done((f32[19,128,128]{2,1,0:T(8,128)}, f32[19,128,128]{2,1,0:T(8,128)}, u32[]{:S(2)}, u32[]{:S(2)}) %collective-permute-start.14) | collective-permute-done | bytes 1245216 | tf_op jit(solution)/shard_map/ppermute | solution.py:797
  690.5 39.1 %add_tiles.10.before = f32[1,16,128,32,128]{4,3,2,1,0:T(8,128)} custom-call(s32[16,128]{1,0:T(8,128)} %bitcast.370, s32[34]{0:T(128)} %constant.362.clone.order_ref, s32[408]{0:T(512)} %concatenate.64.picks_ref, s32[408]{0:T(512)} %concatenate.65.stands_ref, f32[1,16,128,32,128]{4,3,2,1,0:T(8,128)} %add_tiles.9.before, ...), custom_call_target="tpu_custom_call", output_to_operand_aliasing={{}: (4, {})} | custom-call | bytes 267386 | tf_op jit(solution)/shard_map/add_tiles/pallas_call | solution.py:589
  729.6 20.5 %add_tiles.11.before = f32[1,16,128,32,128]{4,3,2,1,0:T(8,128)} custom-call(s32[16,128]{1,0:T(8,128)} %bitcast.371, s32[24]{0:T(128)} %constant.370.clone.order_ref, s32[180]{0:T(256)} %constant.525.picks_ref, s32[180]{0:T(256)} %concatenate.63.stands_ref, f32[1,16,128,32,128]{4,3,2,1,0:T(8,128)} %add_tiles.10.before, ...), custom_call_target="tpu_custom_call", output_to_operand_aliasing={{}: (4, {})} | custom-call | bytes 188743 | tf_op jit(solution)/shard_map/add_tiles/pallas_call | solution.py:589
  750.1 14.6 %add_tiles.12.before = f32[1,16,128,32,128]{4,3,2,1,0:T(8,128)} custom-call(s32[16,128]{1,0:T(8,128)} %bitcast.372, s32[16]{0:T(128)} %constant.383.clone.order_ref, s32[120]{0:T(128)} %constant.494.picks_ref, s32[120]{0:T(128)} %concatenate.61.stands_ref, f32[1,16,128,32,128]{4,3,2,1,0:T(8,128)} %add_tiles.11.before, ...), custom_call_target="tpu_custom_call", output_to_operand_aliasing={{}: (4, {})} | custom-call | bytes 125829 | tf_op jit(solution)/shard_map/add_tiles/pallas_call | solution.py:589
  764.7 8.8 %add_tiles.13.before = f32[1,16,128,32,128]{4,3,2,1,0:T(8,128)} custom-call(s32[16,128]{1,0:T(8,128)} %bitcast.373, s32[8]{0:T(128)} %constant.396.clone.order_ref, s32[60]{0:T(128)} %constant.463.picks_ref, s32[60]{0:T(128)} %concatenate.59.stands_ref, f32[1,16,128,32,128]{4,3,2,1,0:T(8,128)} %add_tiles.12.before, ...), custom_call_target="tpu_custom_call", output_to_operand_aliasing={{}: (4, {})} | custom-call | bytes 62914 | tf_op jit(solution)/shard_map/add_tiles/pallas_call | solution.py:589
  773.6 28.7 %add_tiles.14.before = f32[1,16,128,32,128]{4,3,2,1,0:T(8,128)} custom-call(s32[16,128]{1,0:T(8,128)} %bitcast.374, s32[30]{0:T(128)} %constant.401.clone.order_ref, s32[240]{0:T(256)} %concatenate.56.picks_ref, s32[240]{0:T(256)} %concatenate.57.stands_ref, f32[1,16,128,32,128]{4,3,2,1,0:T(8,128)} %add_tiles.13.before, ...), custom_call_target="tpu_custom_call", output_to_operand_aliasing={{}: (4, {})} | custom-call | bytes 235929 | tf_op jit(solution)/shard_map/add_tiles/pallas_call | solution.py:589
  803.3 9.0 %add_tiles.15 = f32[1,16,128,32,128]{4,3,2,1,0:T(8,128)} custom-call(s32[16,128]{1,0:T(8,128)} %bitcast.375, s32[8]{0:T(128)} %constant.408.clone.order_ref, s32[60]{0:T(128)} %constant.440.picks_ref, s32[60]{0:T(128)} %concatenate.55.stands_ref, f32[1,16,128,32,128]{4,3,2,1,0:T(8,128)} %add_tiles.14.before, ...), custom_call_target="tpu_custom_call", output_to_operand_aliasing={{}: (4, {})} | custom-call | bytes 62914 | tf_op jit(solution)/shard_map/add_tiles/pallas_call | solution.py:589
  (276 shorter events, 49.6 us)
Async XLA Ops:
  6.5 206.0 %all-gather.5.cloned.1.call-start = ((), (), s32[]{:S(2)}) async-start(), calls=%async_computation.1 | async-start | bytes 4325376 | tf_op jit(solution)/shard_map/all_gather | solution.py:729
  11.8 62.8 %collective-permute-start = (f32[16,2,128,128]{3,2,1,0:T(8,128)}, f32[16,2,128,128]{3,2,1,0:T(8,128)S(1)}, u32[]{:S(2)}, u32[]{:S(2)}) collective-permute-start(f32[16,2,128,128]{3,2,1,0:T(8,128)} %pack_panel.2), channel_id=1, source_target_pairs={{0,16},{4,20},{8,24},{12,28},{16,0},{20,4},{24,8},{28,12},{1,17},{... | collective-permute-start | bytes 6291464 | tf_op jit(solution)/shard_map/ppermute | solution.py:33
  80.5 256.2 %all-gather.3.cloned.1.call-start = ((), (), s32[]{:S(2)}) async-start(), calls=%async_computation | async-start | bytes 10485760 | tf_op jit(solution)/shard_map/all_gather | solution.py:730
  87.1 104.4 %collective-permute-start.2 = (f32[2,128,32,128]{3,2,1,0:T(8,128)}, f32[2,128,32,128]{3,2,1,0:T(8,128)}, u32[]{:S(2)}, u32[]{:S(2)}) collective-permute-start(f32[2,128,32,128]{3,2,1,0:T(8,128)} %slice_bitcast_fusion.u0), channel_id=1, source_target_pairs={{0,16},{4,20},{8,24},{12,28},{16,0},{20,4},{24,8},{28,12},{1,17},{... | collective-permute-start | bytes 12582920 | tf_op jit(solution)/shard_map/ppermute | solution.py:33
  207.3 148.8 %collective-permute-start.4 = (f32[2,32,128,128]{3,2,1,0:T(8,128)}, f32[2,32,128,128]{3,2,1,0:T(8,128)}, u32[]{:S(2)}, u32[]{:S(2)}) collective-permute-start(f32[2,32,128,128]{3,2,1,0:T(8,128)} %place_rows.1.refs_0_), channel_id=1, source_target_pairs={{0,8},{4,12},{8,0},{12,4},{1,9},{5,13},{9,1},{13,5},{2,10},{6,14},... | collective-permute-start | bytes 12582920 | tf_op jit(solution)/shard_map/ppermute | solution.py:33
  207.6 129.1 %collective-permute-start.3 = (f32[27,128,128]{2,1,0:T(8,128)S(1)}, f32[27,128,128]{2,1,0:T(8,128)}, u32[]{:S(2)}, u32[]{:S(2)}) collective-permute-start(f32[27,128,128]{2,1,0:T(8,128)S(1)} %copy-done.8), channel_id=1, source_target_pairs={{0,16},{4,20},{8,24},{12,28},{16,0},{20,4},{24,8},{28,12},{1,17},{... | collective-permute-start | bytes 5308424 | tf_op jit(solution)/shard_map/ppermute | solution.py:33
  209.3 146.7 %collective-permute-start.5 = (f32[23,128,128]{2,1,0:T(8,128)}, f32[23,128,128]{2,1,0:T(8,128)}, u32[]{:S(2)}, u32[]{:S(2)}) collective-permute-start(f32[23,128,128]{2,1,0:T(8,128)} %pack_lower.7), channel_id=1, source_target_pairs={{0,16},{4,20},{8,24},{12,28},{16,0},{20,4},{24,8},{28,12},{1,17},{... | collective-permute-start | bytes 4521992 | tf_op jit(solution)/shard_map/ppermute | solution.py:33
  209.6 146.5 %collective-permute-start.6 = (f32[19,128,128]{2,1,0:T(8,128)}, f32[19,128,128]{2,1,0:T(8,128)}, u32[]{:S(2)}, u32[]{:S(2)}) collective-permute-start(f32[19,128,128]{2,1,0:T(8,128)} %pack_lower.8), channel_id=1, source_target_pairs={{0,16},{4,20},{8,24},{12,28},{16,0},{20,4},{24,8},{28,12},{1,17},{... | collective-permute-start | bytes 3735560 | tf_op jit(solution)/shard_map/ppermute | solution.py:33
  211.3 125.4 %collective-permute-start.1 = (f32[15,128,128]{2,1,0:T(8,128)}, f32[15,128,128]{2,1,0:T(8,128)S(1)}, u32[]{:S(2)}, u32[]{:S(2)}) collective-permute-start(f32[15,128,128]{2,1,0:T(8,128)} %pack_lower.5), channel_id=1, source_target_pairs={{0,16},{4,20},{8,24},{12,28},{16,0},{20,4},{24,8},{28,12},{1,17},{... | collective-permute-start | bytes 2949128 | tf_op jit(solution)/shard_map/ppermute | solution.py:33
  363.1 36.2 %collective-permute-start.7 = (f32[4,32,128,128]{3,2,1,0:T(8,128)}, f32[4,32,128,128]{3,2,1,0:T(8,128)}, u32[]{:S(2)}, u32[]{:S(2)}) collective-permute-start(f32[4,32,128,128]{3,2,1,0:T(8,128)} %pad_maximum_fusion), channel_id=1, source_target_pairs={{0,4},{4,0},{8,12},{12,8},{1,5},{5,1},{9,13},{13,9},{2,6},{6,2},{1... | collective-permute-start | bytes 25165832 | tf_op jit(solution)/shard_map/ppermute | solution.py:33
  377.0 197.5 %collective-permute-start.11 = (f32[5,15,128,128]{3,2,1,0:T(8,128)}, f32[5,15,128,128]{3,2,1,0:T(8,128)}, u32[]{:S(2)}, u32[]{:S(2)}) collective-permute-start(f32[5,15,128,128]{3,2,1,0:T(8,128)} %slice.1042), channel_id=1, source_target_pairs={{0,16},{4,20},{8,24},{12,28},{16,0},{20,4},{24,8},{28,12},{1,17},{... | collective-permute-start | bytes 14745608 | tf_op jit(solution)/shard_map/ppermute | solution.py:33
  383.0 175.4 %collective-permute-start.10 = (f32[36,128,128]{2,1,0:T(8,128)S(1)}, f32[36,128,128]{2,1,0:T(8,128)S(1)}, u32[]{:S(2)}, u32[]{:S(2)}) collective-permute-start(f32[36,128,128]{2,1,0:T(8,128)S(1)} %copy-done.7), channel_id=1, source_target_pairs={{0,16},{4,20},{8,24},{12,28},{16,0},{20,4},{24,8},{28,12},{1,17},{... | collective-permute-start | bytes 7077896 | tf_op jit(solution)/shard_map/ppermute | solution.py:33
  383.9 103.6 %collective-permute-start.8 = (f32[15,128,128]{2,1,0:T(8,128)S(1)}, f32[15,128,128]{2,1,0:T(8,128)S(1)}, u32[]{:S(2)}, u32[]{:S(2)}) collective-permute-start(f32[15,128,128]{2,1,0:T(8,128)S(1)} %collective-permute-done.1.refs_4_.refs_5_.refs_6_.refs_7_), channel_id=1, source_target_pairs={{1,4},{2,8},{3,12},{4,1},{6,9},{7,13},{8,2},{9,6},{11,14},{12,3},{... | collective-permute-start | bytes 2949128 | tf_op jit(solution)/shard_map/ppermute | solution.py:771
  397.3 169.3 %collective-permute-start.9 = (f32[23,128,128]{2,1,0:T(8,128)}, f32[23,128,128]{2,1,0:T(8,128)}, u32[]{:S(2)}, u32[]{:S(2)}) collective-permute-start(f32[23,128,128]{2,1,0:T(8,128)} %collective-permute-done.5.refs_7_.refs_8_.refs_20_.refs_21_.refs_22_.refs_23_), channel_id=1, source_target_pairs={{1,4},{2,8},{3,12},{4,1},{6,9},{7,13},{8,2},{9,6},{11,14},{12,3},{... | collective-permute-start | bytes 4521992 | tf_op jit(solution)/shard_map/ppermute | solution.py:797
  425.3 71.3 %copy-start.71 = (pred[4,15]{1,0:T(4,128)(4,1)S(1)}, pred[4,15]{1,0:T(4,128)(4,1)}, u32[]{:S(2)}) copy-start(pred[4,15]{1,0:T(4,128)(4,1)} %constant.397.clone) | copy-start | bytes 184
  425.3 71.3 %copy-start.72 = (pred[4,15]{1,0:T(4,128)(4,1)S(1)}, pred[4,15]{1,0:T(4,128)(4,1)}, u32[]{:S(2)}) copy-start(pred[4,15]{1,0:T(4,128)(4,1)} %constant.399.clone) | copy-start | bytes 184
  487.5 70.8 %copy-start.5 = (f32[15,128,128]{2,1,0:T(8,128)}, f32[15,128,128]{2,1,0:T(8,128)S(1)}, u32[]{:S(2)}) copy-start(f32[15,128,128]{2,1,0:T(8,128)S(1)} %collective-permute-done.8.refs_0_.refs_1_.refs_2_.refs_3_) | copy-start | bytes 2949124
  487.5 125.5 %collective-permute-start.13 = (f32[3,15,128,128]{3,2,1,0:T(8,128)}, f32[3,15,128,128]{3,2,1,0:T(8,128)}, u32[]{:S(2)}, u32[]{:S(2)}) collective-permute-start(f32[3,15,128,128]{3,2,1,0:T(8,128)} %get-tuple-element.66), channel_id=1, source_target_pairs={{0,16},{4,20},{8,24},{12,28},{16,0},{20,4},{24,8},{28,12},{1,17},{... | collective-permute-start | bytes 8847368 | tf_op jit(solution)/shard_map/ppermute | solution.py:33
  489.5 117.9 %collective-permute-start.12 = (f32[27,128,128]{2,1,0:T(8,128)}, f32[27,128,128]{2,1,0:T(8,128)}, u32[]{:S(2)}, u32[]{:S(2)}) collective-permute-start(f32[27,128,128]{2,1,0:T(8,128)} %collective-permute-done.3.refs_5_.refs_6_.refs_12_.refs_13_.refs_14_.refs_15_), channel_id=1, source_target_pairs={{1,4},{2,8},{3,12},{4,1},{6,9},{7,13},{8,2},{9,6},{11,14},{12,3},{... | collective-permute-start | bytes 5308424 | tf_op jit(solution)/shard_map/ppermute | solution.py:771
  496.7 63.1 %copy-start.10 = (s32[32,1,128]{2,1,0:T(1,128)S(1)}, s32[32,1,128]{2,1,0:T(1,128)}, u32[]{:S(2)}) copy-start(s32[32,1,128]{2,1,0:T(1,128)} %constant_dynamic-slice_fusion.3) | copy-start | bytes 49156
  558.4 171.2 %collective-permute-start.15 = (f32[3,15,128,128]{3,2,1,0:T(8,128)}, f32[3,15,128,128]{3,2,1,0:T(8,128)}, u32[]{:S(2)}, u32[]{:S(2)}) collective-permute-start(f32[3,15,128,128]{3,2,1,0:T(8,128)} %get-tuple-element.68), channel_id=1, source_target_pairs={{0,16},{4,20},{8,24},{12,28},{16,0},{20,4},{24,8},{28,12},{1,17},{... | collective-permute-start | bytes 8847368 | tf_op jit(solution)/shard_map/ppermute | solution.py:33
  566.6 111.1 %collective-permute-start.14 = (f32[19,128,128]{2,1,0:T(8,128)}, f32[19,128,128]{2,1,0:T(8,128)}, u32[]{:S(2)}, u32[]{:S(2)}) collective-permute-start(f32[19,128,128]{2,1,0:T(8,128)} %collective-permute-done.6.refs_9_.refs_10_.refs_4_.refs_5_.refs_6_.refs_7_), channel_id=1, source_target_pairs={{1,4},{2,8},{3,12},{4,1},{6,9},{7,13},{8,2},{9,6},{11,14},{12,3},{... | collective-permute-start | bytes 3735560 | tf_op jit(solution)/shard_map/ppermute | solution.py:797
  601.1 172.5 %collective-permute-start.18 = (f32[36,128,128]{2,1,0:T(8,128)S(1)}, f32[36,128,128]{2,1,0:T(8,128)}, u32[]{:S(2)}, u32[]{:S(2)}) collective-permute-start(f32[36,128,128]{2,1,0:T(8,128)S(1)} %collective-permute-done.10.refs_11_.refs_12_.refs_13_.refs_14_.refs_15_), channel_id=1, source_target_pairs={{1,4},{2,8},{3,12},{4,1},{6,9},{7,13},{8,2},{9,6},{11,14},{12,3},{... | collective-permute-start | bytes 7077896 | tf_op jit(solution)/shard_map/ppermute | solution.py:848
  607.4 142.7 %collective-permute-start.16 = (f32[2,15,128,128]{3,2,1,0:T(8,128)}, f32[2,15,128,128]{3,2,1,0:T(8,128)}, u32[]{:S(2)}, u32[]{:S(2)}) collective-permute-start(f32[2,15,128,128]{3,2,1,0:T(8,128)} %slice.1045), channel_id=1, source_target_pairs={{0,16},{4,20},{8,24},{12,28},{16,0},{20,4},{24,8},{28,12},{1,17},{... | collective-permute-start | bytes 5898248 | tf_op jit(solution)/shard_map/ppermute | solution.py:33
  613.0 151.7 %collective-permute-start.17 = (f32[1,15,128,128]{3,2,1,0:T(8,128)}, f32[1,15,128,128]{3,2,1,0:T(8,128)}, u32[]{:S(2)}, u32[]{:S(2)}) collective-permute-start(f32[1,15,128,128]{3,2,1,0:T(8,128)} %get-tuple-element.70), channel_id=1, source_target_pairs={{0,16},{4,20},{8,24},{12,28},{16,0},{20,4},{24,8},{28,12},{1,17},{... | collective-permute-start | bytes 2949128 | tf_op jit(solution)/shard_map/ppermute | solution.py:33
  613.7 66.4 %copy-start.14 = (s32[4]{0:T(128)S(1)}, s32[4]{0:T(128)}, u32[]{:S(2)}) copy-start(s32[4]{0:T(128)} %get-tuple-element.219) | copy-start | bytes 52
  613.7 66.4 %copy-start.15 = (s32[4]{0:T(128)S(1)}, s32[4]{0:T(128)}, u32[]{:S(2)}) copy-start(s32[4]{0:T(128)} %get-tuple-element.220) | copy-start | bytes 52
  613.7 66.4 %copy-start.16 = (s32[4]{0:T(128)S(1)}, s32[4]{0:T(128)}, u32[]{:S(2)}) copy-start(s32[4]{0:T(128)} %get-tuple-element.221) | copy-start | bytes 52
  613.7 66.4 %copy-start.17 = (s32[4]{0:T(128)S(1)}, s32[4]{0:T(128)}, u32[]{:S(2)}) copy-start(s32[4]{0:T(128)} %get-tuple-element.222) | copy-start | bytes 52
  613.7 66.4 %copy-start.18 = (s32[4]{0:T(128)S(1)}, s32[4]{0:T(128)}, u32[]{:S(2)}) copy-start(s32[4]{0:T(128)} %get-tuple-element.223) | copy-start | bytes 52
  613.7 66.4 %copy-start.19 = (s32[4]{0:T(128)S(1)}, s32[4]{0:T(128)}, u32[]{:S(2)}) copy-start(s32[4]{0:T(128)} %get-tuple-element.224) | copy-start | bytes 52
  613.8 66.4 %copy-start.20 = (s32[4]{0:T(128)S(1)}, s32[4]{0:T(128)}, u32[]{:S(2)}) copy-start(s32[4]{0:T(128)} %get-tuple-element.225) | copy-start | bytes 52
  613.8 66.4 %copy-start.21 = (s32[4]{0:T(128)S(1)}, s32[4]{0:T(128)}, u32[]{:S(2)}) copy-start(s32[4]{0:T(128)} %get-tuple-element.226) | copy-start | bytes 52
  613.8 66.4 %copy-start.22 = (s32[4]{0:T(128)S(1)}, s32[4]{0:T(128)}, u32[]{:S(2)}) copy-start(s32[4]{0:T(128)} %get-tuple-element.227) | copy-start | bytes 52
  613.8 66.4 %copy-start.23 = (s32[4]{0:T(128)S(1)}, s32[4]{0:T(128)}, u32[]{:S(2)}) copy-start(s32[4]{0:T(128)} %get-tuple-element.228) | copy-start | bytes 52
  613.8 69.0 %copy-start.25 = (s32[12]{0:T(128)S(1)}, s32[12]{0:T(128)}, u32[]{:S(2)}) copy-start(s32[12]{0:T(128)} %get-tuple-element.151) | copy-start | bytes 148
  613.8 69.0 %copy-start.26 = (s32[12]{0:T(128)S(1)}, s32[12]{0:T(128)}, u32[]{:S(2)}) copy-start(s32[12]{0:T(128)} %get-tuple-element.152) | copy-start | bytes 148
  613.8 70.3 %copy-start.27 = (s32[8]{0:T(128)S(1)}, s32[8]{0:T(128)}, u32[]{:S(2)}) copy-start(s32[8]{0:T(128)} %get-tuple-element.165) | copy-start | bytes 100
  613.8 70.3 %copy-start.28 = (s32[8]{0:T(128)S(1)}, s32[8]{0:T(128)}, u32[]{:S(2)}) copy-start(s32[8]{0:T(128)} %get-tuple-element.166) | copy-start | bytes 100
  613.8 70.3 %copy-start.29 = (s32[8]{0:T(128)S(1)}, s32[8]{0:T(128)}, u32[]{:S(2)}) copy-start(s32[8]{0:T(128)} %get-tuple-element.167) | copy-start | bytes 100
  613.8 70.3 %copy-start.30 = (s32[8]{0:T(128)S(1)}, s32[8]{0:T(128)}, u32[]{:S(2)}) copy-start(s32[8]{0:T(128)} %get-tuple-element.168) | copy-start | bytes 100
  613.9 70.3 %copy-start.31 = (s32[8]{0:T(128)S(1)}, s32[8]{0:T(128)}, u32[]{:S(2)}) copy-start(s32[8]{0:T(128)} %get-tuple-element.169) | copy-start | bytes 100
  613.9 70.3 %copy-start.32 = (s32[8]{0:T(128)S(1)}, s32[8]{0:T(128)}, u32[]{:S(2)}) copy-start(s32[8]{0:T(128)} %get-tuple-element.170) | copy-start | bytes 100
  613.9 75.2 %copy-start.37 = (s32[17]{0:T(128)S(1)}, s32[17]{0:T(128)}, u32[]{:S(2)}) copy-start(s32[17]{0:T(128)} %get-tuple-element.137) | copy-start | bytes 208
  613.9 75.2 %copy-start.38 = (s32[17]{0:T(128)S(1)}, s32[17]{0:T(128)}, u32[]{:S(2)}) copy-start(s32[17]{0:T(128)} %get-tuple-element.138) | copy-start | bytes 208
  613.9 75.2 %copy-start.39 = (s32[17]{0:T(128)S(1)}, s32[17]{0:T(128)}, u32[]{:S(2)}) copy-start(s32[17]{0:T(128)} %get-tuple-element.139) | copy-start | bytes 208
  613.9 75.2 %copy-start.40 = (s32[17]{0:T(128)S(1)}, s32[17]{0:T(128)}, u32[]{:S(2)}) copy-start(s32[17]{0:T(128)} %get-tuple-element.140) | copy-start | bytes 208
  677.7 124.6 %collective-permute-start.19 = (f32[1,15,128,128]{3,2,1,0:T(8,128)}, f32[1,15,128,128]{3,2,1,0:T(8,128)S(1)}, u32[]{:S(2)}, u32[]{:S(2)}) collective-permute-start(f32[1,15,128,128]{3,2,1,0:T(8,128)} %get-tuple-element.72), channel_id=1, source_target_pairs={{0,16},{4,20},{8,24},{12,28},{16,0},{20,4},{24,8},{28,12},{1,17},{... | collective-permute-start | bytes 2949128 | tf_op jit(solution)/shard_map/ppermute | solution.py:33
  (47 other events, 761.4 us)
Sparse Core Ops, SparseCore 0:
  80.6 72.2 all-gather.4
  154.5 149.5 all-gather.2
